TPU v7x, 32 devices: a whole 2x2x4 slice. The times are simulated.
32 devices in a mesh: layer: 4 (over x, core), feat: 2 (over y), width: 4 (over z).
Axes of the slice: x: 2, y: 2, z: 4, core: 2. Of those that a mesh axis runs over, the one named last changes fastest.
Arguments:
- residuals: bfloat16 [4, 64, 2304], P('layer', 'feat', 'width'), may hold values from -6 to 6
- cotangent: bfloat16 [4, 64, 2304], P('layer', 'feat', 'width'), may hold values from -6 to 6
- enc_weight: bfloat16 [4, 2304, 8192], P('layer', 'width', 'feat'), may hold values from -0.125 to 0.125
- enc_bias: float32 [4, 8192], P('layer', 'feat'), may hold values from -3 to 3
- dec_weight: bfloat16 [4, 4, 8192, 2304], P('layer', None, 'feat', 'width'), may hold values from -0.0625 to 0.0625
- active: int32 [4, 64, 8192], P('layer', None, 'feat'), may hold values 0 or 1
Outputs:
- dec_grad: bfloat16 [4, 4, 8192, 2304], P('layer', None, 'feat', 'width')
- enc_grad: bfloat16 [4, 2304, 8192], P('layer', 'width', 'feat')
- bias_grad: float32 [4, 8192], P('layer', 'feat')
- feat_grad: bfloat16 [4, 64, 8192], P('layer', None, 'feat')
All inputs are finite; a program needn't handle non-finite values. No bound on the sum of `active` on one device may be relied on, other than what follows from the above.
Results may differ from a plain program's by a relative error of at most 0.005.
Values may be sent and summed in bfloat16 or wider, within the bound.
No kernel may reach another device: no remote copies, remote signals or barrier semaphores. Data moves between devices by JAX's collectives and lax.ppermute only.
A program may use at most 128 MiB of HBM per device.

v0:
```python
import jax
import jax.numpy as jnp
from jax import lax
from jax.sharding import PartitionSpec as P


def local(residuals, cotangent, enc_weight, enc_bias, dec_weight, active):
    layers = dec_weight.shape[1]
    source = lax.axis_index("layer")
    local_grads = lax.all_gather(cotangent, "layer", axis=0, tiled=True)
    whole_resid, whole_grads = (
        lax.all_gather(residuals[0], "feat", axis=0, tiled=True),
        lax.all_gather(local_grads, "feat", axis=1, tiled=True),
    )
    later_mask = (jnp.arange(layers) >= source)[:, None, None]
    used_grads = jnp.where(later_mask, whole_grads, jnp.zeros_like(whole_grads))
    enc_part = jnp.dot(whole_resid, enc_weight[0], preferred_element_type=jnp.float32)
    feat_part = jnp.einsum(
        "ktd,kfd->tf", used_grads, dec_weight[0], preferred_element_type=jnp.float32
    )
    enc_share, feat_share = (
        lax.psum_scatter(enc_part, "width", scatter_dimension=0, tiled=True),
        lax.psum_scatter(feat_part, "width", scatter_dimension=0, tiled=True),
    )
    share_rows = enc_share.shape[0]
    gate_share = lax.dynamic_slice_in_dim(
        active[0], lax.axis_index("width") * share_rows, share_rows, 0
    ).astype(jnp.float32)
    act_share = ((enc_share + enc_bias) * gate_share).astype(jnp.bfloat16)
    grad_share = (feat_share * gate_share).astype(jnp.bfloat16)
    activation, feat_grad = (
        lax.all_gather(act_share, "width", axis=0, tiled=True),
        lax.all_gather(grad_share, "width", axis=0, tiled=True),
    )
    dec_grad = jnp.einsum(
        "tf,ktd->kfd", activation, used_grads, preferred_element_type=jnp.float32
    ).astype(jnp.bfloat16)
    enc_grad = lax.dot_general(
        whole_resid, feat_grad, (((0,), (0,)), ((), ())), preferred_element_type=jnp.float32
    ).astype(jnp.bfloat16)
    bias_grad = jnp.sum(feat_grad, axis=0, dtype=jnp.float32)
    return (dec_grad[None], enc_grad[None], bias_grad[None], feat_grad[None])


def solution(mesh):
    in_specs = (
        P("layer", "feat", "width"),
        P("layer", "feat", "width"),
        P("layer", "width", "feat"),
        P("layer", "feat"),
        P("layer", None, "feat", "width"),
        P("layer", None, "feat"),
    )
    out_specs = (
        P("layer", None, "feat", "width"),
        P("layer", "width", "feat"),
        P("layer", "feat"),
        P("layer", None, "feat"),
    )
    return jax.shard_map(local, mesh=mesh, in_specs=in_specs, out_specs=out_specs, check_vma=False)
```

profile of v0, /device:TPU:0, one launch (start us, length us, event | category | flops | bytes accessed | tf_op | source)
XLA Modules:
  0.0 143.9 jit_solution(6196853825714760755)
XLA Ops:
  7.2 0.0 copy-start
  7.2 0.0 copy-start.1
  7.2 0.0 reduce-scatter.5.cloned.1.call-start
  7.2 6.9 %all_gather.15 = bf16[4,32,576]{2,1,0:T(8,128)(2,1)S(1)} all-gather(bf16[1,32,576]{2,1,0:T(8,128)(2,1)} %param.7), channel_id=1, replica_groups=mesh['layer'=4,'feat'=2,'width'=4] {'layer'}, dimensions={0}, use_global_device_ids=true | all-gather | bytes 184320 | tf_op jit(solution)/shard_map/all_gather | solution.py:10
  14.1 7.2 %all_gather.16 = bf16[4,64,576]{2,1,0:T(8,128)(2,1)S(1)} all-gather(bf16[4,32,576]{2,1,0:T(8,128)(2,1)S(1)} %all_gather.15), channel_id=1, replica_groups=mesh['layer'=4,'feat'=2,'width'=4] {'feat'}, dimensions={1}, use_global_device_ids=true | all-gather | bytes 442368 | tf_op jit(solution)/shard_map/all_gather | solution.py:13
  21.3 10.8 %fusion.5 = f32[64,4096]{1,0:T(8,128)} fusion(bf16[1,4,4096,576]{2,3,1,0:T(8,128)(2,1)} %param.10, bf16[4,64,576]{2,1,0:T(8,128)(2,1)S(1)} %all_gather.16, pred[4]{0:T(512)(128)(4,1)S(1)} %iota_compare_fusion), kind=kOutput, calls=%fused_computation.7 | convolution fusion | flops 1208107008 | bytes 20217860 | tf_op jit(solution)/shard_map/ktd,kfd->tf/dot_general | solution.py:18
  32.1 0.0 reduce-scatter.5.cloned.1.call-update
  32.1 0.0 reduce-scatter.3.cloned.1.call-start
  32.2 0.0 copy-done
  32.2 4.7 %all-gather = bf16[1,64,576]{2,1,0:T(8,128)(2,1)S(1)} all-gather(bf16[1,32,576]{2,1,0:T(8,128)(2,1)S(1)} %copy-done), channel_id=2, replica_groups=mesh['layer'=4,'feat'=2,'width'=4] {'feat'}, dimensions={1}, use_global_device_ids=true | all-gather | bytes 110592 | tf_op jit(solution)/shard_map/all_gather | solution.py:12
  36.9 4.3 %fusion.3 = f32[64,4096]{1,0:T(8,128)} fusion(bf16[1,576,4096]{2,1,0:T(8,128)(2,1)} %param.8, bf16[1,64,576]{2,1,0:T(8,128)(2,1)S(1)} %all-gather), kind=kOutput, calls=%fused_computation.5 | convolution fusion | flops 301989888 | bytes 5840896 | tf_op jit(solution)/shard_map/dot_general | solution.py:17
  41.2 0.0 reduce-scatter.3.cloned.1.call-update
  41.2 19.7 %reduce-scatter.5.cloned.1.call-done = f32[16,4096]{1,0:T(8,128)} async-done(((f32[64,4096]{1,0:T(8,128)}), f32[16,4096]{1,0:T(8,128)}) %reduce-scatter.5.cloned.1.call-update) | async-done | bytes 262160 | tf_op jit(solution)/shard_map/reduce_scatter | solution.py:23
  60.9 28.8 %reduce-scatter.3.cloned.1.call-done = f32[16,4096]{1,0:T(8,128)} async-done(((f32[64,4096]{1,0:T(8,128)}), f32[16,4096]{1,0:T(8,128)}) %reduce-scatter.3.cloned.1.call-update) | async-done | bytes 262160 | tf_op jit(solution)/shard_map/reduce_scatter | solution.py:22
  89.7 0.0 copy-done.1
  89.7 1.2 fusion.10
  90.9 16.1 %all_gather.19 = bf16[64,4096]{1,0:T(8,128)(2,1)S(1)} all-gather(bf16[16,4096]{1,0:T(8,128)(2,1)S(1)} %get-tuple-element.4), channel_id=1, replica_groups=mesh['layer'=4,'feat'=2,'width'=4] {'width'}, dimensions={0}, use_global_device_ids=true | all-gather | bytes 655360 | tf_op jit(solution)/shard_map/all_gather | solution.py:33
  106.9 3.6 %fusion.2 = bf16[1,576,4096]{2,1,0:T(8,128)(2,1)} fusion(bf16[64,4096]{1,0:T(8,128)(2,1)S(1)} %all_gather.19, bf16[1,64,576]{2,1,0:T(8,128)(2,1)S(1)} %all-gather), kind=kOutput, calls=%fused_computation.4 | convolution fusion | flops 304349184 | bytes 5316608 | tf_op jit(solution)/shard_map/dot_general | solution.py:38
  110.6 0.7 convert_reduce_fusion
  111.3 15.4 %all_gather.18 = bf16[64,4096]{1,0:T(8,128)(2,1)S(1)} all-gather(bf16[16,4096]{1,0:T(8,128)(2,1)S(1)} %get-tuple-element.5), channel_id=1, replica_groups=mesh['layer'=4,'feat'=2,'width'=4] {'width'}, dimensions={0}, use_global_device_ids=true | all-gather | bytes 655360 | tf_op jit(solution)/shard_map/all_gather | solution.py:32
  126.7 9.6 %convert_bitcast_fusion = bf16[1,4,4096,576]{2,3,1,0:T(8,128)(2,1)} fusion(bf16[64,4096]{1,0:T(8,128)(2,1)S(1)} %all_gather.18, bf16[4,64,576]{2,1,0:T(8,128)(2,1)S(1)} %all_gather.16, pred[4]{0:T(512)(128)(4,1)S(1)} %iota_compare_fusion), kind=kOutput, calls=%fused_computation.2 | convolution fusion | flops 1217544192 | bytes 19693572 | tf_op jit(solution)/shard_map/tf,ktd->kfd/dot_general | solution.py:35
  136.2 0.8 copy.11
  (1 shorter events, 0.0 us)
Async XLA Ops:
  7.2 25.0 %copy-start = (bf16[1,32,576]{2,1,0:T(8,128)(2,1)S(1)}, bf16[1,32,576]{2,1,0:T(8,128)(2,1)}, u32[]{:S(2)}) copy-start(bf16[1,32,576]{2,1,0:T(8,128)(2,1)} %param.6) | copy-start | bytes 110596
  7.2 82.5 %copy-start.1 = (f32[1,4096]{1,0:T(1,128)S(1)}, f32[1,4096]{1,0:T(1,128)}, u32[]{:S(2)}) copy-start(f32[1,4096]{1,0:T(1,128)} %param.9) | copy-start | bytes 49156
  7.2 53.7 %reduce-scatter.5.cloned.1.call-start = ((), (), s32[]{:S(2)}) async-start(), calls=%async_computation.3 | async-start | bytes 1310720 | tf_op jit(solution)/shard_map/reduce_scatter | solution.py:23
  32.1 57.6 %reduce-scatter.3.cloned.1.call-start = ((), (), s32[]{:S(2)}) async-start(), calls=%async_computation.2 | async-start | bytes 1310720 | tf_op jit(solution)/shard_map/reduce_scatter | solution.py:22
Sparse Core Ops, SparseCore 0:
  32.3 28.6 reduce-scatter.4
  63.9 25.7 reduce-scatter.2
where the time goes:
time: 144 us
  blocking collectives  50.2 us (35%)
  waiting for transfers between devices  48.5 us (34%)
  matrix products  28.3 us (20%)
  between operations  14.1 us (10%)
  other arithmetic  1.87 us (1%)
    reduce_scatter x1, waiting for transfers between devices, local(): lax.psum_scatter(enc_part, 'width', scatter_dimension=0, tiled=True)  28.8 us
    reduce_scatter x1, waiting for transfers between devices, local(): lax.psum_scatter(feat_part, 'width', scatter_dimension=0, tiled=True)  19.7 us
    all_gather x1, blocking collectives, local(): lax.all_gather(grad_share, 'width', axis=0, tiled=True)  16.1 us
    all_gather x1, blocking collectives, local(): lax.all_gather(act_share, 'width', axis=0, tiled=True)  15.4 us
    dot_general x1, matrix products, local(): jnp.einsum('ktd,kfd->tf', used_grads, dec_weight[0], preferred_element_ty...  10.8 us
    dot_general x1, matrix products, local(): jnp.einsum('tf,ktd->kfd', activation, used_grads, preferred_element_type=...  9.58 us
    all_gather x1, blocking collectives, local(): lax.all_gather(local_grads, 'feat', axis=1, tiled=True)  7.18 us
    all_gather x1, blocking collectives, local(): local_grads = lax.all_gather(cotangent, 'layer', axis=0, tiled=True)  6.87 us
  transfers between devices with their start and end apart: 2, of which 2 were waited for; matrix products, arithmetic and copies ran while one was open for 3% of the time, Pallas kernels for 0%

commit v1 on v0

v1 whole, which is shorter than its diff:
```python
import functools

import jax
import jax.numpy as jnp
from jax import lax
from jax.experimental import pallas as pl
from jax.experimental.pallas import tpu as pltpu
from jax.sharding import PartitionSpec as P

MIB = 1 << 20


def tile(extent, most):
    best = extent
    for size in range(128, min(extent, most) + 1, 128):
        if extent % size == 0:
            best = size
    return best


def swap(x, axis, size, bit):
    return lax.ppermute(x, axis, [(i, i ^ bit) for i in range(size)])


def partial_kernel(x_ref, w_ref, keep_ref, send_ref):
    kept = keep_ref.shape[0]
    out = jnp.dot(x_ref[...], w_ref[...], preferred_element_type=jnp.float32)
    keep_ref[...] = out[:kept]
    send_ref[...] = out[kept:].astype(send_ref.dtype)


def partial_product(x, weight, first, count, most):
    rows, depth = x.shape
    half = rows // 2
    width = tile(count, most)
    start = first // width
    return pl.pallas_call(
        partial_kernel,
        grid=(count // width,),
        in_specs=[
            pl.BlockSpec((rows, depth), lambda j: (0, 0)),
            pl.BlockSpec((depth, width), lambda j: (0, start + j)),
        ],
        out_specs=[
            pl.BlockSpec((half, width), lambda j: (0, j)),
            pl.BlockSpec((half, width), lambda j: (0, j)),
        ],
        out_shape=[
            jax.ShapeDtypeStruct((half, count), jnp.float32),
            jax.ShapeDtypeStruct((half, count), jnp.bfloat16),
        ],
        compiler_params=pltpu.CompilerParams(vmem_limit_bytes=40 * MIB),
        cost_estimate=pl.CostEstimate(
            flops=2 * rows * depth * count, bytes_accessed=2 * depth * count, transcendentals=0
        ),
    )(x, weight)


def dec_kernel(pieces, *refs):
    cot_ref, act_refs, out_ref = refs[0], refs[1 : 1 + pieces], refs[1 + pieces]
    act = jnp.concatenate([ref[...] for ref in act_refs], axis=0)
    out_ref[...] = jnp.dot(cot_ref[...], act, preferred_element_type=jnp.float32).astype(out_ref.dtype)


def dec_product(cot_t, acts, most):
    layers, depth, tokens = cot_t.shape
    feats = acts[0].shape[1]
    width = tile(feats, most)
    return pl.pallas_call(
        functools.partial(dec_kernel, len(acts)),
        grid=(feats // width, layers),
        in_specs=[pl.BlockSpec((None, depth, tokens), lambda j, k: (k, 0, 0))]
        + [pl.BlockSpec((a.shape[0], width), lambda j, k: (0, j)) for a in acts],
        out_specs=pl.BlockSpec((None, depth, width), lambda j, k: (k, 0, j)),
        out_shape=jax.ShapeDtypeStruct((layers, depth, feats), jnp.bfloat16),
        compiler_params=pltpu.CompilerParams(vmem_limit_bytes=40 * MIB),
        cost_estimate=pl.CostEstimate(
            flops=2 * layers * tokens * depth * feats,
            bytes_accessed=2 * layers * depth * feats,
            transcendentals=0,
        ),
    )(cot_t, *acts)


def enc_kernel(chained, role_ref, *refs):
    res_ref, mine_ref, other_ref = refs[:3]
    enc_ref, bias_ref, feat_ref = refs[3 + 3 * chained :]
    half = mine_ref.shape[0]
    mine, other = mine_ref[...], other_ref[...]
    grad = jnp.concatenate([mine, other], axis=0)
    enc_ref[...] = jnp.dot(res_ref[...], grad, preferred_element_type=jnp.float32).astype(enc_ref.dtype)
    bias_ref[...] = jnp.sum(grad.astype(jnp.float32), axis=0, keepdims=True)

    @pl.when(role_ref[0] == 0)
    def _():
        feat_ref[:half] = mine
        feat_ref[half:] = other

    @pl.when(role_ref[0] != 0)
    def _():
        feat_ref[:half] = other
        feat_ref[half:] = mine


def enc_product(role, res_t, mine, other, first, feats, before, most):
    depth, tokens = res_t.shape
    half, count = mine.shape
    width = tile(count, most)
    start = first // width
    chained = before is not None
    shapes = [
        jax.ShapeDtypeStruct((depth, feats), jnp.bfloat16),
        jax.ShapeDtypeStruct((1, feats), jnp.float32),
        jax.ShapeDtypeStruct((tokens, feats), jnp.bfloat16),
    ]
    return pl.pallas_call(
        functools.partial(enc_kernel, int(chained)),
        grid_spec=pltpu.PrefetchScalarGridSpec(
            num_scalar_prefetch=1,
            grid=(count // width,),
            in_specs=[
                pl.BlockSpec((depth, tokens), lambda j, r: (0, 0)),
                pl.BlockSpec((half, width), lambda j, r: (0, j)),
                pl.BlockSpec((half, width), lambda j, r: (0, j)),
            ]
            + [pl.BlockSpec(memory_space=pl.ANY)] * (3 * chained),
            out_specs=[
                pl.BlockSpec((depth, width), lambda j, r: (0, start + j)),
                pl.BlockSpec((1, width), lambda j, r: (0, start + j)),
                pl.BlockSpec((tokens, width), lambda j, r: (0, start + j)),
            ],
        ),
        out_shape=shapes,
        input_output_aliases={4: 0, 5: 1, 6: 2} if chained else {},
        compiler_params=pltpu.CompilerParams(vmem_limit_bytes=40 * MIB),
        cost_estimate=pl.CostEstimate(
            flops=2 * tokens * depth * count, bytes_accessed=2 * depth * count, transcendentals=0
        ),
    )(role, res_t, mine, other, *(before if chained else ()))


def both(x, role):
    half = x.shape[-2] // 2
    low, high = x[..., :half, :], x[..., half:, :]
    first = role == 0
    return jnp.concatenate([jnp.where(first, low, high), jnp.where(first, high, low)], axis=-2)


def cross_sum(keep, send, axis, size):
    total = keep + swap(send, axis, size, 1).astype(jnp.float32)
    bit = 2
    while bit < size:
        total = lax.reduce_precision(total, 8, 7)
        total = total + swap(total.astype(jnp.bfloat16), axis, size, bit).astype(jnp.float32)
        bit *= 2
    return total


def rows_of(x, role, half):
    return lax.dynamic_slice_in_dim(x, role * half, half, 0)


def local(feat_size, layer_size, width_size, residuals, cotangent, enc_weight, enc_bias, dec_weight, active):
    layers = dec_weight.shape[1]
    source = lax.axis_index("layer")
    role = lax.axis_index("width") % 2
    role_ref = jnp.reshape(role, (1,)).astype(jnp.int32)
    res, cot = residuals[0], cotangent[0]
    own, depth = res.shape
    feats = enc_weight.shape[2]
    gate = active[0]
    tokens = gate.shape[0]
    weight = jnp.swapaxes(dec_weight[0], 1, 2).reshape(layers * depth, feats)

    if feat_size == 2:
        place = lax.axis_index("feat")
        other = swap(jnp.concatenate([res, cot], axis=0), "feat", 2, 1)
        res_blocks = [res, other[:own]]
        block_rows = [place * own, (1 - place) * own]
        cot_own_first = jnp.concatenate([cot, other[own:]], axis=0)
        res_all = jnp.where(place == 0, jnp.concatenate(res_blocks, 0), jnp.concatenate(res_blocks[::-1], 0))
    else:
        res_all = lax.all_gather(res, "feat", axis=0, tiled=True)
        cot_own_first = lax.all_gather(cot, "feat", axis=0, tiled=True)
        res_blocks = [res_all]
        block_rows = [0]

    acts = []
    for rows, first in zip(res_blocks, block_rows):
        keep, send = partial_product(both(rows, role), enc_weight[0], 0, feats, 512)
        total = cross_sum(keep, send, "width", width_size)
        half = total.shape[0]
        mask = lax.dynamic_slice_in_dim(gate, first + role * half, half, 0).astype(jnp.float32)
        act = ((total + enc_bias) * mask).astype(jnp.bfloat16)
        acts += [act, swap(act, "width", width_size, 1)]

    held = [cot_own_first]
    bit = layer_size // 2
    while bit:
        held = held + list(swap(jnp.stack(held), "layer", layer_size, bit))
        bit //= 2
    order = [0]
    bit = layer_size // 2
    while bit:
        order = order + [o ^ bit for o in order]
        bit //= 2
    by_xor = [held[order.index(j)] for j in range(layer_size)]
    grads = jnp.stack(by_xor)
    grads = jnp.take(grads, jnp.arange(layers) ^ source, axis=0)
    later = (jnp.arange(layers) >= source)[:, None, None]
    grads = jnp.where(later, grads, jnp.zeros_like(grads))
    if feat_size == 2:
        grads_true = jnp.where(place == 0, grads, jnp.roll(grads, own, axis=1))
    else:
        grads_true = grads
    rows_true = both(grads_true, role)
    lhs = jnp.swapaxes(rows_true, 0, 1).reshape(tokens, layers * depth)

    parts = 2
    count = feats // parts
    half = tokens // 2
    mask = rows_of(gate, role, half).astype(jnp.float32)
    mine, theirs = [], []
    for part in range(parts):
        keep, send = partial_product(lhs, weight, part * count, count, 512)
        total = cross_sum(keep, send, "width", width_size)
        grad = (total * mask[:, part * count : (part + 1) * count]).astype(jnp.bfloat16)
        mine.append(grad)
        theirs.append(swap(grad, "width", width_size, 1))

    ends = [sum(r.shape[0] for r in res_blocks[:i]) for i in range(len(res_blocks) + 1)]
    rows_act = jnp.concatenate([both(grads[:, a:b], role) for a, b in zip(ends, ends[1:])], axis=1)
    dec_grad = dec_product(jnp.swapaxes(rows_act, 1, 2), acts, 1024)

    res_t = both(res_all, role).T
    out = None
    for part in range(parts):
        out = enc_product(role_ref, res_t, mine[part], theirs[part], part * count, feats, out, 512)
    enc_grad, bias_grad, feat_grad = out
    return (jnp.swapaxes(dec_grad, 1, 2)[None], enc_grad[None], bias_grad, feat_grad[None])


def solution(mesh):
    in_specs = (
        P("layer", "feat", "width"),
        P("layer", "feat", "width"),
        P("layer", "width", "feat"),
        P("layer", "feat"),
        P("layer", None, "feat", "width"),
        P("layer", None, "feat"),
    )
    out_specs = (
        P("layer", None, "feat", "width"),
        P("layer", "width", "feat"),
        P("layer", "feat"),
        P("layer", None, "feat"),
    )
    sizes = (mesh.shape["feat"], mesh.shape["layer"], mesh.shape["width"])
    return jax.shard_map(
        functools.partial(local, *sizes), mesh=mesh, in_specs=in_specs, out_specs=out_specs, check_vma=False
    )
```

time: 144 us -> 77.9 us (0.54)
  blocking collectives: 50.2 us -> 0 us
  waiting for transfers between devices: 48.5 us -> 9.41 us
  Pallas kernels: 0 us -> 32.4 us
  matrix products: 28.3 us -> 0 us
  starting transfers between devices: 0.08 us -> 22.1 us
  between operations: 14.1 us -> 0.92 us
  local copies, waits for them, and re-layouts: 0.8 us -> 8 us
  other arithmetic: 1.87 us -> 4.63 us
    all_gather x5 -> x0, blocking collectives: 50.2 us -> none  [the longest x1 16.1 us: local(): lax.all_gather(grad_share, 'width', axis=0, tiled=True)]
    reduce_scatter x2 -> x0, waiting for transfers between devices: 48.5 us -> none  [the longest x1 28.8 us: local(): lax.psum_scatter(enc_part, 'width', scatter_dimension=0, tiled=True)]
    pallas_call x0 -> x7, Pallas kernels: none -> 32.4 us  [the longest x4 14.9 us: partial_product(): pl.pallas_call(partial_kernel, grid=(count // width,), in_specs=[pl.Block...]
    dot_general x4 -> x0, matrix products: 28.3 us -> none  [the longest x1 10.8 us: local(): jnp.einsum('ktd,kfd->tf', used_grads, dec_weight[0], preferred_element_ty...]
    ppermute x0 -> x15, starting transfers between devices: none -> 22.1 us  [swap(): return lax.ppermute(x, axis, [(i, i ^ bit) for i in range(size)])]
    ppermute x0 -> x15, waiting for transfers between devices: none -> 9.41 us  [swap(): return lax.ppermute(x, axis, [(i, i ^ bit) for i in range(size)])]
    unnamed x5 -> x12, local copies, waits for them, and re-layouts: 0.8 us -> 6.52 us
    select_n x0 -> x9, other arithmetic: none -> 2.52 us  [the longest x5 1.73 us: both(): jnp.where(first, low, high)]
  transfers between devices with their start and end apart: 2 -> 15, of which waited for: 2 -> 5; matrix products, arithmetic and copies ran while one was open for 3% -> 8% of each run, Pallas kernels for 0% -> 38%
where the time goes in v1:
time: 77.9 us; the launch traced here: 77.5 us
  Pallas kernels  32.4 us (42%)
  starting transfers between devices  22.1 us (28%)
  waiting for transfers between devices  9.41 us (12%)
  local copies, waits for them, and re-layouts  8 us (10%)
  other arithmetic  4.63 us (6%)
  between operations  0.92 us (1%)
    ppermute x15, starting transfers between devices, swap(): return lax.ppermute(x, axis, [(i, i ^ bit) for i in range(size)])  22.1 us
    pallas_call x4, Pallas kernels, partial_product(): pl.pallas_call(partial_kernel, grid=(count // width,), in_specs=[pl.Block...  14.9 us
    pallas_call x1, Pallas kernels, dec_product(): pl.pallas_call(functools.partial(dec_kernel, len(acts)), grid=(feats // w...  12.2 us
    ppermute x15, waiting for transfers between devices, swap(): return lax.ppermute(x, axis, [(i, i ^ bit) for i in range(size)])  9.41 us
    unnamed x12, local copies, waits for them, and re-layouts  6.52 us
    pallas_call x2, Pallas kernels, enc_product(): pl.pallas_call(functools.partial(enc_kernel, int(chained)), grid_spec=plt...  5.3 us
    select_n x5, other arithmetic, both(): jnp.where(first, low, high)  1.73 us
  transfers between devices with their start and end apart: 15, of which 5 were waited for; matrix products, arithmetic and copies ran while one was open for 8% of the time, Pallas kernels for 38%

profile of v1, /device:TPU:0, one launch (start us, length us, event | category | flops | bytes accessed | tf_op | source)
XLA Modules:
  0.0 77.5 jit_solution(14066401163406390718)
XLA Ops:
  0.6 0.9 %copy.18 = bf16[1,32,576]{1,2,0:T(8,128)(2,1)S(1)} copy(bf16[1,32,576]{2,1,0:T(8,128)(2,1)} %param.7) | data formatting | bytes 73728 | tf_op args[1]
  1.5 0.9 %copy.19 = bf16[1,32,576]{1,2,0:T(8,128)(2,1)S(1)} copy(bf16[1,32,576]{2,1,0:T(8,128)(2,1)} %param.6) | data formatting | bytes 73728 | tf_op args[0]
  2.5 0.1 pad_maximum_fusion.3
  2.6 3.0 %collective-permute-start = (bf16[64,576]{0,1:T(8,128)(2,1)S(1)}, bf16[64,576]{0,1:T(8,128)(2,1)S(1)}, u32[]{:S(2)}, u32[]{:S(2)}) collective-permute-start(bf16[64,576]{0,1:T(8,128)(2,1)S(1)} %pad_maximum_fusion.3), channel_id=1, source_target_pairs={{0,4},{4,0},{1,5},{5,1},{2,6},{6,2},{3,7},{7,3},{8,12},{12,8},{9,1... | collective-permute-start | bytes 221192 | tf_op jit(solution)/shard_map/ppermute | solution.py:22
  5.6 0.8 select_bitcast_fusion.1
  6.4 2.3 %copy-done = bf16[1,576,4096]{2,1,0:T(8,128)(2,1)S(1)} copy-done((bf16[1,576,4096]{2,1,0:T(8,128)(2,1)S(1)}, bf16[1,576,4096]{2,1,0:T(8,128)(2,1)}, u32[]{:S(2)}) %copy-start) | copy-done | bytes 4718616
  8.7 2.1 %shard_map.93 = (f32[16,4096]{1,0:T(8,128)S(1)}, bf16[16,4096]{1,0:T(8,128)(2,1)S(1)}) custom-call(bf16[32,576]{1,0:T(8,128)(2,1)S(1)} %pad_maximum_fusion.4.x_ref, bf16[576,4096]{1,0:T(8,128)(2,1)S(1)} %bitcast.40), custom_call_target="tpu_custom_call" | custom-call | flops 150994944 | bytes 4718592 | tf_op jit(solution)/shard_map/pallas_call | solution.py:37
  10.9 1.6 %collective-permute-start.3 = (bf16[16,4096]{1,0:T(8,128)(2,1)S(1)}, bf16[16,4096]{1,0:T(8,128)(2,1)S(1)}, u32[]{:S(2)}, u32[]{:S(2)}) collective-permute-start(bf16[16,4096]{1,0:T(8,128)(2,1)S(1)} %get-tuple-element.19), channel_id=1, source_target_pairs={{0,1},{1,0},{2,3},{3,2},{4,5},{5,4},{6,7},{7,6},{8,9},{9,8},{10,11... | collective-permute-start | bytes 393224 | tf_op jit(solution)/shard_map/ppermute | solution.py:22
  12.6 0.1 fusion.11
  12.7 0.1 maximum_bitcast_fusion.1
  12.8 0.2 maximum_select_fusion.1
  13.0 0.1 broadcast_select_fusion.7
  13.3 0.1 copy.21
  13.5 1.5 %collective-permute-start.1 = (bf16[1,64,576]{1,2,0:T(8,128)(2,1)S(1)}, bf16[1,64,576]{1,2,0:T(8,128)(2,1)S(1)}, u32[]{:S(2)}, u32[]{:S(2)}) collective-permute-start(bf16[1,64,576]{1,2,0:T(8,128)(2,1)S(1)} %maximum_bitcast_fusion.1), channel_id=1, source_target_pairs={{0,16},{8,24},{16,0},{24,8},{1,17},{9,25},{17,1},{25,9},{2,18},{10... | collective-permute-start | bytes 221192 | tf_op jit(solution)/shard_map/ppermute | solution.py:22
  15.0 2.3 %copy-done.1 = bf16[1,576,4096]{2,1,0:T(8,128)(2,1)S(1)} copy-done((bf16[1,576,4096]{2,1,0:T(8,128)(2,1)S(1)}, bf16[1,576,4096]{2,1,0:T(8,128)(2,1)}, u32[]{:S(2)}) %copy-start.1) | copy-done | bytes 4718616
  17.4 2.1 %shard_map.94 = (f32[16,4096]{1,0:T(8,128)S(1)}, bf16[16,4096]{1,0:T(8,128)(2,1)S(1)}) custom-call(bf16[32,576]{1,0:T(8,128)(2,1)S(1)} %pad_maximum_fusion.5.x_ref, bf16[576,4096]{1,0:T(8,128)(2,1)S(1)} %bitcast.41), custom_call_target="tpu_custom_call" | custom-call | flops 150994944 | bytes 4718592 | tf_op jit(solution)/shard_map/pallas_call | solution.py:37
  19.5 0.5 collective-permute-start.6
  20.0 0.1 maximum_bitcast_fusion.2.refs_0_
  20.2 2.6 %collective-permute-start.4 = (bf16[16,4096]{1,0:T(8,128)(2,1)S(1)}, bf16[16,4096]{1,0:T(8,128)(2,1)S(1)}, u32[]{:S(2)}, u32[]{:S(2)}) collective-permute-start(bf16[16,4096]{1,0:T(8,128)(2,1)S(1)} %fusion.4), channel_id=1, source_target_pairs={{0,2},{1,3},{2,0},{3,1},{4,6},{5,7},{6,4},{7,5},{8,10},{9,11},{10,... | collective-permute-start | bytes 393224 | tf_op jit(solution)/shard_map/ppermute | solution.py:22
  23.0 2.5 %collective-permute-done.6 = bf16[16,4096]{1,0:T(8,128)(2,1)S(1)} collective-permute-done((bf16[16,4096]{1,0:T(8,128)(2,1)S(1)}, bf16[16,4096]{1,0:T(8,128)(2,1)S(1)}, u32[]{:S(2)}, u32[]{:S(2)}) %collective-permute-start.6) | collective-permute-done | bytes 131104 | tf_op jit(solution)/shard_map/ppermute | solution.py:22
  25.5 2.5 %collective-permute-start.7 = (bf16[16,4096]{1,0:T(8,128)(2,1)S(1)}, bf16[16,4096]{1,0:T(8,128)(2,1)S(1)}, u32[]{:S(2)}, u32[]{:S(2)}) collective-permute-start(bf16[16,4096]{1,0:T(8,128)(2,1)S(1)} %fusion.5), channel_id=1, source_target_pairs={{0,2},{1,3},{2,0},{3,1},{4,6},{5,7},{6,4},{7,5},{8,10},{9,11},{10,... | collective-permute-start | bytes 393224 | tf_op jit(solution)/shard_map/ppermute | solution.py:22
  28.1 0.2 pad_maximum_fusion
  28.2 0.7 gather_fusion
  28.9 0.1 select_select_fusion
  29.0 0.2 fusion.9
  29.3 0.5 maximum_select_fusion
  29.8 0.2 broadcast_select_fusion.1
  30.0 0.3 pad_maximum_fusion.1
  30.3 0.2 copy.22.x_ref
  30.6 5.3 %shard_map.96 = (f32[32,2048]{1,0:T(8,128)S(1)}, bf16[32,2048]{1,0:T(8,128)(2,1)S(1)}) custom-call(bf16[64,2304]{1,0:T(8,128)(2,1)S(1)} %copy.22.x_ref, bf16[2304,4096]{1,0:T(8,128)(2,1)} %bitcast.42), custom_call_target="tpu_custom_call" | custom-call | flops 603979776 | bytes 9437184 | tf_op jit(solution)/shard_map/pallas_call | solution.py:37
  35.9 0.6 collective-permute-start.9
  36.5 0.5 broadcast_select_fusion.5
  37.0 5.3 %shard_map.97 = (f32[32,2048]{1,0:T(8,128)S(1)}, bf16[32,2048]{1,0:T(8,128)(2,1)S(1)}) custom-call(bf16[64,2304]{1,0:T(8,128)(2,1)S(1)} %copy.22.x_ref, bf16[2304,4096]{1,0:T(8,128)(2,1)} %bitcast.43), custom_call_target="tpu_custom_call" | custom-call | flops 603979776 | bytes 9437184 | tf_op jit(solution)/shard_map/pallas_call | solution.py:37
  42.4 1.6 %collective-permute-start.12 = (bf16[32,2048]{1,0:T(8,128)(2,1)S(1)}, bf16[32,2048]{1,0:T(8,128)(2,1)S(1)}, u32[]{:S(2)}, u32[]{:S(2)}) collective-permute-start(bf16[32,2048]{1,0:T(8,128)(2,1)S(1)} %get-tuple-element.25), channel_id=1, source_target_pairs={{0,1},{1,0},{2,3},{3,2},{4,5},{5,4},{6,7},{7,6},{8,9},{9,8},{10,11... | collective-permute-start | bytes 393224 | tf_op jit(solution)/shard_map/ppermute | solution.py:22
  44.0 0.5 collective-permute-start.10
  44.5 3.1 %collective-permute-done.12 = bf16[32,2048]{1,0:T(8,128)(2,1)S(1)} collective-permute-done((bf16[32,2048]{1,0:T(8,128)(2,1)S(1)}, bf16[32,2048]{1,0:T(8,128)(2,1)S(1)}, u32[]{:S(2)}, u32[]{:S(2)}) %collective-permute-start.12) | collective-permute-done | bytes 131104 | tf_op jit(solution)/shard_map/ppermute | solution.py:22
  47.7 2.6 %collective-permute-start.13 = (bf16[32,2048]{1,0:T(8,128)(2,1)S(1)}, bf16[32,2048]{1,0:T(8,128)(2,1)S(1)}, u32[]{:S(2)}, u32[]{:S(2)}) collective-permute-start(bf16[32,2048]{1,0:T(8,128)(2,1)S(1)} %fusion.7), channel_id=1, source_target_pairs={{0,2},{1,3},{2,0},{3,1},{4,6},{5,7},{6,4},{7,5},{8,10},{9,11},{10,... | collective-permute-start | bytes 393224 | tf_op jit(solution)/shard_map/ppermute | solution.py:22
  50.3 0.2 fusion.2
  50.5 2.7 %collective-permute-start.8 = (bf16[16,4096]{1,0:T(8,128)(2,1)S(1)}, bf16[16,4096]{1,0:T(8,128)(2,1)S(1)}, u32[]{:S(2)}, u32[]{:S(2)}) collective-permute-start(bf16[16,4096]{1,0:T(8,128)(2,1)S(1)} %get-tuple-element.32.refs_3_), channel_id=1, source_target_pairs={{0,1},{1,0},{2,3},{3,2},{4,5},{5,4},{6,7},{7,6},{8,9},{9,8},{10,11... | collective-permute-start | bytes 393224 | tf_op jit(solution)/shard_map/ppermute | solution.py:22
  53.2 0.2 collective-permute-done.10
  53.4 2.9 %collective-permute-done.13 = bf16[32,2048]{1,0:T(8,128)(2,1)S(1)} collective-permute-done((bf16[32,2048]{1,0:T(8,128)(2,1)S(1)}, bf16[32,2048]{1,0:T(8,128)(2,1)S(1)}, u32[]{:S(2)}, u32[]{:S(2)}) %collective-permute-start.13) | collective-permute-done | bytes 131104 | tf_op jit(solution)/shard_map/ppermute | solution.py:22
  56.2 0.1 fusion
  56.5 2.0 %collective-permute-start.11 = (bf16[32,2048]{1,0:T(8,128)(2,1)S(1)}, bf16[32,2048]{1,0:T(8,128)(2,1)S(1)}, u32[]{:S(2)}, u32[]{:S(2)}) collective-permute-start(bf16[32,2048]{1,0:T(8,128)(2,1)S(1)} %get-tuple-element.43.refs_1_), channel_id=1, source_target_pairs={{0,1},{1,0},{2,3},{3,2},{4,5},{5,4},{6,7},{7,6},{8,9},{9,8},{10,11... | collective-permute-start | bytes 393224 | tf_op jit(solution)/shard_map/ppermute | solution.py:22
  58.5 0.8 maximum_bitcast_fusion.refs_0_
  59.2 0.7 collective-permute-done.5.refs_2_
  59.9 12.2 %shard_map.95 = bf16[4,576,4096]{2,1,0:T(8,128)(2,1)} custom-call(bf16[4,576,64]{2,1,0:T(8,128)(2,1)S(1)} %maximum_bitcast_fusion.refs_0_, bf16[16,4096]{1,0:T(8,128)(2,1)S(1)} %get-tuple-element.33.refs_1_, bf16[16,4096]{1,0:T(8,128)(2,1)S(1)} %collective-permute-done.5.refs_2_, bf16[16,4096]{1,0:T(8,128)(2,1)S(1)} %get-tuple-element.32.refs_3_, ...), custom_call_target="tpu_custom_call" | custom-call | flops 1207959552 | bytes 18874368 | tf_op jit(solution)/shard_map/pallas_call | solution.py:69
  72.1 2.6 %shard_map.98 = (bf16[576,4096]{1,0:T(8,128)(2,1)}, f32[1,4096]{1,0:T(1,128)}, bf16[64,4096]{1,0:T(8,128)(2,1)}) custom-call(s32[1]{0:T(128)} %bitcast.13.role_ref, bf16[576,64]{1,0:T(8,128)(2,1)S(1)} %maximum_bitcast_fusion.2.refs_0_, bf16[32,2048]{1,0:T(8,128)(2,1)S(1)} %get-tuple-element.42.refs_1_, bf16[32,2048]{1,0:T(8,128)(2,1)S(1)} %collective-permute-done.14.refs_2_), custom_call_target="tpu_custom_call" | custom-call | flops 150994944 | bytes 2359296 | tf_op jit(solution)/shard_map/pallas_call | solution.py:116
  74.8 2.7 %shard_map.99 = (bf16[576,4096]{1,0:T(8,128)(2,1)}, f32[1,4096]{1,0:T(1,128)}, bf16[64,4096]{1,0:T(8,128)(2,1)}) custom-call(s32[1]{0:T(128)} %bitcast.13.role_ref, bf16[576,64]{1,0:T(8,128)(2,1)S(1)} %maximum_bitcast_fusion.2.refs_0_, bf16[32,2048]{1,0:T(8,128)(2,1)S(1)} %get-tuple-element.43.refs_1_, ...), custom_call_target="tpu_custom_call", output_to_operand_aliasing={{0}: (4, {}), {1}: (5, {}), {2}: (6, {})} | custom-call | flops 150994944 | bytes 2359296 | tf_op jit(solution)/shard_map/pallas_call | solution.py:116
  (35 shorter events, 0.8 us)
Async XLA Ops:
  2.6 10.0 %collective-permute-start = (bf16[64,576]{0,1:T(8,128)(2,1)S(1)}, bf16[64,576]{0,1:T(8,128)(2,1)S(1)}, u32[]{:S(2)}, u32[]{:S(2)}) collective-permute-start(bf16[64,576]{0,1:T(8,128)(2,1)S(1)} %pad_maximum_fusion.3), channel_id=1, source_target_pairs={{0,4},{4,0},{1,5},{5,1},{2,6},{6,2},{3,7},{7,3},{8,12},{12,8},{9,1... | collective-permute-start | bytes 221192 | tf_op jit(solution)/shard_map/ppermute | solution.py:22
  6.4 2.3 %copy-start = (bf16[1,576,4096]{2,1,0:T(8,128)(2,1)S(1)}, bf16[1,576,4096]{2,1,0:T(8,128)(2,1)}, u32[]{:S(2)}) copy-start(bf16[1,576,4096]{2,1,0:T(8,128)(2,1)} %param.8) | copy-start | bytes 14155780
  8.7 3.8 %copy-start.2 = (s32[1,64,4096]{2,1,0:T(8,128)S(1)}, s32[1,64,4096]{2,1,0:T(8,128)}, u32[]{:S(2)}) copy-start(s32[1,64,4096]{2,1,0:T(8,128)} %param.11) | copy-start | bytes 3145732
  10.9 9.2 %collective-permute-start.3 = (bf16[16,4096]{1,0:T(8,128)(2,1)S(1)}, bf16[16,4096]{1,0:T(8,128)(2,1)S(1)}, u32[]{:S(2)}, u32[]{:S(2)}) collective-permute-start(bf16[16,4096]{1,0:T(8,128)(2,1)S(1)} %get-tuple-element.19), channel_id=1, source_target_pairs={{0,1},{1,0},{2,3},{3,2},{4,5},{5,4},{6,7},{7,6},{8,9},{9,8},{10,11... | collective-permute-start | bytes 393224 | tf_op jit(solution)/shard_map/ppermute | solution.py:22
  13.5 9.3 %collective-permute-start.1 = (bf16[1,64,576]{1,2,0:T(8,128)(2,1)S(1)}, bf16[1,64,576]{1,2,0:T(8,128)(2,1)S(1)}, u32[]{:S(2)}, u32[]{:S(2)}) collective-permute-start(bf16[1,64,576]{1,2,0:T(8,128)(2,1)S(1)} %maximum_bitcast_fusion.1), channel_id=1, source_target_pairs={{0,16},{8,24},{16,0},{24,8},{1,17},{9,25},{17,1},{25,9},{2,18},{10... | collective-permute-start | bytes 221192 | tf_op jit(solution)/shard_map/ppermute | solution.py:22
  15.0 2.3 %copy-start.1 = (bf16[1,576,4096]{2,1,0:T(8,128)(2,1)S(1)}, bf16[1,576,4096]{2,1,0:T(8,128)(2,1)}, u32[]{:S(2)}) copy-start(bf16[1,576,4096]{2,1,0:T(8,128)(2,1)} %param.8) | copy-start | bytes 14155780
  19.5 6.0 %collective-permute-start.6 = (bf16[16,4096]{1,0:T(8,128)(2,1)S(1)}, bf16[16,4096]{1,0:T(8,128)(2,1)S(1)}, u32[]{:S(2)}, u32[]{:S(2)}) collective-permute-start(bf16[16,4096]{1,0:T(8,128)(2,1)S(1)} %get-tuple-element.21), channel_id=1, source_target_pairs={{0,1},{1,0},{2,3},{3,2},{4,5},{5,4},{6,7},{7,6},{8,9},{9,8},{10,11... | collective-permute-start | bytes 393224 | tf_op jit(solution)/shard_map/ppermute | solution.py:22
  20.2 30.1 %collective-permute-start.4 = (bf16[16,4096]{1,0:T(8,128)(2,1)S(1)}, bf16[16,4096]{1,0:T(8,128)(2,1)S(1)}, u32[]{:S(2)}, u32[]{:S(2)}) collective-permute-start(bf16[16,4096]{1,0:T(8,128)(2,1)S(1)} %fusion.4), channel_id=1, source_target_pairs={{0,2},{1,3},{2,0},{3,1},{4,6},{5,7},{6,4},{7,5},{8,10},{9,11},{10,... | collective-permute-start | bytes 393224 | tf_op jit(solution)/shard_map/ppermute | solution.py:22
  22.9 5.2 %collective-permute-start.2 = (bf16[2,64,576]{1,2,0:T(8,128)(2,1)S(1)}, bf16[2,64,576]{1,2,0:T(8,128)(2,1)S(1)}, u32[]{:S(2)}, u32[]{:S(2)}) collective-permute-start(bf16[2,64,576]{1,2,0:T(8,128)(2,1)S(1)} %pad_maximum_fusion.2), channel_id=1, source_target_pairs={{0,8},{8,0},{16,24},{24,16},{1,9},{9,1},{17,25},{25,17},{2,10},{10... | collective-permute-start | bytes 442376 | tf_op jit(solution)/shard_map/ppermute | solution.py:22
  25.5 24.8 %collective-permute-start.7 = (bf16[16,4096]{1,0:T(8,128)(2,1)S(1)}, bf16[16,4096]{1,0:T(8,128)(2,1)S(1)}, u32[]{:S(2)}, u32[]{:S(2)}) collective-permute-start(bf16[16,4096]{1,0:T(8,128)(2,1)S(1)} %fusion.5), channel_id=1, source_target_pairs={{0,2},{1,3},{2,0},{3,1},{4,6},{5,7},{6,4},{7,5},{8,10},{9,11},{10,... | collective-permute-start | bytes 393224 | tf_op jit(solution)/shard_map/ppermute | solution.py:22
  35.9 8.0 %collective-permute-start.9 = (bf16[32,2048]{1,0:T(8,128)(2,1)S(1)}, bf16[32,2048]{1,0:T(8,128)(2,1)S(1)}, u32[]{:S(2)}, u32[]{:S(2)}) collective-permute-start(bf16[32,2048]{1,0:T(8,128)(2,1)S(1)} %get-tuple-element.23), channel_id=1, source_target_pairs={{0,1},{1,0},{2,3},{3,2},{4,5},{5,4},{6,7},{7,6},{8,9},{9,8},{10,11... | collective-permute-start | bytes 393224 | tf_op jit(solution)/shard_map/ppermute | solution.py:22
  37.0 13.2 %copy-start.4 = (f32[1,4096]{1,0:T(1,128)S(1)}, f32[1,4096]{1,0:T(1,128)}, u32[]{:S(2)}) copy-start(f32[1,4096]{1,0:T(1,128)} %param.9) | copy-start | bytes 49156
  42.4 7.9 %copy-start.3 = (s32[1,64,4096]{2,1,0:T(8,128)S(1)}, s32[1,64,4096]{2,1,0:T(8,128)}, u32[]{:S(2)}) copy-start(s32[1,64,4096]{2,1,0:T(8,128)} %param.11) | copy-start | bytes 3145732
  42.4 5.3 %collective-permute-start.12 = (bf16[32,2048]{1,0:T(8,128)(2,1)S(1)}, bf16[32,2048]{1,0:T(8,128)(2,1)S(1)}, u32[]{:S(2)}, u32[]{:S(2)}) collective-permute-start(bf16[32,2048]{1,0:T(8,128)(2,1)S(1)} %get-tuple-element.25), channel_id=1, source_target_pairs={{0,1},{1,0},{2,3},{3,2},{4,5},{5,4},{6,7},{7,6},{8,9},{9,8},{10,11... | collective-permute-start | bytes 393224 | tf_op jit(solution)/shard_map/ppermute | solution.py:22
  44.0 9.4 %collective-permute-start.10 = (bf16[32,2048]{1,0:T(8,128)(2,1)S(1)}, bf16[32,2048]{1,0:T(8,128)(2,1)S(1)}, u32[]{:S(2)}, u32[]{:S(2)}) collective-permute-start(bf16[32,2048]{1,0:T(8,128)(2,1)S(1)} %fusion.6), channel_id=1, source_target_pairs={{0,2},{1,3},{2,0},{3,1},{4,6},{5,7},{6,4},{7,5},{8,10},{9,11},{10,... | collective-permute-start | bytes 393224 | tf_op jit(solution)/shard_map/ppermute | solution.py:22
  47.7 8.6 %collective-permute-start.13 = (bf16[32,2048]{1,0:T(8,128)(2,1)S(1)}, bf16[32,2048]{1,0:T(8,128)(2,1)S(1)}, u32[]{:S(2)}, u32[]{:S(2)}) collective-permute-start(bf16[32,2048]{1,0:T(8,128)(2,1)S(1)} %fusion.7), channel_id=1, source_target_pairs={{0,2},{1,3},{2,0},{3,1},{4,6},{5,7},{6,4},{7,5},{8,10},{9,11},{10,... | collective-permute-start | bytes 393224 | tf_op jit(solution)/shard_map/ppermute | solution.py:22
  50.5 8.8 %collective-permute-start.8 = (bf16[16,4096]{1,0:T(8,128)(2,1)S(1)}, bf16[16,4096]{1,0:T(8,128)(2,1)S(1)}, u32[]{:S(2)}, u32[]{:S(2)}) collective-permute-start(bf16[16,4096]{1,0:T(8,128)(2,1)S(1)} %get-tuple-element.32.refs_3_), channel_id=1, source_target_pairs={{0,1},{1,0},{2,3},{3,2},{4,5},{5,4},{6,7},{7,6},{8,9},{9,8},{10,11... | collective-permute-start | bytes 393224 | tf_op jit(solution)/shard_map/ppermute | solution.py:22
  53.1 6.8 %collective-permute-start.5 = (bf16[16,4096]{1,0:T(8,128)(2,1)S(1)}, bf16[16,4096]{1,0:T(8,128)(2,1)S(1)}, u32[]{:S(2)}, u32[]{:S(2)}) collective-permute-start(bf16[16,4096]{1,0:T(8,128)(2,1)S(1)} %get-tuple-element.33.refs_1_), channel_id=1, source_target_pairs={{0,1},{1,0},{2,3},{3,2},{4,5},{5,4},{6,7},{7,6},{8,9},{9,8},{10,11... | collective-permute-start | bytes 393224 | tf_op jit(solution)/shard_map/ppermute | solution.py:22
  56.4 15.8 %collective-permute-start.14 = (bf16[32,2048]{1,0:T(8,128)(2,1)S(1)}, bf16[32,2048]{1,0:T(8,128)(2,1)S(1)}, u32[]{:S(2)}, u32[]{:S(2)}) collective-permute-start(bf16[32,2048]{1,0:T(8,128)(2,1)S(1)} %get-tuple-element.42.refs_1_), channel_id=1, source_target_pairs={{0,1},{1,0},{2,3},{3,2},{4,5},{5,4},{6,7},{7,6},{8,9},{9,8},{10,11... | collective-permute-start | bytes 393224 | tf_op jit(solution)/shard_map/ppermute | solution.py:22
  56.5 18.3 %collective-permute-start.11 = (bf16[32,2048]{1,0:T(8,128)(2,1)S(1)}, bf16[32,2048]{1,0:T(8,128)(2,1)S(1)}, u32[]{:S(2)}, u32[]{:S(2)}) collective-permute-start(bf16[32,2048]{1,0:T(8,128)(2,1)S(1)} %get-tuple-element.43.refs_1_), channel_id=1, source_target_pairs={{0,1},{1,0},{2,3},{3,2},{4,5},{5,4},{6,7},{7,6},{8,9},{9,8},{10,11... | collective-permute-start | bytes 393224 | tf_op jit(solution)/shard_map/ppermute | solution.py:22

commit v2 on v0

v2 whole, which is shorter than its diff:
```python
import functools

import jax
import jax.numpy as jnp
from jax import lax
from jax.experimental import pallas as pl
from jax.experimental.pallas import tpu as pltpu
from jax.sharding import PartitionSpec as P

MIB = 1 << 20
VMEM = pl.BlockSpec(memory_space=pltpu.VMEM)
SMEM = pl.BlockSpec(memory_space=pltpu.SMEM)
ANY = pl.BlockSpec(memory_space=pl.ANY)
HBM = pl.BlockSpec(memory_space=pltpu.HBM)
LIMIT = 16 * MIB
FEAT_LIMIT = 16 * MIB
JA2 = False
JB2 = False
KBW = False
DEC_LIMIT = 24 * MIB
JOINT = False
EPARTS = 1
DPARTS = 2
ORDER = {
    "feat": lambda part, sums, ready: () if part == 0 else (sums[0],),
    "dec": lambda part, sums, ready: (sums[0],) if part == 0 else (ready[0],),
}


def tile(extent, most):
    best = extent
    for size in range(128, min(extent, most) + 1, 128):
        if extent % size == 0:
            best = size
    return best


def swap(x, axis, size, bit):
    return lax.ppermute(x, axis, [(i, i ^ bit) for i in range(size)])


def cost(rows, depth, columns, passed):
    return pl.CostEstimate(flops=2 * rows * depth * columns, bytes_accessed=passed, transcendentals=0)


def in_hbm(x):
    return pltpu.with_memory_space_constraint(x, pltpu.HBM)


def ordered(low, first, second):
    return jnp.concatenate([jnp.where(low, first, second), jnp.where(low, second, first)], axis=0)


def enc_part_kernel(steps, role_ref, x_ref, w_hbm, *refs):
    keep_ref, send_ref, w_ref, x_buf, acc, x_sem, sems = refs[-7:]
    half = keep_ref.shape[0]
    rows = w_ref.shape[0] // steps

    def get(i):
        here = pl.ds(i * rows, rows)
        return pltpu.make_async_copy(w_hbm.at[here], w_ref.at[here], sems.at[i])

    x_copy = pltpu.make_async_copy(x_ref, x_buf, x_sem)
    x_copy.start()
    for i in range(steps):
        get(i).start()
    x_copy.wait()
    x = ordered(role_ref[0] == 0, x_buf[:half], x_buf[half:])
    for i in range(steps):
        get(i).wait()
        here = slice(i * rows, (i + 1) * rows)
        out = jnp.dot(x[:, here], w_ref[here], preferred_element_type=jnp.float32)
        if i:
            out += acc[...]
        if i < steps - 1:
            acc[...] = out
        else:
            keep_ref[...] = out[:half]
            send_ref[...] = out[half:].astype(send_ref.dtype)


def enc_part(role, x, weight, after=()):
    rows, depth = x.shape
    feats = weight.shape[1]
    half = rows // 2
    steps = next(n for n in (9, 8, 4, 2, 1) if depth % (16 * n) == 0)
    return pl.pallas_call(
        functools.partial(enc_part_kernel, steps),
        in_specs=[SMEM, ANY, HBM] + [ANY] * len(after),
        out_specs=[VMEM, VMEM],
        out_shape=[
            jax.ShapeDtypeStruct((half, feats), jnp.float32),
            jax.ShapeDtypeStruct((half, feats), jnp.bfloat16),
        ],
        scratch_shapes=[
            pltpu.VMEM((depth, feats), jnp.bfloat16),
            pltpu.VMEM((rows, depth), jnp.bfloat16),
            pltpu.VMEM((rows, feats), jnp.float32),
            pltpu.SemaphoreType.DMA,
            pltpu.SemaphoreType.DMA((steps,)),
        ],
        compiler_params=pltpu.CompilerParams(vmem_limit_bytes=LIMIT),
        cost_estimate=cost(rows, depth, feats, 2 * depth * feats),
    )(role, x, in_hbm(weight), *after)


def feat_part_kernel(first, pieces, ids_ref, *refs):
    piece_refs, w_hbm = refs[:pieces], refs[pieces]
    keep_ref, send_ref, w_buf, acc, sems = refs[-5:]
    half, count = keep_ref.shape
    source = ids_ref[0]

    def get(k):
        return pltpu.make_async_copy(w_hbm.at[source ^ k, :, pl.ds(first, count)], w_buf.at[k], sems.at[k])

    for k in range(pieces):
        get(k).start()
    for k in range(pieces):
        rows = piece_refs[k][...]
        rows = jnp.where((source ^ k) >= source, rows, jnp.zeros_like(rows))
        rows = ordered(ids_ref[1] == 0, rows[:half], rows[half:])
        get(k).wait()
        out = jnp.dot(rows, w_buf[k], preferred_element_type=jnp.float32)
        if k:
            out += acc[...]
        if k < pieces - 1:
            acc[...] = out
        else:
            keep_ref[...] = out[:half]
            send_ref[...] = out[half:].astype(send_ref.dtype)


def feat_part(ids, grads, weight, first, count, after=()):
    tokens, depth = grads[0].shape
    half = tokens // 2
    return pl.pallas_call(
        functools.partial(feat_part_kernel, first, len(grads)),
        in_specs=[SMEM] + [VMEM] * len(grads) + [HBM] + [ANY] * len(after),
        out_specs=[VMEM, VMEM],
        out_shape=[
            jax.ShapeDtypeStruct((half, count), jnp.float32),
            jax.ShapeDtypeStruct((half, count), jnp.bfloat16),
        ],
        scratch_shapes=[
            pltpu.VMEM((len(grads), depth, count), jnp.bfloat16),
            pltpu.VMEM((tokens, count), jnp.float32),
            pltpu.SemaphoreType.DMA((len(grads),)),
        ],
        compiler_params=pltpu.CompilerParams(vmem_limit_bytes=FEAT_LIMIT),
        cost_estimate=cost(tokens, len(grads) * depth, count, 2 * len(grads) * depth * count),
    )(ids, *grads, in_hbm(weight), *after)


def dec_kernel(first_block, blocks, width, kept, ids_ref, grad_refs, act_refs, out_hbm, act_buf, out_buf, sems):
    source = ids_ref[0]
    first = ids_ref[2] == 0
    start = 0
    for mine_ref, other_ref in zip(act_refs[::2], act_refs[1::2]):
        for row in range(0, mine_ref.shape[0], kept):
            mine, other = mine_ref[row : row + kept], other_ref[row : row + kept]
            act_buf[start : start + kept] = jnp.where(first, mine, other)
            act_buf[start + kept : start + 2 * kept] = jnp.where(first, other, mine)
            start += 2 * kept
    steps = act_buf.shape[1] // width

    def put(b, j):
        columns = pl.ds(j * width, width)
        return pltpu.make_async_copy(
            out_buf.at[b, :, columns], out_hbm.at[source ^ (first_block + b), :, columns], sems.at[b, j]
        )

    for b in range(blocks):
        grad = grad_refs[first_block + b][...]
        grad = jnp.where((source ^ (first_block + b)) >= source, grad, jnp.zeros_like(grad)).T
        for j in range(steps):
            columns = slice(j * width, (j + 1) * width)
            out = jnp.dot(grad, act_buf[:, columns], preferred_element_type=jnp.float32)
            out_buf[b, :, columns] = out.astype(out_buf.dtype)
            put(b, j).start()
    for b in range(blocks):
        for j in range(steps):
            put(b, j).wait()


def dec_product(ids, grads, acts, kept, first, blocks, before=None, after=()):
    tokens, depth = grads[0].shape
    layers = len(grads)
    feats = acts[0].shape[1]
    held = () if before is None else (before,)
    width = tile(feats, 1024)

    def body(ids_ref, *refs):
        dec_kernel(
            first, blocks, width, kept, ids_ref, refs[:layers], refs[layers : layers + len(acts)], refs[-4], *refs[-3:]
        )

    return pl.pallas_call(
        body,
        in_specs=[SMEM] + [VMEM] * (layers + len(acts)) + [ANY] * (len(held) + len(after)),
        out_specs=HBM,
        out_shape=jax.ShapeDtypeStruct((layers, depth, feats), jnp.bfloat16),
        scratch_shapes=[
            pltpu.VMEM((tokens, feats), jnp.bfloat16),
            pltpu.VMEM((blocks, depth, feats), jnp.bfloat16),
            pltpu.SemaphoreType.DMA((blocks, feats // width)),
        ],
        input_output_aliases={1 + layers + len(acts): 0} if held else {},
        compiler_params=pltpu.CompilerParams(vmem_limit_bytes=DEC_LIMIT),
        cost_estimate=cost(blocks * tokens, depth, feats, 2 * blocks * depth * feats),
    )(ids, *grads, *acts, *held, *after)


def enc_kernel(first_column, width, res_refs, ids_ref, mine_ref, other_ref, enc_hbm, bias_hbm, feat_hbm, res_t, enc_buf, bias_buf, feat_buf, sems):
    count = enc_buf.shape[1]
    low, first = ids_ref[1] == 0, ids_ref[2] == 0
    res_t[...] = jnp.concatenate([ref[...] for ref in res_refs], axis=0).T
    mine, other = mine_ref[...], other_ref[...]
    feat_buf[...] = jnp.concatenate([jnp.where(first, mine, other), jnp.where(first, other, mine)], axis=0)
    here = pl.ds(first_column, count)
    puts = [pltpu.make_async_copy(feat_buf, feat_hbm.at[:, here], sems.at[0])]
    puts[0].start()
    grad = jnp.concatenate([jnp.where(low, mine, other), jnp.where(low, other, mine)], axis=0)
    for j in range(count // width):
        columns = slice(j * width, (j + 1) * width)
        out = jnp.dot(res_t[...], grad[:, columns], preferred_element_type=jnp.float32)
        enc_buf[:, columns] = out.astype(enc_buf.dtype)
        puts.append(
            pltpu.make_async_copy(
                enc_buf.at[:, columns], enc_hbm.at[:, pl.ds(first_column + j * width, width)], sems.at[2 + j]
            )
        )
        puts[-1].start()
    bias_buf[...] = jnp.sum(grad.astype(jnp.float32), axis=0, keepdims=True)
    puts.append(pltpu.make_async_copy(bias_buf, bias_hbm.at[:, here], sems.at[1]))
    puts[-1].start()
    for put in puts:
        put.wait()


def enc_product(ids, blocks, mine, other, first, feats, before=None, after=()):
    depth = blocks[0].shape[1]
    half, count = mine.shape
    tokens = 2 * half
    width = tile(count, 512)
    held = () if before is None else tuple(before)
    extra = len(held) + len(after)

    def body(ids_ref, *refs):
        ends = refs[len(blocks) + 2 + extra :]
        enc_kernel(first, width, refs[: len(blocks)], ids_ref, *refs[len(blocks) : len(blocks) + 2], *ends)

    at = 3 + len(blocks)
    return pl.pallas_call(
        body,
        in_specs=[SMEM] + [VMEM] * (len(blocks) + 2) + [ANY] * extra,
        out_specs=[HBM] * 3,
        out_shape=[
            jax.ShapeDtypeStruct((depth, feats), jnp.bfloat16),
            jax.ShapeDtypeStruct((1, feats), jnp.float32),
            jax.ShapeDtypeStruct((tokens, feats), jnp.bfloat16),
        ],
        scratch_shapes=[
            pltpu.VMEM((depth, tokens), jnp.bfloat16),
            pltpu.VMEM((depth, count), jnp.bfloat16),
            pltpu.VMEM((1, count), jnp.float32),
            pltpu.VMEM((tokens, count), jnp.bfloat16),
            pltpu.SemaphoreType.DMA((2 + count // width,)),
        ],
        input_output_aliases={at: 0, at + 1: 1, at + 2: 2} if held else {},
        compiler_params=pltpu.CompilerParams(vmem_limit_bytes=LIMIT),
        cost_estimate=cost(tokens, depth, count, 2 * depth * count),
    )(ids, *blocks, mine, other, *held, *after)


def rounded(x):
    return lax.reduce_precision(x, 8, 7)


def local(feat_size, layer_size, width_size, residuals, cotangent, enc_weight, enc_bias, dec_weight, active):
    layers = dec_weight.shape[1]
    source = lax.axis_index("layer")
    role = lax.axis_index("width") % 2
    res, cot = residuals[0], cotangent[0]
    own, depth = res.shape
    feats = enc_weight.shape[2]
    gate = active[0]
    tokens = gate.shape[0]
    half = tokens // 2
    weight = jnp.swapaxes(dec_weight[0], 1, 2)
    role_ref = jnp.reshape(role, (1,)).astype(jnp.int32)

    def neighbour(x):
        return swap(x, "width", width_size, 1)

    def across(x):
        bit, stage = 2, x
        while bit < width_size:
            x = rounded(x)
            stage = x.astype(jnp.bfloat16)
            x = x + swap(stage, "width", width_size, bit).astype(jnp.float32)
            bit *= 2
        return x, stage

    if feat_size == 2:
        place = lax.axis_index("feat")
        sent = lax.optimization_barrier(jnp.concatenate([res, cot], axis=0))
        other = swap(sent, "feat", 2, 1)
        blocks = [res, other[:own]]
        starts = [place * own, (1 - place) * own]
        grads = jnp.concatenate([sent[own:], other[own:]], axis=0)
    else:
        place = 0
        blocks = [lax.all_gather(res, "feat", axis=0, tiled=True)]
        starts = [0]
        grads = lax.all_gather(cot, "feat", axis=0, tiled=True)
    low = role ^ place
    ids = jnp.stack([source, low, role]).astype(jnp.int32)

    held, order = [grads], [0]
    bit = layer_size // 2
    while bit:
        got = swap(jnp.stack(held), "layer", layer_size, bit)
        held = held + [got[i] for i in range(len(held))]
        order = order + [o ^ bit for o in order]
        bit //= 2
    grads = [held[order.index(j)] for j in range(layer_size)]

    sides, gates, sums, ready, acts = [], [], [], [], []
    after = ()
    for rows, first in zip(blocks, starts):
        keep, send = enc_part(role_ref, in_hbm(rows) if rows is res else rows, enc_weight[0], after)
        after = (send,)
        sides.append(keep + neighbour(send).astype(jnp.float32))
        kept = keep.shape[0]
        gates.append(lax.dynamic_slice_in_dim(gate, first + role * kept, kept, 0).astype(jnp.float32))
    if JOINT:
        sides, gates = [jnp.concatenate(sides, axis=0)], [jnp.concatenate(gates, axis=0)]
    if KBW:
        whole = feat_part(ids, grads, weight, 0, feats, ORDER["feat"](0, sums, ready))
    for pair, mask in zip(sides, gates):
        total, stage = across(pair)
        sums.append(stage)
        act = ((total + enc_bias) * mask).astype(jnp.bfloat16)
        ready.append(act)
        if not JA2:
            acts += [act, neighbour(act)]
    if JA2:
        act = jnp.concatenate(ready, axis=0)
        acts = [act, neighbour(act)]

    parts = 2
    count = feats // parts
    mask = lax.dynamic_slice_in_dim(gate, role * half, half, 0).astype(jnp.float32)
    pairs, feat_sums, feat_ready = [], [], []
    for part in range(parts):
        if KBW:
            keep, send = [w[:, part * count : (part + 1) * count] for w in whole]
        else:
            keep, send = feat_part(ids, grads, weight, part * count, count, ORDER["feat"](part, sums, ready))
        pair = keep + neighbour(send).astype(jnp.float32)
        total, stage = across(pair)
        feat_sums.append(stage)
        grad = (total * mask[:, part * count : (part + 1) * count]).astype(jnp.bfloat16)
        feat_ready.append(grad)
        if not JB2:
            pairs.append((grad, neighbour(grad)))
    if JB2:
        grad = jnp.concatenate(feat_ready, axis=1)
        pairs = [(grad, neighbour(grad))]

    dec_grad = None
    for part in range(DPARTS):
        dec_grad = dec_product(ids, grads, acts, blocks[0].shape[0] // 2, part * layers // DPARTS, layers // DPARTS, dec_grad, ORDER["dec"](part, feat_sums, feat_ready))

    out = None
    if EPARTS == 1 and not JB2:
        pairs = [[jnp.concatenate(side, axis=1) for side in zip(*pairs)]]
    for part in range(EPARTS):
        out = enc_product(ids, blocks, *pairs[part], part * feats // EPARTS, feats, out)
    enc_grad, bias_grad, feat_grad = out
    return (jnp.swapaxes(dec_grad, 1, 2)[None], enc_grad[None], bias_grad, feat_grad[None])


def solution(mesh):
    in_specs = (
        P("layer", "feat", "width"),
        P("layer", "feat", "width"),
        P("layer", "width", "feat"),
        P("layer", "feat"),
        P("layer", None, "feat", "width"),
        P("layer", None, "feat"),
    )
    out_specs = (
        P("layer", None, "feat", "width"),
        P("layer", "width", "feat"),
        P("layer", "feat"),
        P("layer", None, "feat"),
    )
    sizes = (mesh.shape["feat"], mesh.shape["layer"], mesh.shape["width"])
    return jax.shard_map(
        functools.partial(local, *sizes), mesh=mesh, in_specs=in_specs, out_specs=out_specs, check_vma=False
    )
```

time: 144 us -> 61.3 us (0.43)
  blocking collectives: 50.2 us -> 0 us
  waiting for transfers between devices: 48.5 us -> 8.77 us
  Pallas kernels: 0 us -> 28.6 us
  matrix products: 28.3 us -> 0 us
  starting transfers between devices: 0.08 us -> 21.3 us
  between operations: 14.1 us -> 0.86 us
    all_gather x5 -> x0, blocking collectives: 50.2 us -> none  [the longest x1 16.1 us: local(): lax.all_gather(grad_share, 'width', axis=0, tiled=True)]
    reduce_scatter x2 -> x0, waiting for transfers between devices: 48.5 us -> none  [the longest x1 28.8 us: local(): lax.psum_scatter(enc_part, 'width', scatter_dimension=0, tiled=True)]
    pallas_call x0 -> x7, Pallas kernels: none -> 28.6 us  [the longest x2 9.82 us: feat_part(): pl.pallas_call(functools.partial(feat_part_kernel, first, len(grads)), in...]
    dot_general x4 -> x0, matrix products: 28.3 us -> none  [the longest x1 10.8 us: local(): jnp.einsum('ktd,kfd->tf', used_grads, dec_weight[0], preferred_element_ty...]
    ppermute x0 -> x15, starting transfers between devices: none -> 21.3 us  [swap(): return lax.ppermute(x, axis, [(i, i ^ bit) for i in range(size)])]
    ppermute x0 -> x15, waiting for transfers between devices: none -> 8.77 us  [swap(): return lax.ppermute(x, axis, [(i, i ^ bit) for i in range(size)])]
  transfers between devices with their start and end apart: 2 -> 15, of which waited for: 2 -> 4; matrix products, arithmetic and copies ran while one was open for 3% -> 1% of each run, Pallas kernels for 0% -> 41%
where the time goes in v2:
time: 61.3 us; the launch traced here: 61.1 us
  Pallas kernels  28.6 us (47%)
  starting transfers between devices  21.3 us (35%)
  waiting for transfers between devices  8.77 us (14%)
  other arithmetic  1.43 us (2%)
  between operations  0.86 us (1%)
    ppermute x15, starting transfers between devices, swap(): return lax.ppermute(x, axis, [(i, i ^ bit) for i in range(size)])  21.3 us
    pallas_call x2, Pallas kernels, feat_part(): pl.pallas_call(functools.partial(feat_part_kernel, first, len(grads)), in...  9.82 us
    pallas_call x2, Pallas kernels, dec_product(): pl.pallas_call(body, in_specs=[SMEM] + [VMEM] * (layers + len(acts)) + [A...  9.48 us
    ppermute x15, waiting for transfers between devices, swap(): return lax.ppermute(x, axis, [(i, i ^ bit) for i in range(size)])  8.77 us
    pallas_call x2, Pallas kernels, enc_part(): pl.pallas_call(functools.partial(enc_part_kernel, steps), in_specs=[SMEM,...  6.02 us
    pallas_call x1, Pallas kernels, enc_product(): pl.pallas_call(body, in_specs=[SMEM] + [VMEM] * (len(blocks) + 2) + [ANY]...  3.3 us
  transfers between devices with their start and end apart: 15, of which 4 were waited for; matrix products, arithmetic and copies ran while one was open for 1% of the time, Pallas kernels for 41%

profile of v2, /device:TPU:0, one launch (start us, length us, event | category | flops | bytes accessed | tf_op | source)
XLA Modules:
  0.0 61.1 jit_solution(399692116216054678)
XLA Ops:
  0.6 0.8 %pad_maximum_fusion.3 = bf16[64,576]{1,0:T(8,128)(2,1)S(1)} fusion(bf16[32,576]{1,0:T(8,128)(2,1)} %bitcast.44, bf16[32,576]{1,0:T(8,128)(2,1)} %bitcast.36), kind=kLoop, calls=%fused_computation.22 | loop fusion | flops 147456 | bytes 147456 | tf_op jit(solution)/shard_map/concatenate | solution.py:306
  1.4 3.0 %collective-permute-start = (bf16[64,576]{1,0:T(8,128)(2,1)S(1)}, bf16[64,576]{1,0:T(8,128)(2,1)S(1)}, u32[]{:S(2)}, u32[]{:S(2)}) collective-permute-start(bf16[64,576]{1,0:T(8,128)(2,1)S(1)} %pad_maximum_fusion.3), channel_id=1, source_target_pairs={{0,4},{4,0},{1,5},{5,1},{2,6},{6,2},{3,7},{7,3},{8,12},{12,8},{9,1... | collective-permute-start | bytes 221192 | tf_op jit(solution)/shard_map/ppermute | solution.py:39
  4.5 3.4 %shard_map.93 = (f32[16,4096]{1,0:T(8,128)S(1)}, bf16[16,4096]{1,0:T(8,128)(2,1)S(1)}) custom-call(s32[1]{0:T(128)} %bitcast.2.role_ref, bf16[32,576]{1,0:T(8,128)(2,1)} %bitcast.37, bf16[576,4096]{1,0:T(8,128)(2,1)} %bitcast.42), custom_call_target="tpu_custom_call" | custom-call | flops 150994944 | bytes 4718592 | tf_op jit(solution)/shard_map/pallas_call | solution.py:87
  7.9 1.6 %collective-permute-start.3 = (bf16[16,4096]{1,0:T(8,128)(2,1)S(1)}, bf16[16,4096]{1,0:T(8,128)(2,1)S(1)}, u32[]{:S(2)}, u32[]{:S(2)}) collective-permute-start(bf16[16,4096]{1,0:T(8,128)(2,1)S(1)} %get-tuple-element.16.refs_0_), channel_id=1, source_target_pairs={{0,1},{1,0},{2,3},{3,2},{4,5},{5,4},{6,7},{7,6},{8,9},{9,8},{10,11... | collective-permute-start | bytes 393224 | tf_op jit(solution)/shard_map/ppermute | solution.py:39
  9.5 0.1 pad_add_fusion.ids_ref
  9.6 0.0 collective-permute-done
  9.6 1.6 %collective-permute-start.1 = (bf16[1,64,576]{2,1,0:T(8,128)(2,1)S(1)}, bf16[1,64,576]{2,1,0:T(8,128)(2,1)S(1)}, u32[]{:S(2)}, u32[]{:S(2)}) collective-permute-start(bf16[1,64,576]{2,1,0:T(8,128)(2,1)S(1)} %get-tuple-element.34), channel_id=1, source_target_pairs={{0,16},{8,24},{16,0},{24,8},{1,17},{9,25},{17,1},{25,9},{2,18},{10... | collective-permute-start | bytes 221192 | tf_op jit(solution)/shard_map/ppermute | solution.py:39
  11.2 2.6 %shard_map.94 = (f32[16,4096]{1,0:T(8,128)S(1)}, bf16[16,4096]{1,0:T(8,128)(2,1)S(1)}) custom-call(s32[1]{0:T(128)} %bitcast.2.role_ref, bf16[32,576]{1,0:T(8,128)(2,1)S(1)} %get-tuple-element.32.x_ref.refs_1_, bf16[576,4096]{1,0:T(8,128)(2,1)} %bitcast.43, bf16[16,4096]{1,0:T(8,128)(2,1)S(1)} %get-tuple-element.16.refs_0_), custom_call_target="tpu_custom_call" | custom-call | flops 150994944 | bytes 4718592 | tf_op jit(solution)/shard_map/pallas_call | solution.py:87
  13.8 0.5 collective-permute-start.6
  14.3 0.0 collective-permute-done.3
  14.4 2.7 %collective-permute-start.4 = (bf16[16,4096]{1,0:T(8,128)(2,1)S(1)}, bf16[16,4096]{1,0:T(8,128)(2,1)S(1)}, u32[]{:S(2)}, u32[]{:S(2)}) collective-permute-start(bf16[16,4096]{1,0:T(8,128)(2,1)S(1)} %fusion.4.refs_5_), channel_id=1, source_target_pairs={{0,2},{1,3},{2,0},{3,1},{4,6},{5,7},{6,4},{7,5},{8,10},{9,11},{10,... | collective-permute-start | bytes 393224 | tf_op jit(solution)/shard_map/ppermute | solution.py:39
  17.0 0.0 collective-permute-done.1
  17.1 0.1 collective-permute-start.2
  17.1 2.7 %collective-permute-done.6 = bf16[16,4096]{1,0:T(8,128)(2,1)S(1)} collective-permute-done((bf16[16,4096]{1,0:T(8,128)(2,1)S(1)}, bf16[16,4096]{1,0:T(8,128)(2,1)S(1)}, u32[]{:S(2)}, u32[]{:S(2)}) %collective-permute-start.6) | collective-permute-done | bytes 131104 | tf_op jit(solution)/shard_map/ppermute | solution.py:39
  19.9 2.5 %collective-permute-start.7 = (bf16[16,4096]{1,0:T(8,128)(2,1)S(1)}, bf16[16,4096]{1,0:T(8,128)(2,1)S(1)}, u32[]{:S(2)}, u32[]{:S(2)}) collective-permute-start(bf16[16,4096]{1,0:T(8,128)(2,1)S(1)} %fusion.5), channel_id=1, source_target_pairs={{0,2},{1,3},{2,0},{3,1},{4,6},{5,7},{6,4},{7,5},{8,10},{9,11},{10,... | collective-permute-start | bytes 393224 | tf_op jit(solution)/shard_map/ppermute | solution.py:39
  22.4 0.0 collective-permute-done.2
  22.4 0.0 copy-start.1
  22.4 0.0 copy-start.2
  22.4 4.9 %shard_map.95 = (f32[32,2048]{1,0:T(8,128)S(1)}, bf16[32,2048]{1,0:T(8,128)(2,1)S(1)}) custom-call(s32[3]{0:T(128)S(1)} %pad_add_fusion.ids_ref, bf16[64,576]{1,0:T(8,128)(2,1)S(1)} %get-tuple-element.35.refs_0_, bf16[64,576]{1,0:T(8,128)(2,1)S(1)} %get-tuple-element.31.refs_1_, bf16[64,576]{1,0:T(8,128)(2,1)S(1)} %bitcast.32, ...), custom_call_target="tpu_custom_call" | custom-call | flops 603979776 | bytes 9437184 | tf_op jit(solution)/shard_map/pallas_call | solution.py:136
  27.3 0.7 %collective-permute-start.9 = (bf16[32,2048]{1,0:T(8,128)(2,1)S(1)}, bf16[32,2048]{1,0:T(8,128)(2,1)S(1)}, u32[]{:S(2)}, u32[]{:S(2)}) collective-permute-start(bf16[32,2048]{1,0:T(8,128)(2,1)S(1)} %get-tuple-element.20), channel_id=1, source_target_pairs={{0,1},{1,0},{2,3},{3,2},{4,5},{5,4},{6,7},{7,6},{8,9},{9,8},{10,11... | collective-permute-start | bytes 393224 | tf_op jit(solution)/shard_map/ppermute | solution.py:39
  28.1 4.9 %shard_map.98 = (f32[32,2048]{1,0:T(8,128)S(1)}, bf16[32,2048]{1,0:T(8,128)(2,1)S(1)}) custom-call(s32[3]{0:T(128)S(1)} %pad_add_fusion.ids_ref, bf16[64,576]{1,0:T(8,128)(2,1)S(1)} %get-tuple-element.35.refs_0_, bf16[64,576]{1,0:T(8,128)(2,1)S(1)} %get-tuple-element.31.refs_1_, bf16[64,576]{1,0:T(8,128)(2,1)S(1)} %bitcast.33, ...), custom_call_target="tpu_custom_call" | custom-call | flops 603979776 | bytes 9437184 | tf_op jit(solution)/shard_map/pallas_call | solution.py:136
  33.0 1.4 %collective-permute-start.11 = (bf16[32,2048]{1,0:T(8,128)(2,1)S(1)}, bf16[32,2048]{1,0:T(8,128)(2,1)S(1)}, u32[]{:S(2)}, u32[]{:S(2)}) collective-permute-start(bf16[32,2048]{1,0:T(8,128)(2,1)S(1)} %get-tuple-element.22), channel_id=1, source_target_pairs={{0,1},{1,0},{2,3},{3,2},{4,5},{5,4},{6,7},{7,6},{8,9},{9,8},{10,11... | collective-permute-start | bytes 393224 | tf_op jit(solution)/shard_map/ppermute | solution.py:39
  34.4 0.0 collective-permute-done.4
  34.4 0.0 collective-permute-done.7
  34.4 0.0 copy-done.1
  34.4 0.0 copy-done.2
  34.4 0.2 fusion.2
  34.6 0.7 %collective-permute-start.5 = (bf16[16,4096]{1,0:T(8,128)(2,1)S(1)}, bf16[16,4096]{1,0:T(8,128)(2,1)S(1)}, u32[]{:S(2)}, u32[]{:S(2)}) collective-permute-start(bf16[16,4096]{1,0:T(8,128)(2,1)S(1)} %get-tuple-element.27.refs_4_), channel_id=1, source_target_pairs={{0,1},{1,0},{2,3},{3,2},{4,5},{5,4},{6,7},{7,6},{8,9},{9,8},{10,11... | collective-permute-start | bytes 393224 | tf_op jit(solution)/shard_map/ppermute | solution.py:39
  35.4 1.4 %collective-permute-start.8 = (bf16[16,4096]{1,0:T(8,128)(2,1)S(1)}, bf16[16,4096]{1,0:T(8,128)(2,1)S(1)}, u32[]{:S(2)}, u32[]{:S(2)}) collective-permute-start(bf16[16,4096]{1,0:T(8,128)(2,1)S(1)} %get-tuple-element.26.refs_6_), channel_id=1, source_target_pairs={{0,1},{1,0},{2,3},{3,2},{4,5},{5,4},{6,7},{7,6},{8,9},{9,8},{10,11... | collective-permute-start | bytes 393224 | tf_op jit(solution)/shard_map/ppermute | solution.py:39
  36.7 4.1 %collective-permute-done.11 = bf16[32,2048]{1,0:T(8,128)(2,1)S(1)} collective-permute-done((bf16[32,2048]{1,0:T(8,128)(2,1)S(1)}, bf16[32,2048]{1,0:T(8,128)(2,1)S(1)}, u32[]{:S(2)}, u32[]{:S(2)}) %collective-permute-start.11) | collective-permute-done | bytes 131104 | tf_op jit(solution)/shard_map/ppermute | solution.py:39
  40.8 0.1 collective-permute-start.12
  40.9 0.0 collective-permute-done.9
  40.9 3.0 %collective-permute-start.10 = (bf16[32,2048]{1,0:T(8,128)(2,1)S(1)}, bf16[32,2048]{1,0:T(8,128)(2,1)S(1)}, u32[]{:S(2)}, u32[]{:S(2)}) collective-permute-start(bf16[32,2048]{1,0:T(8,128)(2,1)S(1)} %fusion.6.refs_8_), channel_id=1, source_target_pairs={{0,2},{1,3},{2,0},{3,1},{4,6},{5,7},{6,4},{7,5},{8,10},{9,11},{10,... | collective-permute-start | bytes 393224 | tf_op jit(solution)/shard_map/ppermute | solution.py:39
  43.9 0.0 collective-permute-done.5.refs_5_
  43.9 0.0 collective-permute-done.8.refs_7_
  44.0 4.7 %shard_map.96.refs_8_ = bf16[4,576,4096]{2,1,0:T(8,128)(2,1)} custom-call(s32[3]{0:T(128)S(1)} %pad_add_fusion.ids_ref, bf16[64,576]{1,0:T(8,128)(2,1)S(1)} %get-tuple-element.35.refs_0_, bf16[64,576]{1,0:T(8,128)(2,1)S(1)} %get-tuple-element.31.refs_1_, bf16[64,576]{1,0:T(8,128)(2,1)S(1)} %bitcast.34, bf16[64,576]{1,0:T(8,128)(2,1)S(1)} %get-tuple-element.30.refs_3_, ...), custom_call_target="tpu_custom_call" | custom-call | flops 603979776 | bytes 9437184 | tf_op jit(solution)/shard_map/pallas_call | solution.py:197
  48.7 0.6 collective-permute-done.12
  49.3 1.4 %collective-permute-done.10 = bf16[32,2048]{1,0:T(8,128)(2,1)S(1)} collective-permute-done((bf16[32,2048]{1,0:T(8,128)(2,1)S(1)}, bf16[32,2048]{1,0:T(8,128)(2,1)S(1)}, u32[]{:S(2)}, u32[]{:S(2)}) %collective-permute-start.10) | collective-permute-done | bytes 131104 | tf_op jit(solution)/shard_map/ppermute | solution.py:39
  50.7 0.1 fusion
  50.8 0.1 collective-permute-start.14
  50.9 2.0 %collective-permute-start.13 = (bf16[32,2048]{1,0:T(8,128)(2,1)S(1)}, bf16[32,2048]{1,0:T(8,128)(2,1)S(1)}, u32[]{:S(2)}, u32[]{:S(2)}) collective-permute-start(bf16[32,2048]{1,0:T(8,128)(2,1)S(1)} %get-tuple-element.29.refs_9_), channel_id=1, source_target_pairs={{0,1},{1,0},{2,3},{3,2},{4,5},{5,4},{6,7},{7,6},{8,9},{9,8},{10,11... | collective-permute-start | bytes 393224 | tf_op jit(solution)/shard_map/ppermute | solution.py:39
  53.0 0.0 copy-start
  53.0 4.7 %shard_map.97 = bf16[4,576,4096]{2,1,0:T(8,128)(2,1)} custom-call(s32[3]{0:T(128)S(1)} %pad_add_fusion.ids_ref, bf16[64,576]{1,0:T(8,128)(2,1)S(1)} %get-tuple-element.35.refs_0_, bf16[64,576]{1,0:T(8,128)(2,1)S(1)} %get-tuple-element.31.refs_1_, bf16[64,576]{1,0:T(8,128)(2,1)S(1)} %bitcast.35, ...), custom_call_target="tpu_custom_call", output_to_operand_aliasing={{}: (9, {})} | custom-call | flops 603979776 | bytes 9437184 | tf_op jit(solution)/shard_map/pallas_call | solution.py:197
  57.7 0.0 collective-permute-done.14
  57.7 0.0 collective-permute-done.13
  57.8 0.0 copy-done
  57.8 3.3 %shard_map.99 = (bf16[576,4096]{1,0:T(8,128)(2,1)}, f32[1,4096]{1,0:T(1,128)}, bf16[64,4096]{1,0:T(8,128)(2,1)}) custom-call(s32[3]{0:T(128)S(1)} %pad_add_fusion.ids_ref, bf16[32,576]{1,0:T(8,128)(2,1)S(1)} %bitcast.38, bf16[32,576]{1,0:T(8,128)(2,1)S(1)} %get-tuple-element.32.x_ref.refs_1_, bf16[32,4096]{1,0:T(8,128)(2,1)S(1)} %pad_maximum_fusion.refs_2_, ...), custom_call_target="tpu_custom_call" | custom-call | flops 301989888 | bytes 4718592 | tf_op jit(solution)/shard_map/pallas_call | solution.py:253
  (12 shorter events, 0.3 us)
Async XLA Ops:
  1.4 8.2 %collective-permute-start = (bf16[64,576]{1,0:T(8,128)(2,1)S(1)}, bf16[64,576]{1,0:T(8,128)(2,1)S(1)}, u32[]{:S(2)}, u32[]{:S(2)}) collective-permute-start(bf16[64,576]{1,0:T(8,128)(2,1)S(1)} %pad_maximum_fusion.3), channel_id=1, source_target_pairs={{0,4},{4,0},{1,5},{5,1},{2,6},{6,2},{3,7},{7,3},{8,12},{12,8},{9,1... | collective-permute-start | bytes 221192 | tf_op jit(solution)/shard_map/ppermute | solution.py:39
  7.9 6.5 %collective-permute-start.3 = (bf16[16,4096]{1,0:T(8,128)(2,1)S(1)}, bf16[16,4096]{1,0:T(8,128)(2,1)S(1)}, u32[]{:S(2)}, u32[]{:S(2)}) collective-permute-start(bf16[16,4096]{1,0:T(8,128)(2,1)S(1)} %get-tuple-element.16.refs_0_), channel_id=1, source_target_pairs={{0,1},{1,0},{2,3},{3,2},{4,5},{5,4},{6,7},{7,6},{8,9},{9,8},{10,11... | collective-permute-start | bytes 393224 | tf_op jit(solution)/shard_map/ppermute | solution.py:39
  9.6 7.4 %collective-permute-start.1 = (bf16[1,64,576]{2,1,0:T(8,128)(2,1)S(1)}, bf16[1,64,576]{2,1,0:T(8,128)(2,1)S(1)}, u32[]{:S(2)}, u32[]{:S(2)}) collective-permute-start(bf16[1,64,576]{2,1,0:T(8,128)(2,1)S(1)} %get-tuple-element.34), channel_id=1, source_target_pairs={{0,16},{8,24},{16,0},{24,8},{1,17},{9,25},{17,1},{25,9},{2,18},{10... | collective-permute-start | bytes 221192 | tf_op jit(solution)/shard_map/ppermute | solution.py:39
  13.8 6.0 %collective-permute-start.6 = (bf16[16,4096]{1,0:T(8,128)(2,1)S(1)}, bf16[16,4096]{1,0:T(8,128)(2,1)S(1)}, u32[]{:S(2)}, u32[]{:S(2)}) collective-permute-start(bf16[16,4096]{1,0:T(8,128)(2,1)S(1)} %get-tuple-element.18), channel_id=1, source_target_pairs={{0,1},{1,0},{2,3},{3,2},{4,5},{5,4},{6,7},{7,6},{8,9},{9,8},{10,11... | collective-permute-start | bytes 393224 | tf_op jit(solution)/shard_map/ppermute | solution.py:39
  14.4 20.1 %collective-permute-start.4 = (bf16[16,4096]{1,0:T(8,128)(2,1)S(1)}, bf16[16,4096]{1,0:T(8,128)(2,1)S(1)}, u32[]{:S(2)}, u32[]{:S(2)}) collective-permute-start(bf16[16,4096]{1,0:T(8,128)(2,1)S(1)} %fusion.4.refs_5_), channel_id=1, source_target_pairs={{0,2},{1,3},{2,0},{3,1},{4,6},{5,7},{6,4},{7,5},{8,10},{9,11},{10,... | collective-permute-start | bytes 393224 | tf_op jit(solution)/shard_map/ppermute | solution.py:39
  17.1 5.3 %collective-permute-start.2 = (bf16[2,64,576]{2,1,0:T(8,128)(2,1)S(1)}, bf16[2,64,576]{2,1,0:T(8,128)(2,1)S(1)}, u32[]{:S(2)}, u32[]{:S(2)}) collective-permute-start(bf16[2,64,576]{2,1,0:T(8,128)(2,1)S(1)} %pad_maximum_fusion.2), channel_id=1, source_target_pairs={{0,8},{8,0},{16,24},{24,16},{1,9},{9,1},{17,25},{25,17},{2,10},{10... | collective-permute-start | bytes 442376 | tf_op jit(solution)/shard_map/ppermute | solution.py:39
  19.9 14.6 %collective-permute-start.7 = (bf16[16,4096]{1,0:T(8,128)(2,1)S(1)}, bf16[16,4096]{1,0:T(8,128)(2,1)S(1)}, u32[]{:S(2)}, u32[]{:S(2)}) collective-permute-start(bf16[16,4096]{1,0:T(8,128)(2,1)S(1)} %fusion.5), channel_id=1, source_target_pairs={{0,2},{1,3},{2,0},{3,1},{4,6},{5,7},{6,4},{7,5},{8,10},{9,11},{10,... | collective-permute-start | bytes 393224 | tf_op jit(solution)/shard_map/ppermute | solution.py:39
  22.4 12.0 %copy-start.1 = (s32[1,64,4096]{2,1,0:T(8,128)S(1)}, s32[1,64,4096]{2,1,0:T(8,128)}, u32[]{:S(2)}) copy-start(s32[1,64,4096]{2,1,0:T(8,128)} %param.11) | copy-start | bytes 3145732
  22.4 12.0 %copy-start.2 = (f32[1,4096]{1,0:T(1,128)S(1)}, f32[1,4096]{1,0:T(1,128)}, u32[]{:S(2)}) copy-start(f32[1,4096]{1,0:T(1,128)} %param.9) | copy-start | bytes 49156
  27.3 13.5 %collective-permute-start.9 = (bf16[32,2048]{1,0:T(8,128)(2,1)S(1)}, bf16[32,2048]{1,0:T(8,128)(2,1)S(1)}, u32[]{:S(2)}, u32[]{:S(2)}) collective-permute-start(bf16[32,2048]{1,0:T(8,128)(2,1)S(1)} %get-tuple-element.20), channel_id=1, source_target_pairs={{0,1},{1,0},{2,3},{3,2},{4,5},{5,4},{6,7},{7,6},{8,9},{9,8},{10,11... | collective-permute-start | bytes 393224 | tf_op jit(solution)/shard_map/ppermute | solution.py:39
  33.0 7.8 %collective-permute-start.11 = (bf16[32,2048]{1,0:T(8,128)(2,1)S(1)}, bf16[32,2048]{1,0:T(8,128)(2,1)S(1)}, u32[]{:S(2)}, u32[]{:S(2)}) collective-permute-start(bf16[32,2048]{1,0:T(8,128)(2,1)S(1)} %get-tuple-element.22), channel_id=1, source_target_pairs={{0,1},{1,0},{2,3},{3,2},{4,5},{5,4},{6,7},{7,6},{8,9},{9,8},{10,11... | collective-permute-start | bytes 393224 | tf_op jit(solution)/shard_map/ppermute | solution.py:39
  34.6 9.3 %collective-permute-start.5 = (bf16[16,4096]{1,0:T(8,128)(2,1)S(1)}, bf16[16,4096]{1,0:T(8,128)(2,1)S(1)}, u32[]{:S(2)}, u32[]{:S(2)}) collective-permute-start(bf16[16,4096]{1,0:T(8,128)(2,1)S(1)} %get-tuple-element.27.refs_4_), channel_id=1, source_target_pairs={{0,1},{1,0},{2,3},{3,2},{4,5},{5,4},{6,7},{7,6},{8,9},{9,8},{10,11... | collective-permute-start | bytes 393224 | tf_op jit(solution)/shard_map/ppermute | solution.py:39
  35.4 8.6 %collective-permute-start.8 = (bf16[16,4096]{1,0:T(8,128)(2,1)S(1)}, bf16[16,4096]{1,0:T(8,128)(2,1)S(1)}, u32[]{:S(2)}, u32[]{:S(2)}) collective-permute-start(bf16[16,4096]{1,0:T(8,128)(2,1)S(1)} %get-tuple-element.26.refs_6_), channel_id=1, source_target_pairs={{0,1},{1,0},{2,3},{3,2},{4,5},{5,4},{6,7},{7,6},{8,9},{9,8},{10,11... | collective-permute-start | bytes 393224 | tf_op jit(solution)/shard_map/ppermute | solution.py:39
  40.8 8.5 %collective-permute-start.12 = (bf16[32,2048]{1,0:T(8,128)(2,1)S(1)}, bf16[32,2048]{1,0:T(8,128)(2,1)S(1)}, u32[]{:S(2)}, u32[]{:S(2)}) collective-permute-start(bf16[32,2048]{1,0:T(8,128)(2,1)S(1)} %fusion.7), channel_id=1, source_target_pairs={{0,2},{1,3},{2,0},{3,1},{4,6},{5,7},{6,4},{7,5},{8,10},{9,11},{10,... | collective-permute-start | bytes 393224 | tf_op jit(solution)/shard_map/ppermute | solution.py:39
  40.9 9.8 %collective-permute-start.10 = (bf16[32,2048]{1,0:T(8,128)(2,1)S(1)}, bf16[32,2048]{1,0:T(8,128)(2,1)S(1)}, u32[]{:S(2)}, u32[]{:S(2)}) collective-permute-start(bf16[32,2048]{1,0:T(8,128)(2,1)S(1)} %fusion.6.refs_8_), channel_id=1, source_target_pairs={{0,2},{1,3},{2,0},{3,1},{4,6},{5,7},{6,4},{7,5},{8,10},{9,11},{10,... | collective-permute-start | bytes 393224 | tf_op jit(solution)/shard_map/ppermute | solution.py:39
  50.8 6.9 %collective-permute-start.14 = (bf16[32,2048]{1,0:T(8,128)(2,1)S(1)}, bf16[32,2048]{1,0:T(8,128)(2,1)S(1)}, u32[]{:S(2)}, u32[]{:S(2)}) collective-permute-start(bf16[32,2048]{1,0:T(8,128)(2,1)S(1)} %get-tuple-element.28), channel_id=1, source_target_pairs={{0,1},{1,0},{2,3},{3,2},{4,5},{5,4},{6,7},{7,6},{8,9},{9,8},{10,11... | collective-permute-start | bytes 393224 | tf_op jit(solution)/shard_map/ppermute | solution.py:39
  50.9 6.8 %collective-permute-start.13 = (bf16[32,2048]{1,0:T(8,128)(2,1)S(1)}, bf16[32,2048]{1,0:T(8,128)(2,1)S(1)}, u32[]{:S(2)}, u32[]{:S(2)}) collective-permute-start(bf16[32,2048]{1,0:T(8,128)(2,1)S(1)} %get-tuple-element.29.refs_9_), channel_id=1, source_target_pairs={{0,1},{1,0},{2,3},{3,2},{4,5},{5,4},{6,7},{7,6},{8,9},{9,8},{10,11... | collective-permute-start | bytes 393224 | tf_op jit(solution)/shard_map/ppermute | solution.py:39
  53.0 4.8 %copy-start = (bf16[1,32,576]{2,1,0:T(8,128)(2,1)S(1)}, bf16[1,32,576]{2,1,0:T(8,128)(2,1)}, u32[]{:S(2)}) copy-start(bf16[1,32,576]{2,1,0:T(8,128)(2,1)} %param.6) | copy-start | bytes 110596

commit v3 on v2

v3 whole, which is shorter than its diff:
```python
import functools

import jax
import jax.numpy as jnp
from jax import lax
from jax.experimental import pallas as pl
from jax.experimental.pallas import tpu as pltpu
from jax.sharding import PartitionSpec as P

MIB = 1 << 20
VMEM = pl.BlockSpec(memory_space=pltpu.VMEM)
ANY = pl.BlockSpec(memory_space=pl.ANY)
HBM = pl.BlockSpec(memory_space=pltpu.HBM)
LIMIT = 16 * MIB
DEC_LIMIT = 24 * MIB


def tile(extent, most):
    best = extent
    for size in range(128, min(extent, most) + 1, 128):
        if extent % size == 0:
            best = size
    return best


def swap(x, axis, size, bit):
    return lax.ppermute(x, axis, [(i, i ^ bit) for i in range(size)])


def cost(rows, depth, columns, passed):
    return pl.CostEstimate(flops=2 * rows * depth * columns, bytes_accessed=passed, transcendentals=0)


def in_hbm(x):
    return pltpu.with_memory_space_constraint(x, pltpu.HBM)


def place_of(feat_size):
    role = lax.rem(lax.axis_index("width"), 2)
    place = lax.axis_index("feat") if feat_size == 2 else 0
    return lax.axis_index("layer"), role ^ place, role


def ordered(low, first, second):
    return jnp.concatenate([jnp.where(low, first, second), jnp.where(low, second, first)], axis=0)


def enc_part_kernel(steps, x_ref, w_hbm, *refs):
    keep_ref, send_ref, w_ref, x_buf, acc, x_sem, sems = refs[-7:]
    half = keep_ref.shape[0]
    rows = w_ref.shape[0] // steps

    def get(i):
        here = pl.ds(i * rows, rows)
        return pltpu.make_async_copy(w_hbm.at[here], w_ref.at[here], sems.at[i])

    x_copy = pltpu.make_async_copy(x_ref, x_buf, x_sem)
    x_copy.start()
    for i in range(steps):
        get(i).start()
    x_copy.wait()
    x = ordered(place_of(0)[2] == 0, x_buf[:half], x_buf[half:])
    for i in range(steps):
        get(i).wait()
        here = slice(i * rows, (i + 1) * rows)
        out = jnp.dot(x[:, here], w_ref[here], preferred_element_type=jnp.float32)
        if i:
            out += acc[...]
        if i < steps - 1:
            acc[...] = out
        else:
            keep_ref[...] = out[:half]
            send_ref[...] = out[half:].astype(send_ref.dtype)


def enc_part(x, weight, after=()):
    rows, depth = x.shape
    feats = weight.shape[1]
    half = rows // 2
    steps = next(n for n in (3, 2, 1) if depth % (16 * n) == 0)
    return pl.pallas_call(
        functools.partial(enc_part_kernel, steps),
        in_specs=[ANY, HBM] + [ANY] * len(after),
        out_specs=[VMEM, VMEM],
        out_shape=[
            jax.ShapeDtypeStruct((half, feats), jnp.float32),
            jax.ShapeDtypeStruct((half, feats), jnp.bfloat16),
        ],
        scratch_shapes=[
            pltpu.VMEM((depth, feats), jnp.bfloat16),
            pltpu.VMEM((rows, depth), jnp.bfloat16),
            pltpu.VMEM((rows, feats), jnp.float32),
            pltpu.SemaphoreType.DMA,
            pltpu.SemaphoreType.DMA((steps,)),
        ],
        compiler_params=pltpu.CompilerParams(vmem_limit_bytes=LIMIT),
        cost_estimate=cost(rows, depth, feats, 2 * depth * feats),
    )(x, in_hbm(weight), *after)


def feat_part_kernel(feat_size, first, pieces, *refs):
    piece_refs, w_hbm = refs[:pieces], refs[pieces]
    keep_ref, send_ref, w_buf, acc, sems = refs[-5:]
    half, count = keep_ref.shape
    source, low, _ = place_of(feat_size)

    def get(k):
        return pltpu.make_async_copy(w_hbm.at[source ^ k, :, pl.ds(first, count)], w_buf.at[k], sems.at[k])

    for k in range(pieces):
        get(k).start()
    for k in range(pieces):
        rows = piece_refs[k][...]
        rows = jnp.where((source ^ k) >= source, rows, jnp.zeros_like(rows))
        rows = ordered(low == 0, rows[:half], rows[half:])
        get(k).wait()
        out = jnp.dot(rows, w_buf[k], preferred_element_type=jnp.float32)
        if k:
            out += acc[...]
        if k < pieces - 1:
            acc[...] = out
        else:
            keep_ref[...] = out[:half]
            send_ref[...] = out[half:].astype(send_ref.dtype)


def feat_part(feat_size, grads, weight, first, count, after=()):
    tokens, depth = grads[0].shape
    half = tokens // 2
    return pl.pallas_call(
        functools.partial(feat_part_kernel, feat_size, first, len(grads)),
        in_specs=[VMEM] * len(grads) + [HBM] + [ANY] * len(after),
        out_specs=[VMEM, VMEM],
        out_shape=[
            jax.ShapeDtypeStruct((half, count), jnp.float32),
            jax.ShapeDtypeStruct((half, count), jnp.bfloat16),
        ],
        scratch_shapes=[
            pltpu.VMEM((len(grads), depth, count), jnp.bfloat16),
            pltpu.VMEM((tokens, count), jnp.float32),
            pltpu.SemaphoreType.DMA((len(grads),)),
        ],
        compiler_params=pltpu.CompilerParams(vmem_limit_bytes=LIMIT),
        cost_estimate=cost(tokens, len(grads) * depth, count, 2 * len(grads) * depth * count),
    )(*grads, in_hbm(weight), *after)


def dec_kernel(first_block, blocks, width, kept, grad_refs, act_refs, out_hbm, act_buf, out_buf, sems):
    source, _, role = place_of(0)
    first = role == 0
    start = 0
    for mine_ref, other_ref in zip(act_refs[::2], act_refs[1::2]):
        for row in range(0, mine_ref.shape[0], kept):
            mine, other = mine_ref[row : row + kept], other_ref[row : row + kept]
            act_buf[start : start + kept] = jnp.where(first, mine, other)
            act_buf[start + kept : start + 2 * kept] = jnp.where(first, other, mine)
            start += 2 * kept
    steps = act_buf.shape[1] // width

    def put(b, j):
        columns = pl.ds(j * width, width)
        return pltpu.make_async_copy(
            out_buf.at[b, :, columns], out_hbm.at[source ^ (first_block + b), :, columns], sems.at[b, j]
        )

    for b in range(blocks):
        grad = grad_refs[first_block + b][...]
        grad = jnp.where((source ^ (first_block + b)) >= source, grad, jnp.zeros_like(grad)).T
        for j in range(steps):
            columns = slice(j * width, (j + 1) * width)
            out = jnp.dot(grad, act_buf[:, columns], preferred_element_type=jnp.float32)
            out_buf[b, :, columns] = out.astype(out_buf.dtype)
            put(b, j).start()
    for b in range(blocks):
        for j in range(steps):
            put(b, j).wait()


def dec_product(grads, acts, kept, first, blocks, before=None, after=()):
    tokens, depth = grads[0].shape
    layers = len(grads)
    feats = acts[0].shape[1]
    held = () if before is None else (before,)
    width = tile(feats, 1024)

    def body(*refs):
        dec_kernel(
            first, blocks, width, kept, refs[:layers], refs[layers : layers + len(acts)], refs[-4], *refs[-3:]
        )

    return pl.pallas_call(
        body,
        in_specs=[VMEM] * (layers + len(acts)) + [ANY] * (len(held) + len(after)),
        out_specs=HBM,
        out_shape=jax.ShapeDtypeStruct((layers, depth, feats), jnp.bfloat16),
        scratch_shapes=[
            pltpu.VMEM((tokens, feats), jnp.bfloat16),
            pltpu.VMEM((blocks, depth, feats), jnp.bfloat16),
            pltpu.SemaphoreType.DMA((blocks, feats // width)),
        ],
        input_output_aliases={layers + len(acts): 0} if held else {},
        compiler_params=pltpu.CompilerParams(vmem_limit_bytes=DEC_LIMIT),
        cost_estimate=cost(blocks * tokens, depth, feats, 2 * blocks * depth * feats),
    )(*grads, *acts, *held, *after)


def enc_kernel(feat_size, width, res_refs, mine_refs, other_refs, outs, res_t, enc_buf, bias_buf, feat_buf, sems):
    enc_hbm, bias_hbm, feat_hbm = outs
    _, low, role = place_of(feat_size)
    low, first = low == 0, role == 0
    res_t[...] = jnp.concatenate([ref[...] for ref in res_refs], axis=0).T
    puts = []

    def put(source, target):
        puts.append(pltpu.make_async_copy(source, target, sems.at[len(puts)]))
        puts[-1].start()

    start = 0
    for mine_ref, other_ref in zip(mine_refs, other_refs):
        count = mine_ref.shape[1]
        here = pl.ds(start, count)
        mine, other = mine_ref[...], other_ref[...]
        feat_buf[:, here] = jnp.concatenate([jnp.where(first, mine, other), jnp.where(first, other, mine)], axis=0)
        put(feat_buf.at[:, here], feat_hbm.at[:, here])
        grad = jnp.concatenate([jnp.where(low, mine, other), jnp.where(low, other, mine)], axis=0)
        for j in range(0, count, width):
            out = jnp.dot(res_t[...], grad[:, j : j + width], preferred_element_type=jnp.float32)
            columns = pl.ds(start + j, width)
            enc_buf[:, columns] = out.astype(enc_buf.dtype)
            put(enc_buf.at[:, columns], enc_hbm.at[:, columns])
        bias_buf[:, here] = jnp.sum(grad.astype(jnp.float32), axis=0, keepdims=True)
        start += count
    put(bias_buf, bias_hbm)
    for copy in puts:
        copy.wait()


def enc_product(feat_size, blocks, mine, others):
    depth = blocks[0].shape[1]
    tokens = 2 * mine[0].shape[0]
    feats = sum(x.shape[1] for x in mine)
    width = tile(mine[0].shape[1], 512)
    ends = [len(blocks), len(blocks) + len(mine), len(blocks) + 2 * len(mine)]

    def body(*refs):
        pieces = refs[: ends[0]], refs[ends[0] : ends[1]], refs[ends[1] : ends[2]]
        enc_kernel(feat_size, width, *pieces, refs[ends[2] : ends[2] + 3], *refs[ends[2] + 3 :])

    return pl.pallas_call(
        body,
        in_specs=[VMEM] * ends[2],
        out_specs=[HBM] * 3,
        out_shape=[
            jax.ShapeDtypeStruct((depth, feats), jnp.bfloat16),
            jax.ShapeDtypeStruct((1, feats), jnp.float32),
            jax.ShapeDtypeStruct((tokens, feats), jnp.bfloat16),
        ],
        scratch_shapes=[
            pltpu.VMEM((depth, tokens), jnp.bfloat16),
            pltpu.VMEM((depth, feats), jnp.bfloat16),
            pltpu.VMEM((1, feats), jnp.float32),
            pltpu.VMEM((tokens, feats), jnp.bfloat16),
            pltpu.SemaphoreType.DMA((1 + len(mine) + feats // width,)),
        ],
        compiler_params=pltpu.CompilerParams(vmem_limit_bytes=LIMIT),
        cost_estimate=cost(tokens, depth, feats, 2 * depth * feats),
    )(*blocks, *mine, *others)


def after(x, *others):
    return lax.optimization_barrier((x, *others))[0] if others else x


def rounded(x):
    return lax.reduce_precision(x, 8, 7)


def local(feat_size, layer_size, width_size, residuals, cotangent, enc_weight, enc_bias, dec_weight, active):
    layers = dec_weight.shape[1]
    source = lax.axis_index("layer")
    role = lax.axis_index("width") % 2
    res, cot = residuals[0], cotangent[0]
    own, depth = res.shape
    feats = enc_weight.shape[2]
    gate = active[0]
    tokens = gate.shape[0]
    weight = jnp.swapaxes(dec_weight[0], 1, 2)

    def neighbour(x):
        return swap(x, "width", width_size, 1)

    def pair_sum(keep, got, *before):
        got = after(got, *before)
        total = rounded(keep + got.astype(jnp.float32))
        return total, total.astype(jnp.bfloat16)

    def across(total, stage):
        bit, parts = 2, []
        while bit < width_size:
            if parts:
                total = rounded(total + parts.pop().astype(jnp.float32))
                stage = total.astype(jnp.bfloat16)
            parts.append(swap(stage, "width", width_size, bit))
            bit *= 2
        return total, parts

    def whole_sum(total, parts, *before):
        for part in parts:
            total = total + after(part, *before).astype(jnp.float32)
        return total

    if feat_size == 2:
        place = lax.axis_index("feat")
        sent = lax.optimization_barrier(jnp.concatenate([res, cot], axis=0))
        halves = [enc_part(in_hbm(res), enc_weight[0])]
        other = after(swap(sent, "feat", 2, 1), halves[0][1])
        blocks = [res, other[:own]]
        starts = [place * own, (1 - place) * own]
        grads = jnp.concatenate([sent[own:], other[own:]], axis=0)
    else:
        place, halves = 0, []
        blocks = [lax.all_gather(res, "feat", axis=0, tiled=True)]
        starts = [0]
        grads = lax.all_gather(cot, "feat", axis=0, tiled=True)
    held, order = [grads], [0]
    bit = layer_size // 2
    while bit:
        got = swap(jnp.stack(held), "layer", layer_size, bit)
        held = held + [got[i] for i in range(len(held))]
        order = order + [o ^ bit for o in order]
        bit //= 2
    grads = [held[order.index(j)] for j in range(layer_size)]

    for rows in blocks[len(halves) :]:
        halves.append(enc_part(rows, enc_weight[0]))
    got = [neighbour(send) for _, send in halves]
    act_sums = []
    for (keep, _), other in zip(halves, got):
        act_sums.append(across(*pair_sum(keep, other, *[total for total, _ in act_sums[-1:]])))

    def activation(i, *before):
        kept = halves[i][0].shape[0]
        mask = lax.dynamic_slice_in_dim(gate, starts[i] + role * kept, kept, 0).astype(jnp.float32)
        return ((whole_sum(*act_sums[i], *before) + enc_bias) * mask).astype(jnp.bfloat16)

    count = feats // 2
    half = tokens // 2

    def feature(i, *before):
        mask = lax.dynamic_slice(gate, (role * half, i * count), (half, count)).astype(jnp.float32)
        return (whole_sum(*feat_sums[i], *before) * mask).astype(jnp.bfloat16)

    keep, send = feat_part(feat_size, grads, weight, 0, count, [act_sums[-1][0]])
    first = keep, neighbour(send)
    acts = [activation(0, send)]
    backs = [neighbour(acts[0])]
    keep, send = feat_part(feat_size, grads, weight, count, count, acts)
    second = keep, neighbour(send)
    feat_sums = [across(*pair_sum(*first, send))]
    for i in range(1, len(blocks)):
        acts.append(activation(i, feat_sums[0][0]))
        backs.append(neighbour(acts[i]))
    feat_sums.append(across(*pair_sum(*second, acts[-1])))

    pieces = [piece for pair in zip(acts, backs) for piece in pair]
    kept, middle = halves[0][0].shape[0], layers // 2
    dec_grad = dec_product(grads, pieces, kept, 0, middle, None, [feat_sums[1][0]])
    feat_grads = [feature(0, dec_grad)]
    feat_backs = [neighbour(feat_grads[0])]
    feat_grads.append(feature(1, feat_grads[0]))
    feat_backs.append(neighbour(feat_grads[1]))
    dec_grad = dec_product(grads, pieces, kept, middle, layers - middle, dec_grad, feat_grads[:1])
    enc_grad, bias_grad, feat_grad = enc_product(
        feat_size, blocks, [jnp.concatenate(feat_grads, axis=1)], [jnp.concatenate(feat_backs, axis=1)]
    )
    return (jnp.swapaxes(dec_grad, 1, 2)[None], enc_grad[None], bias_grad, feat_grad[None])


def solution(mesh):
    in_specs = (
        P("layer", "feat", "width"),
        P("layer", "feat", "width"),
        P("layer", "width", "feat"),
        P("layer", "feat"),
        P("layer", None, "feat", "width"),
        P("layer", None, "feat"),
    )
    out_specs = (
        P("layer", None, "feat", "width"),
        P("layer", "width", "feat"),
        P("layer", "feat"),
        P("layer", None, "feat"),
    )
    sizes = (mesh.shape["feat"], mesh.shape["layer"], mesh.shape["width"])
    return jax.shard_map(
        functools.partial(local, *sizes), mesh=mesh, in_specs=in_specs, out_specs=out_specs, check_vma=False
    )
```

time: 61.3 us -> 57.1 us (0.931)
  Pallas kernels: 28.6 us -> 25.5 us
  starting transfers between devices: 21.3 us -> 19.1 us
  waiting for transfers between devices: 8.77 us -> 10.1 us
    pallas_call x7, Pallas kernels: 28.6 us -> 25.5 us  [the longest x2 8.75 us: feat_part(): pl.pallas_call(functools.partial(feat_part_kernel, feat_size, first, len(...]
    ppermute x15, starting transfers between devices: 21.3 us -> 19.1 us  [swap(): return lax.ppermute(x, axis, [(i, i ^ bit) for i in range(size)])]
    ppermute x15, waiting for transfers between devices: 8.77 us -> 10.1 us  [swap(): return lax.ppermute(x, axis, [(i, i ^ bit) for i in range(size)])]
  transfers between devices with their start and end apart: 15 -> 15, of which waited for: 4 -> 6; matrix products, arithmetic and copies ran while one was open for 1% -> 1% of each run, Pallas kernels for 41% -> 40%
where the time goes in v3:
time: 57.1 us; the launch traced here: 56.9 us
  Pallas kernels  25.5 us (45%)
  starting transfers between devices  19.1 us (33%)
  waiting for transfers between devices  10.1 us (18%)
  other arithmetic  1.35 us (2%)
  between operations  0.82 us (1%)
    ppermute x15, starting transfers between devices, swap(): return lax.ppermute(x, axis, [(i, i ^ bit) for i in range(size)])  19.1 us
    ppermute x15, waiting for transfers between devices, swap(): return lax.ppermute(x, axis, [(i, i ^ bit) for i in range(size)])  10.1 us
    pallas_call x2, Pallas kernels, feat_part(): pl.pallas_call(functools.partial(feat_part_kernel, feat_size, first, len(...  8.75 us
    pallas_call x2, Pallas kernels, dec_product(): pl.pallas_call(body, in_specs=[VMEM] * (layers + len(acts)) + [ANY] * (le...  8.39 us
    pallas_call x2, Pallas kernels, enc_part(): pl.pallas_call(functools.partial(enc_part_kernel, steps), in_specs=[ANY,...  5.64 us
    pallas_call x1, Pallas kernels, enc_product(): pl.pallas_call(body, in_specs=[VMEM] * ends[2], out_specs=[HBM] * 3, out_...  2.76 us
  transfers between devices with their start and end apart: 15, of which 6 were waited for; matrix products, arithmetic and copies ran while one was open for 1% of the time, Pallas kernels for 40%

profile of v3, /device:TPU:0, one launch (start us, length us, event | category | flops | bytes accessed | tf_op | source)
XLA Modules:
  0.0 56.9 jit_solution(6383407892225451309)
XLA Ops:
  0.6 0.0 copy-start.1
  0.6 0.0 copy-start.2
  0.7 0.9 %pad_maximum_fusion.3 = bf16[64,576]{1,0:T(8,128)(2,1)S(1)} fusion(bf16[32,576]{1,0:T(8,128)(2,1)} %bitcast.49, bf16[32,576]{1,0:T(8,128)(2,1)} %bitcast.39), kind=kLoop, calls=%fused_computation.17 | loop fusion | flops 147456 | bytes 147456 | tf_op jit(solution)/shard_map/concatenate | solution.py:314
  1.5 3.0 %collective-permute-start = (bf16[64,576]{1,0:T(8,128)(2,1)S(1)}, bf16[64,576]{1,0:T(8,128)(2,1)S(1)}, u32[]{:S(2)}, u32[]{:S(2)}) collective-permute-start(bf16[64,576]{1,0:T(8,128)(2,1)S(1)} %pad_maximum_fusion.3), channel_id=1, source_target_pairs={{0,4},{4,0},{1,5},{5,1},{2,6},{6,2},{3,7},{7,3},{8,12},{12,8},{9,1... | collective-permute-start | bytes 221192 | tf_op jit(solution)/shard_map/ppermute | solution.py:27
  4.6 2.8 %shard_map.93 = (f32[16,4096]{1,0:T(8,128)S(1)}, bf16[16,4096]{1,0:T(8,128)(2,1)S(1)}) custom-call(bf16[32,576]{1,0:T(8,128)(2,1)} %bitcast.40, bf16[576,4096]{1,0:T(8,128)(2,1)} %bitcast.45), custom_call_target="tpu_custom_call" | custom-call | flops 150994944 | bytes 4718592 | tf_op jit(solution)/shard_map/pallas_call | solution.py:81
  7.4 1.6 %collective-permute-start.3 = (bf16[16,4096]{1,0:T(8,128)(2,1)S(1)}, bf16[16,4096]{1,0:T(8,128)(2,1)S(1)}, u32[]{:S(2)}, u32[]{:S(2)}) collective-permute-start(bf16[16,4096]{1,0:T(8,128)(2,1)S(1)} %get-tuple-element.23), channel_id=1, source_target_pairs={{0,1},{1,0},{2,3},{3,2},{4,5},{5,4},{6,7},{7,6},{8,9},{9,8},{10,11... | collective-permute-start | bytes 393224 | tf_op jit(solution)/shard_map/ppermute | solution.py:27
  9.1 0.0 collective-permute-done
  9.1 1.6 %collective-permute-start.1 = (bf16[1,64,576]{2,1,0:T(8,128)(2,1)S(1)}, bf16[1,64,576]{2,1,0:T(8,128)(2,1)S(1)}, u32[]{:S(2)}, u32[]{:S(2)}) collective-permute-start(bf16[1,64,576]{2,1,0:T(8,128)(2,1)S(1)} %get-tuple-element.54), channel_id=1, source_target_pairs={{0,16},{8,24},{16,0},{24,8},{1,17},{9,25},{17,1},{25,9},{2,18},{10... | collective-permute-start | bytes 221192 | tf_op jit(solution)/shard_map/ppermute | solution.py:27
  10.7 2.8 %shard_map.94 = (f32[16,4096]{1,0:T(8,128)S(1)}, bf16[16,4096]{1,0:T(8,128)(2,1)S(1)}) custom-call(bf16[32,576]{1,0:T(8,128)(2,1)S(1)} %get-tuple-element.52.x_ref.refs_1_, bf16[576,4096]{1,0:T(8,128)(2,1)} %bitcast.46), custom_call_target="tpu_custom_call" | custom-call | flops 150994944 | bytes 4718592 | tf_op jit(solution)/shard_map/pallas_call | solution.py:81
  13.5 0.5 collective-permute-start.5
  14.0 0.0 collective-permute-done.3
  14.0 2.7 %collective-permute-start.4 = (bf16[16,4096]{1,0:T(8,128)(2,1)S(1)}, bf16[16,4096]{1,0:T(8,128)(2,1)S(1)}, u32[]{:S(2)}, u32[]{:S(2)}) collective-permute-start(bf16[16,4096]{1,0:T(8,128)(2,1)S(1)} %get-tuple-element.48), channel_id=1, source_target_pairs={{0,2},{1,3},{2,0},{3,1},{4,6},{5,7},{6,4},{7,5},{8,10},{9,11},{10,... | collective-permute-start | bytes 393224 | tf_op jit(solution)/shard_map/ppermute | solution.py:27
  16.7 0.0 collective-permute-done.1
  16.7 0.1 collective-permute-start.2
  16.8 2.7 %collective-permute-done.5 = bf16[16,4096]{1,0:T(8,128)(2,1)S(1)} collective-permute-done((bf16[16,4096]{1,0:T(8,128)(2,1)S(1)}, bf16[16,4096]{1,0:T(8,128)(2,1)S(1)}, u32[]{:S(2)}, u32[]{:S(2)}) %collective-permute-start.5) | collective-permute-done | bytes 131104 | tf_op jit(solution)/shard_map/ppermute | solution.py:27
  19.5 2.5 %collective-permute-start.7 = (bf16[16,4096]{1,0:T(8,128)(2,1)S(1)}, bf16[16,4096]{1,0:T(8,128)(2,1)S(1)}, u32[]{:S(2)}, u32[]{:S(2)}) collective-permute-start(bf16[16,4096]{1,0:T(8,128)(2,1)S(1)} %get-tuple-element.46), channel_id=1, source_target_pairs={{0,2},{1,3},{2,0},{3,1},{4,6},{5,7},{6,4},{7,5},{8,10},{9,11},{10,... | collective-permute-start | bytes 393224 | tf_op jit(solution)/shard_map/ppermute | solution.py:27
  22.0 0.0 collective-permute-done.2
  22.1 4.4 %shard_map.95 = (f32[32,2048]{1,0:T(8,128)S(1)}, bf16[32,2048]{1,0:T(8,128)(2,1)S(1)}) custom-call(bf16[64,576]{1,0:T(8,128)(2,1)S(1)} %get-tuple-element.55.refs_0_, bf16[64,576]{1,0:T(8,128)(2,1)S(1)} %get-tuple-element.51.refs_1_, bf16[64,576]{1,0:T(8,128)(2,1)S(1)} %bitcast.35, bf16[64,576]{1,0:T(8,128)(2,1)S(1)} %get-tuple-element.50.refs_3_, ...), custom_call_target="tpu_custom_call" | custom-call | flops 603979776 | bytes 9437184 | tf_op jit(solution)/shard_map/pallas_call | solution.py:130
  26.5 0.7 %collective-permute-start.8 = (bf16[32,2048]{1,0:T(8,128)(2,1)S(1)}, bf16[32,2048]{1,0:T(8,128)(2,1)S(1)}, u32[]{:S(2)}, u32[]{:S(2)}) collective-permute-start(bf16[32,2048]{1,0:T(8,128)(2,1)S(1)} %get-tuple-element.29), channel_id=1, source_target_pairs={{0,1},{1,0},{2,3},{3,2},{4,5},{5,4},{6,7},{7,6},{8,9},{9,8},{10,11... | collective-permute-start | bytes 393224 | tf_op jit(solution)/shard_map/ppermute | solution.py:27
  27.2 0.0 collective-permute-done.4
  27.2 0.0 copy-done.1
  27.2 0.0 copy-done.2
  27.2 0.1 fusion.3.refs_5_.refs_4_
  27.3 1.4 %collective-permute-start.6 = (bf16[16,4096]{1,0:T(8,128)(2,1)S(1)}, bf16[16,4096]{1,0:T(8,128)(2,1)S(1)}, u32[]{:S(2)}, u32[]{:S(2)}) collective-permute-start(bf16[16,4096]{1,0:T(8,128)(2,1)S(1)} %fusion.3.refs_5_.refs_4_), channel_id=1, source_target_pairs={{0,1},{1,0},{2,3},{3,2},{4,5},{5,4},{6,7},{7,6},{8,9},{9,8},{10,11... | collective-permute-start | bytes 393224 | tf_op jit(solution)/shard_map/ppermute | solution.py:27
  28.7 4.4 %shard_map.96 = (f32[32,2048]{1,0:T(8,128)S(1)}, bf16[32,2048]{1,0:T(8,128)(2,1)S(1)}) custom-call(bf16[64,576]{1,0:T(8,128)(2,1)S(1)} %get-tuple-element.55.refs_0_, bf16[64,576]{1,0:T(8,128)(2,1)S(1)} %get-tuple-element.51.refs_1_, bf16[64,576]{1,0:T(8,128)(2,1)S(1)} %bitcast.36, bf16[64,576]{1,0:T(8,128)(2,1)S(1)} %get-tuple-element.50.refs_3_, ...), custom_call_target="tpu_custom_call" | custom-call | flops 603979776 | bytes 9437184 | tf_op jit(solution)/shard_map/pallas_call | solution.py:130
  33.1 0.7 %collective-permute-start.10 = (bf16[32,2048]{1,0:T(8,128)(2,1)S(1)}, bf16[32,2048]{1,0:T(8,128)(2,1)S(1)}, u32[]{:S(2)}, u32[]{:S(2)}) collective-permute-start(bf16[32,2048]{1,0:T(8,128)(2,1)S(1)} %get-tuple-element.32), channel_id=1, source_target_pairs={{0,1},{1,0},{2,3},{3,2},{4,5},{5,4},{6,7},{7,6},{8,9},{9,8},{10,11... | collective-permute-start | bytes 393224 | tf_op jit(solution)/shard_map/ppermute | solution.py:27
  33.8 0.0 collective-permute-done.8
  33.8 0.0 collective-permute-done.7
  33.9 0.1 fusion.2.refs_6_
  33.9 1.4 %collective-permute-start.9 = (bf16[16,4096]{1,0:T(8,128)(2,1)S(1)}, bf16[16,4096]{1,0:T(8,128)(2,1)S(1)}, u32[]{:S(2)}, u32[]{:S(2)}) collective-permute-start(bf16[16,4096]{1,0:T(8,128)(2,1)S(1)} %fusion.2.refs_6_), channel_id=1, source_target_pairs={{0,1},{1,0},{2,3},{3,2},{4,5},{5,4},{6,7},{7,6},{8,9},{9,8},{10,11... | collective-permute-start | bytes 393224 | tf_op jit(solution)/shard_map/ppermute | solution.py:27
  35.4 1.5 %collective-permute-start.11 = (bf16[32,2048]{1,0:T(8,128)(2,1)S(1)}, bf16[32,2048]{1,0:T(8,128)(2,1)S(1)}, u32[]{:S(2)}, u32[]{:S(2)}) collective-permute-start(bf16[32,2048]{1,0:T(8,128)(2,1)S(1)} %get-tuple-element.44), channel_id=1, source_target_pairs={{0,2},{1,3},{2,0},{3,1},{4,6},{5,7},{6,4},{7,5},{8,10},{9,11},{10,... | collective-permute-start | bytes 393224 | tf_op jit(solution)/shard_map/ppermute | solution.py:27
  36.8 2.8 %collective-permute-done.10 = bf16[32,2048]{1,0:T(8,128)(2,1)S(1)} collective-permute-done((bf16[32,2048]{1,0:T(8,128)(2,1)S(1)}, bf16[32,2048]{1,0:T(8,128)(2,1)S(1)}, u32[]{:S(2)}, u32[]{:S(2)}) %collective-permute-start.10) | collective-permute-done | bytes 131104 | tf_op jit(solution)/shard_map/ppermute | solution.py:27
  39.7 0.1 collective-permute-start.12
  39.8 0.0 collective-permute-done.6.refs_5_
  39.8 2.0 %collective-permute-done.9.refs_7_ = bf16[16,4096]{1,0:T(8,128)(2,1)S(1)} collective-permute-done((bf16[16,4096]{1,0:T(8,128)(2,1)S(1)}, bf16[16,4096]{1,0:T(8,128)(2,1)S(1)}, u32[]{:S(2)}, u32[]{:S(2)}) %collective-permute-start.9) | collective-permute-done | bytes 131104 | tf_op jit(solution)/shard_map/ppermute | solution.py:27
  41.8 4.2 %shard_map.97.refs_8_ = bf16[4,576,4096]{2,1,0:T(8,128)(2,1)} custom-call(bf16[64,576]{1,0:T(8,128)(2,1)S(1)} %get-tuple-element.55.refs_0_, bf16[64,576]{1,0:T(8,128)(2,1)S(1)} %get-tuple-element.51.refs_1_, bf16[64,576]{1,0:T(8,128)(2,1)S(1)} %bitcast.37, bf16[64,576]{1,0:T(8,128)(2,1)S(1)} %get-tuple-element.50.refs_3_, ...), custom_call_target="tpu_custom_call" | custom-call | flops 603979776 | bytes 9437184 | tf_op jit(solution)/shard_map/pallas_call | solution.py:191
  46.0 0.6 %collective-permute-done.11 = bf16[32,2048]{1,0:T(8,128)(2,1)S(1)} collective-permute-done((bf16[32,2048]{1,0:T(8,128)(2,1)S(1)}, bf16[32,2048]{1,0:T(8,128)(2,1)S(1)}, u32[]{:S(2)}, u32[]{:S(2)}) %collective-permute-start.11) | collective-permute-done | bytes 131104 | tf_op jit(solution)/shard_map/ppermute | solution.py:27
  46.6 0.8 %collective-permute-start.13 = (bf16[32,2048]{1,0:T(8,128)(2,1)S(1)}, bf16[32,2048]{1,0:T(8,128)(2,1)S(1)}, u32[]{:S(2)}, u32[]{:S(2)}) collective-permute-start(bf16[32,2048]{1,0:T(8,128)(2,1)S(1)} %fusion.1.refs_9_), channel_id=1, source_target_pairs={{0,1},{1,0},{2,3},{3,2},{4,5},{5,4},{6,7},{7,6},{8,9},{9,8},{10,11... | collective-permute-start | bytes 393224 | tf_op jit(solution)/shard_map/ppermute | solution.py:27
  47.5 0.9 %collective-permute-done.12 = bf16[32,2048]{1,0:T(8,128)(2,1)S(1)} collective-permute-done((bf16[32,2048]{1,0:T(8,128)(2,1)S(1)}, bf16[32,2048]{1,0:T(8,128)(2,1)S(1)}, u32[]{:S(2)}, u32[]{:S(2)}) %collective-permute-start.12) | collective-permute-done | bytes 131104 | tf_op jit(solution)/shard_map/ppermute | solution.py:27
  48.4 0.4 collective-permute-start.14
  48.9 0.0 copy-start
  48.9 4.2 %shard_map.98 = bf16[4,576,4096]{2,1,0:T(8,128)(2,1)} custom-call(bf16[64,576]{1,0:T(8,128)(2,1)S(1)} %get-tuple-element.55.refs_0_, bf16[64,576]{1,0:T(8,128)(2,1)S(1)} %get-tuple-element.51.refs_1_, bf16[64,576]{1,0:T(8,128)(2,1)S(1)} %bitcast.38, bf16[64,576]{1,0:T(8,128)(2,1)S(1)} %get-tuple-element.50.refs_3_, ...), custom_call_target="tpu_custom_call", output_to_operand_aliasing={{}: (8, {})} | custom-call | flops 603979776 | bytes 9437184 | tf_op jit(solution)/shard_map/pallas_call | solution.py:191
  53.1 1.1 %collective-permute-done.14 = bf16[32,2048]{1,0:T(8,128)(2,1)S(1)} collective-permute-done((bf16[32,2048]{1,0:T(8,128)(2,1)S(1)}, bf16[32,2048]{1,0:T(8,128)(2,1)S(1)}, u32[]{:S(2)}, u32[]{:S(2)}) %collective-permute-start.14) | collective-permute-done | bytes 131104 | tf_op jit(solution)/shard_map/ppermute | solution.py:27
  54.1 0.0 collective-permute-done.13
  54.2 0.0 copy-done
  54.2 2.8 %shard_map.99 = (bf16[576,4096]{1,0:T(8,128)(2,1)}, f32[1,4096]{1,0:T(1,128)}, bf16[64,4096]{1,0:T(8,128)(2,1)}) custom-call(bf16[32,576]{1,0:T(8,128)(2,1)S(1)} %bitcast.41, bf16[32,576]{1,0:T(8,128)(2,1)S(1)} %get-tuple-element.52.x_ref.refs_1_, bf16[32,4096]{1,0:T(8,128)(2,1)S(1)} %pad_maximum_fusion.refs_2_, bf16[32,4096]{1,0:T(8,128)(2,1)S(1)} %pad_maximum_fusion.1.refs_3_), custom_call_target="tpu_custom_call" | custom-call | flops 301989888 | bytes 4718592 | tf_op jit(solution)/shard_map/pallas_call | solution.py:249
  (13 shorter events, 0.3 us)
Async XLA Ops:
  0.6 26.6 %copy-start.1 = (s32[1,64,4096]{2,1,0:T(8,128)S(1)}, s32[1,64,4096]{2,1,0:T(8,128)}, u32[]{:S(2)}) copy-start(s32[1,64,4096]{2,1,0:T(8,128)} %param.11) | copy-start | bytes 3145732
  0.6 26.5 %copy-start.2 = (f32[1,4096]{1,0:T(1,128)S(1)}, f32[1,4096]{1,0:T(1,128)}, u32[]{:S(2)}) copy-start(f32[1,4096]{1,0:T(1,128)} %param.9) | copy-start | bytes 49156
  1.5 7.5 %collective-permute-start = (bf16[64,576]{1,0:T(8,128)(2,1)S(1)}, bf16[64,576]{1,0:T(8,128)(2,1)S(1)}, u32[]{:S(2)}, u32[]{:S(2)}) collective-permute-start(bf16[64,576]{1,0:T(8,128)(2,1)S(1)} %pad_maximum_fusion.3), channel_id=1, source_target_pairs={{0,4},{4,0},{1,5},{5,1},{2,6},{6,2},{3,7},{7,3},{8,12},{12,8},{9,1... | collective-permute-start | bytes 221192 | tf_op jit(solution)/shard_map/ppermute | solution.py:27
  7.4 6.6 %collective-permute-start.3 = (bf16[16,4096]{1,0:T(8,128)(2,1)S(1)}, bf16[16,4096]{1,0:T(8,128)(2,1)S(1)}, u32[]{:S(2)}, u32[]{:S(2)}) collective-permute-start(bf16[16,4096]{1,0:T(8,128)(2,1)S(1)} %get-tuple-element.23), channel_id=1, source_target_pairs={{0,1},{1,0},{2,3},{3,2},{4,5},{5,4},{6,7},{7,6},{8,9},{9,8},{10,11... | collective-permute-start | bytes 393224 | tf_op jit(solution)/shard_map/ppermute | solution.py:27
  9.1 7.6 %collective-permute-start.1 = (bf16[1,64,576]{2,1,0:T(8,128)(2,1)S(1)}, bf16[1,64,576]{2,1,0:T(8,128)(2,1)S(1)}, u32[]{:S(2)}, u32[]{:S(2)}) collective-permute-start(bf16[1,64,576]{2,1,0:T(8,128)(2,1)S(1)} %get-tuple-element.54), channel_id=1, source_target_pairs={{0,16},{8,24},{16,0},{24,8},{1,17},{9,25},{17,1},{25,9},{2,18},{10... | collective-permute-start | bytes 221192 | tf_op jit(solution)/shard_map/ppermute | solution.py:27
  13.5 6.0 %collective-permute-start.5 = (bf16[16,4096]{1,0:T(8,128)(2,1)S(1)}, bf16[16,4096]{1,0:T(8,128)(2,1)S(1)}, u32[]{:S(2)}, u32[]{:S(2)}) collective-permute-start(bf16[16,4096]{1,0:T(8,128)(2,1)S(1)} %get-tuple-element.27), channel_id=1, source_target_pairs={{0,1},{1,0},{2,3},{3,2},{4,5},{5,4},{6,7},{7,6},{8,9},{9,8},{10,11... | collective-permute-start | bytes 393224 | tf_op jit(solution)/shard_map/ppermute | solution.py:27
  14.0 13.1 %collective-permute-start.4 = (bf16[16,4096]{1,0:T(8,128)(2,1)S(1)}, bf16[16,4096]{1,0:T(8,128)(2,1)S(1)}, u32[]{:S(2)}, u32[]{:S(2)}) collective-permute-start(bf16[16,4096]{1,0:T(8,128)(2,1)S(1)} %get-tuple-element.48), channel_id=1, source_target_pairs={{0,2},{1,3},{2,0},{3,1},{4,6},{5,7},{6,4},{7,5},{8,10},{9,11},{10,... | collective-permute-start | bytes 393224 | tf_op jit(solution)/shard_map/ppermute | solution.py:27
  16.7 5.3 %collective-permute-start.2 = (bf16[2,64,576]{2,1,0:T(8,128)(2,1)S(1)}, bf16[2,64,576]{2,1,0:T(8,128)(2,1)S(1)}, u32[]{:S(2)}, u32[]{:S(2)}) collective-permute-start(bf16[2,64,576]{2,1,0:T(8,128)(2,1)S(1)} %pad_maximum_fusion.2), channel_id=1, source_target_pairs={{0,8},{8,0},{16,24},{24,16},{1,9},{9,1},{17,25},{25,17},{2,10},{10... | collective-permute-start | bytes 442376 | tf_op jit(solution)/shard_map/ppermute | solution.py:27
  19.5 14.3 %collective-permute-start.7 = (bf16[16,4096]{1,0:T(8,128)(2,1)S(1)}, bf16[16,4096]{1,0:T(8,128)(2,1)S(1)}, u32[]{:S(2)}, u32[]{:S(2)}) collective-permute-start(bf16[16,4096]{1,0:T(8,128)(2,1)S(1)} %get-tuple-element.46), channel_id=1, source_target_pairs={{0,2},{1,3},{2,0},{3,1},{4,6},{5,7},{6,4},{7,5},{8,10},{9,11},{10,... | collective-permute-start | bytes 393224 | tf_op jit(solution)/shard_map/ppermute | solution.py:27
  26.5 7.3 %collective-permute-start.8 = (bf16[32,2048]{1,0:T(8,128)(2,1)S(1)}, bf16[32,2048]{1,0:T(8,128)(2,1)S(1)}, u32[]{:S(2)}, u32[]{:S(2)}) collective-permute-start(bf16[32,2048]{1,0:T(8,128)(2,1)S(1)} %get-tuple-element.29), channel_id=1, source_target_pairs={{0,1},{1,0},{2,3},{3,2},{4,5},{5,4},{6,7},{7,6},{8,9},{9,8},{10,11... | collective-permute-start | bytes 393224 | tf_op jit(solution)/shard_map/ppermute | solution.py:27
  27.3 12.5 %collective-permute-start.6 = (bf16[16,4096]{1,0:T(8,128)(2,1)S(1)}, bf16[16,4096]{1,0:T(8,128)(2,1)S(1)}, u32[]{:S(2)}, u32[]{:S(2)}) collective-permute-start(bf16[16,4096]{1,0:T(8,128)(2,1)S(1)} %fusion.3.refs_5_.refs_4_), channel_id=1, source_target_pairs={{0,1},{1,0},{2,3},{3,2},{4,5},{5,4},{6,7},{7,6},{8,9},{9,8},{10,11... | collective-permute-start | bytes 393224 | tf_op jit(solution)/shard_map/ppermute | solution.py:27
  33.1 6.6 %collective-permute-start.10 = (bf16[32,2048]{1,0:T(8,128)(2,1)S(1)}, bf16[32,2048]{1,0:T(8,128)(2,1)S(1)}, u32[]{:S(2)}, u32[]{:S(2)}) collective-permute-start(bf16[32,2048]{1,0:T(8,128)(2,1)S(1)} %get-tuple-element.32), channel_id=1, source_target_pairs={{0,1},{1,0},{2,3},{3,2},{4,5},{5,4},{6,7},{7,6},{8,9},{9,8},{10,11... | collective-permute-start | bytes 393224 | tf_op jit(solution)/shard_map/ppermute | solution.py:27
  33.9 7.9 %collective-permute-start.9 = (bf16[16,4096]{1,0:T(8,128)(2,1)S(1)}, bf16[16,4096]{1,0:T(8,128)(2,1)S(1)}, u32[]{:S(2)}, u32[]{:S(2)}) collective-permute-start(bf16[16,4096]{1,0:T(8,128)(2,1)S(1)} %fusion.2.refs_6_), channel_id=1, source_target_pairs={{0,1},{1,0},{2,3},{3,2},{4,5},{5,4},{6,7},{7,6},{8,9},{9,8},{10,11... | collective-permute-start | bytes 393224 | tf_op jit(solution)/shard_map/ppermute | solution.py:27
  35.4 11.2 %collective-permute-start.11 = (bf16[32,2048]{1,0:T(8,128)(2,1)S(1)}, bf16[32,2048]{1,0:T(8,128)(2,1)S(1)}, u32[]{:S(2)}, u32[]{:S(2)}) collective-permute-start(bf16[32,2048]{1,0:T(8,128)(2,1)S(1)} %get-tuple-element.44), channel_id=1, source_target_pairs={{0,2},{1,3},{2,0},{3,1},{4,6},{5,7},{6,4},{7,5},{8,10},{9,11},{10,... | collective-permute-start | bytes 393224 | tf_op jit(solution)/shard_map/ppermute | solution.py:27
  39.7 8.7 %collective-permute-start.12 = (bf16[32,2048]{1,0:T(8,128)(2,1)S(1)}, bf16[32,2048]{1,0:T(8,128)(2,1)S(1)}, u32[]{:S(2)}, u32[]{:S(2)}) collective-permute-start(bf16[32,2048]{1,0:T(8,128)(2,1)S(1)} %get-tuple-element.42), channel_id=1, source_target_pairs={{0,2},{1,3},{2,0},{3,1},{4,6},{5,7},{6,4},{7,5},{8,10},{9,11},{10,... | collective-permute-start | bytes 393224 | tf_op jit(solution)/shard_map/ppermute | solution.py:27
  46.6 7.5 %collective-permute-start.13 = (bf16[32,2048]{1,0:T(8,128)(2,1)S(1)}, bf16[32,2048]{1,0:T(8,128)(2,1)S(1)}, u32[]{:S(2)}, u32[]{:S(2)}) collective-permute-start(bf16[32,2048]{1,0:T(8,128)(2,1)S(1)} %fusion.1.refs_9_), channel_id=1, source_target_pairs={{0,1},{1,0},{2,3},{3,2},{4,5},{5,4},{6,7},{7,6},{8,9},{9,8},{10,11... | collective-permute-start | bytes 393224 | tf_op jit(solution)/shard_map/ppermute | solution.py:27
  48.4 5.8 %collective-permute-start.14 = (bf16[32,2048]{1,0:T(8,128)(2,1)S(1)}, bf16[32,2048]{1,0:T(8,128)(2,1)S(1)}, u32[]{:S(2)}, u32[]{:S(2)}) collective-permute-start(bf16[32,2048]{1,0:T(8,128)(2,1)S(1)} %fusion), channel_id=1, source_target_pairs={{0,1},{1,0},{2,3},{3,2},{4,5},{5,4},{6,7},{7,6},{8,9},{9,8},{10,11... | collective-permute-start | bytes 393224 | tf_op jit(solution)/shard_map/ppermute | solution.py:27
  48.9 5.3 %copy-start = (bf16[1,32,576]{2,1,0:T(8,128)(2,1)S(1)}, bf16[1,32,576]{2,1,0:T(8,128)(2,1)}, u32[]{:S(2)}) copy-start(bf16[1,32,576]{2,1,0:T(8,128)(2,1)} %param.6) | copy-start | bytes 110596

commit v4 on v3

--- a/solution.py
+++ b/solution.py
@@ -13,6 +13,7 @@
 HBM = pl.BlockSpec(memory_space=pltpu.HBM)
 LIMIT = 16 * MIB
 DEC_LIMIT = 24 * MIB
+SPLIT = 2
 
 
 def tile(extent, most):
@@ -45,8 +46,9 @@
     return jnp.concatenate([jnp.where(low, first, second), jnp.where(low, second, first)], axis=0)
 
 
-def enc_part_kernel(steps, x_ref, w_hbm, *refs):
-    keep_ref, send_ref, w_ref, x_buf, acc, x_sem, sems = refs[-7:]
+def enc_part_kernel(steps, carried, x_ref, w_hbm, *refs):
+    w_ref, x_buf, acc, x_sem, sems = refs[-5:]
+    keep_ref, send_ref = refs[carried : carried + 2]
     half = keep_ref.shape[0]
     rows = w_ref.shape[0] // steps
 
@@ -56,6 +58,9 @@
 
     x_copy = pltpu.make_async_copy(x_ref, x_buf, x_sem)
     x_copy.start()
+    if carried:
+        carry = pltpu.make_async_copy(refs[0], refs[3], sems.at[steps])
+        carry.start()
     for i in range(steps):
         get(i).start()
     x_copy.wait()
@@ -71,57 +76,68 @@
         else:
             keep_ref[...] = out[:half]
             send_ref[...] = out[half:].astype(send_ref.dtype)
-
-
-def enc_part(x, weight, after=()):
+    if carried:
+        carry.wait()
+
+
+def enc_part(x, weight, carried=()):
     rows, depth = x.shape
     feats = weight.shape[1]
     half = rows // 2
     steps = next(n for n in (3, 2, 1) if depth % (16 * n) == 0)
     return pl.pallas_call(
-        functools.partial(enc_part_kernel, steps),
-        in_specs=[ANY, HBM] + [ANY] * len(after),
-        out_specs=[VMEM, VMEM],
+        functools.partial(enc_part_kernel, steps, len(carried)),
+        in_specs=[ANY, HBM] + [HBM] * len(carried),
+        out_specs=[VMEM] * (2 + len(carried)),
         out_shape=[
             jax.ShapeDtypeStruct((half, feats), jnp.float32),
             jax.ShapeDtypeStruct((half, feats), jnp.bfloat16),
-        ],
+        ]
+        + [jax.ShapeDtypeStruct(y.shape, y.dtype) for y in carried],
         scratch_shapes=[
             pltpu.VMEM((depth, feats), jnp.bfloat16),
             pltpu.VMEM((rows, depth), jnp.bfloat16),
             pltpu.VMEM((rows, feats), jnp.float32),
             pltpu.SemaphoreType.DMA,
-            pltpu.SemaphoreType.DMA((steps,)),
+            pltpu.SemaphoreType.DMA((steps + 1,)),
         ],
         compiler_params=pltpu.CompilerParams(vmem_limit_bytes=LIMIT),
         cost_estimate=cost(rows, depth, feats, 2 * depth * feats),
-    )(x, in_hbm(weight), *after)
+    )(x, in_hbm(weight), *[in_hbm(y) for y in carried])
 
 
 def feat_part_kernel(feat_size, first, pieces, *refs):
     piece_refs, w_hbm = refs[:pieces], refs[pieces]
     keep_ref, send_ref, w_buf, acc, sems = refs[-5:]
     half, count = keep_ref.shape
+    width = count // sems.shape[1]
     source, low, _ = place_of(feat_size)
 
-    def get(k):
-        return pltpu.make_async_copy(w_hbm.at[source ^ k, :, pl.ds(first, count)], w_buf.at[k], sems.at[k])
+    def get(k, j):
+        return pltpu.make_async_copy(
+            w_hbm.at[source ^ k, :, pl.ds(first + j * width, width)],
+            w_buf.at[k, :, pl.ds(j * width, width)],
+            sems.at[k, j],
+        )
 
     for k in range(pieces):
-        get(k).start()
+        for j in range(sems.shape[1]):
+            get(k, j).start()
     for k in range(pieces):
         rows = piece_refs[k][...]
         rows = jnp.where((source ^ k) >= source, rows, jnp.zeros_like(rows))
         rows = ordered(low == 0, rows[:half], rows[half:])
-        get(k).wait()
-        out = jnp.dot(rows, w_buf[k], preferred_element_type=jnp.float32)
-        if k:
-            out += acc[...]
-        if k < pieces - 1:
-            acc[...] = out
-        else:
-            keep_ref[...] = out[:half]
-            send_ref[...] = out[half:].astype(send_ref.dtype)
+        for j in range(sems.shape[1]):
+            columns = slice(j * width, (j + 1) * width)
+            get(k, j).wait()
+            out = jnp.dot(rows, w_buf[k, :, columns], preferred_element_type=jnp.float32)
+            if k:
+                out += acc[:, columns]
+            if k < pieces - 1:
+                acc[:, columns] = out
+            else:
+                keep_ref[:, columns] = out[:half]
+                send_ref[:, columns] = out[half:].astype(send_ref.dtype)
 
 
 def feat_part(feat_size, grads, weight, first, count, after=()):
@@ -138,7 +154,7 @@
         scratch_shapes=[
             pltpu.VMEM((len(grads), depth, count), jnp.bfloat16),
             pltpu.VMEM((tokens, count), jnp.float32),
-            pltpu.SemaphoreType.DMA((len(grads),)),
+            pltpu.SemaphoreType.DMA((len(grads), SPLIT if count % (128 * SPLIT) == 0 else 1)),
         ],
         compiler_params=pltpu.CompilerParams(vmem_limit_bytes=LIMIT),
         cost_estimate=cost(tokens, len(grads) * depth, count, 2 * len(grads) * depth * count),
@@ -148,14 +164,16 @@
 def dec_kernel(first_block, blocks, width, kept, grad_refs, act_refs, out_hbm, act_buf, out_buf, sems):
     source, _, role = place_of(0)
     first = role == 0
-    start = 0
-    for mine_ref, other_ref in zip(act_refs[::2], act_refs[1::2]):
-        for row in range(0, mine_ref.shape[0], kept):
-            mine, other = mine_ref[row : row + kept], other_ref[row : row + kept]
-            act_buf[start : start + kept] = jnp.where(first, mine, other)
-            act_buf[start + kept : start + 2 * kept] = jnp.where(first, other, mine)
-            start += 2 * kept
     steps = act_buf.shape[1] // width
+
+    def gather(columns):
+        start = 0
+        for mine_ref, other_ref in zip(act_refs[::2], act_refs[1::2]):
+            for row in range(0, mine_ref.shape[0], kept):
+                mine, other = mine_ref[row : row + kept, columns], other_ref[row : row + kept, columns]
+                act_buf[start : start + kept, columns] = jnp.where(first, mine, other)
+                act_buf[start + kept : start + 2 * kept, columns] = jnp.where(first, other, mine)
+                start += 2 * kept
 
     def put(b, j):
         columns = pl.ds(j * width, width)
@@ -168,6 +186,8 @@
         grad = jnp.where((source ^ (first_block + b)) >= source, grad, jnp.zeros_like(grad)).T
         for j in range(steps):
             columns = slice(j * width, (j + 1) * width)
+            if b == 0:
+                gather(columns)
             out = jnp.dot(grad, act_buf[:, columns], preferred_element_type=jnp.float32)
             out_buf[b, :, columns] = out.astype(out_buf.dtype)
             put(b, j).start()
@@ -311,32 +331,33 @@
 
     if feat_size == 2:
         place = lax.axis_index("feat")
-        sent = lax.optimization_barrier(jnp.concatenate([res, cot], axis=0))
-        halves = [enc_part(in_hbm(res), enc_weight[0])]
-        other = after(swap(sent, "feat", 2, 1), halves[0][1])
-        blocks = [res, other[:own]]
+        *first_half, cot = enc_part(in_hbm(res), enc_weight[0], [cot])
+        halves = [first_half]
+        other = after(swap(residuals, "feat", 2, 1), halves[0][1])[0]
+        blocks = [res, other]
         starts = [place * own, (1 - place) * own]
-        grads = jnp.concatenate([sent[own:], other[own:]], axis=0)
+        halves.append(enc_part(other, enc_weight[0]))
+        grads = jnp.concatenate([cot, after(swap(cot, "feat", 2, 1), halves[1][1])], axis=0)
     else:
         place, halves = 0, []
         blocks = [lax.all_gather(res, "feat", axis=0, tiled=True)]
         starts = [0]
         grads = lax.all_gather(cot, "feat", axis=0, tiled=True)
+    for rows in blocks[len(halves) :]:
+        halves.append(enc_part(rows, enc_weight[0]))
+    sent_back = [neighbour(send) for _, send in halves]
+    act_sums = []
+    for (keep, _), other in zip(halves, sent_back):
+        act_sums.append(across(*pair_sum(keep, other, *[total for total, _ in act_sums[-1:]])))
+
     held, order = [grads], [0]
     bit = layer_size // 2
     while bit:
-        got = swap(jnp.stack(held), "layer", layer_size, bit)
+        got = after(swap(jnp.stack(held), "layer", layer_size, bit), act_sums[0][0])
         held = held + [got[i] for i in range(len(held))]
         order = order + [o ^ bit for o in order]
         bit //= 2
     grads = [held[order.index(j)] for j in range(layer_size)]
-
-    for rows in blocks[len(halves) :]:
-        halves.append(enc_part(rows, enc_weight[0]))
-    got = [neighbour(send) for _, send in halves]
-    act_sums = []
-    for (keep, _), other in zip(halves, got):
-        act_sums.append(across(*pair_sum(keep, other, *[total for total, _ in act_sums[-1:]])))
 
     def activation(i, *before):
         kept = halves[i][0].shape[0]

time: 57.1 us -> 56 us (0.981)
  starting transfers between devices: 19.1 us -> 20.4 us
  waiting for transfers between devices: 10.1 us -> 8.97 us
  other arithmetic: 1.35 us -> 0.42 us
    ppermute x15 -> x16, starting transfers between devices: 19.1 us -> 20.4 us  [swap(): return lax.ppermute(x, axis, [(i, i ^ bit) for i in range(size)])]
    ppermute x15 -> x16, waiting for transfers between devices: 10.1 us -> 8.97 us  [swap(): return lax.ppermute(x, axis, [(i, i ^ bit) for i in range(size)])]
    concatenate x1 -> x0, other arithmetic: 0.9 us -> none  [local(): sent = lax.optimization_barrier(jnp.concatenate([res, cot], axis=0))]
  transfers between devices with their start and end apart: 15 -> 16, of which waited for: 6 -> 5; matrix products, arithmetic and copies ran while one was open for 1% -> 1% of each run, Pallas kernels for 40% -> 40%
where the time goes in v4:
time: 56 us; the launch traced here: 55.9 us
  Pallas kernels  25.2 us (45%)
  starting transfers between devices  20.4 us (36%)
  waiting for transfers between devices  8.97 us (16%)
  between operations  0.81 us (1%)
    ppermute x16, starting transfers between devices, swap(): return lax.ppermute(x, axis, [(i, i ^ bit) for i in range(size)])  20.4 us
    ppermute x16, waiting for transfers between devices, swap(): return lax.ppermute(x, axis, [(i, i ^ bit) for i in range(size)])  8.97 us
    pallas_call x2, Pallas kernels, dec_product(): pl.pallas_call(body, in_specs=[VMEM] * (layers + len(acts)) + [ANY] * (le...  8.4 us
    pallas_call x2, Pallas kernels, feat_part(): pl.pallas_call(functools.partial(feat_part_kernel, feat_size, first, len(...  8.35 us
    pallas_call x2, Pallas kernels, enc_part(): pl.pallas_call(functools.partial(enc_part_kernel, steps, len(carried)), i...  5.71 us
    pallas_call x1, Pallas kernels, enc_product(): pl.pallas_call(body, in_specs=[VMEM] * ends[2], out_specs=[HBM] * 3, out_...  2.76 us
  transfers between devices with their start and end apart: 16, of which 5 were waited for; matrix products, arithmetic and copies ran while one was open for 1% of the time, Pallas kernels for 40%

profile of v4, /device:TPU:0, one launch (start us, length us, event | category | flops | bytes accessed | tf_op | source)
XLA Modules:
  0.0 55.9 jit_solution(4471968667077981992)
XLA Ops:
  0.6 0.0 copy-start.1
  0.6 0.0 copy-start.2
  0.7 3.0 %collective-permute-start.1 = (bf16[1,32,576]{2,1,0:T(8,128)(2,1)}, bf16[1,32,576]{2,1,0:T(8,128)(2,1)S(1)}, u32[]{:S(2)}, u32[]{:S(2)}) collective-permute-start(bf16[1,32,576]{2,1,0:T(8,128)(2,1)} %param.6), channel_id=1, source_target_pairs={{0,4},{4,0},{1,5},{5,1},{2,6},{6,2},{3,7},{7,3},{8,12},{12,8},{9,1... | collective-permute-start | bytes 110600 | tf_op jit(solution)/shard_map/ppermute | solution.py:28
  3.7 2.9 %shard_map.93 = (f32[16,4096]{1,0:T(8,128)S(1)}, bf16[16,4096]{1,0:T(8,128)(2,1)S(1)}, bf16[32,576]{1,0:T(8,128)(2,1)S(1)}) custom-call(bf16[32,576]{1,0:T(8,128)(2,1)} %bitcast.41, bf16[576,4096]{1,0:T(8,128)(2,1)} %bitcast.48, bf16[32,576]{1,0:T(8,128)(2,1)} %bitcast.52), custom_call_target="tpu_custom_call" | custom-call | flops 150994944 | bytes 4718592 | tf_op jit(solution)/shard_map/pallas_call | solution.py:88
  6.5 0.1 collective-permute-start
  6.7 2.0 %collective-permute-start.3 = (bf16[16,4096]{1,0:T(8,128)(2,1)S(1)}, bf16[16,4096]{1,0:T(8,128)(2,1)S(1)}, u32[]{:S(2)}, u32[]{:S(2)}) collective-permute-start(bf16[16,4096]{1,0:T(8,128)(2,1)S(1)} %get-tuple-element.28), channel_id=1, source_target_pairs={{0,1},{1,0},{2,3},{3,2},{4,5},{5,4},{6,7},{7,6},{8,9},{9,8},{10,11... | collective-permute-start | bytes 393224 | tf_op jit(solution)/shard_map/ppermute | solution.py:28
  8.7 0.0 collective-permute-done.1
  8.7 2.9 %shard_map.94 = (f32[16,4096]{1,0:T(8,128)S(1)}, bf16[16,4096]{1,0:T(8,128)(2,1)S(1)}) custom-call(bf16[32,576]{1,0:T(8,128)(2,1)S(1)} %bitcast.43, bf16[576,4096]{1,0:T(8,128)(2,1)} %bitcast.49), custom_call_target="tpu_custom_call" | custom-call | flops 150994944 | bytes 4718592 | tf_op jit(solution)/shard_map/pallas_call | solution.py:88
  11.6 0.1 collective-permute-start.6
  11.7 0.0 collective-permute-done
  11.7 2.0 %collective-permute-start.2 = (bf16[1,64,576]{2,1,0:T(8,128)(2,1)S(1)}, bf16[1,64,576]{2,1,0:T(8,128)(2,1)S(1)}, u32[]{:S(2)}, u32[]{:S(2)}) collective-permute-start(bf16[1,64,576]{2,1,0:T(8,128)(2,1)S(1)} %bitcast.35), channel_id=1, source_target_pairs={{0,16},{8,24},{16,0},{24,8},{1,17},{9,25},{17,1},{25,9},{2,18},{10... | collective-permute-start | bytes 221192 | tf_op jit(solution)/shard_map/ppermute | solution.py:28
  13.7 0.0 collective-permute-done.3
  13.7 2.7 %collective-permute-start.5 = (bf16[16,4096]{1,0:T(8,128)(2,1)S(1)}, bf16[16,4096]{1,0:T(8,128)(2,1)S(1)}, u32[]{:S(2)}, u32[]{:S(2)}) collective-permute-start(bf16[16,4096]{1,0:T(8,128)(2,1)S(1)} %get-tuple-element.56), channel_id=1, source_target_pairs={{0,2},{1,3},{2,0},{3,1},{4,6},{5,7},{6,4},{7,5},{8,10},{9,11},{10,... | collective-permute-start | bytes 393224 | tf_op jit(solution)/shard_map/ppermute | solution.py:28
  16.3 0.0 collective-permute-done.2
  16.4 0.1 collective-permute-start.4
  16.5 1.5 %collective-permute-done.6 = bf16[16,4096]{1,0:T(8,128)(2,1)S(1)} collective-permute-done((bf16[16,4096]{1,0:T(8,128)(2,1)S(1)}, bf16[16,4096]{1,0:T(8,128)(2,1)S(1)}, u32[]{:S(2)}, u32[]{:S(2)}) %collective-permute-start.6) | collective-permute-done | bytes 131104 | tf_op jit(solution)/shard_map/ppermute | solution.py:28
  18.0 2.2 %collective-permute-start.8 = (bf16[16,4096]{1,0:T(8,128)(2,1)S(1)}, bf16[16,4096]{1,0:T(8,128)(2,1)S(1)}, u32[]{:S(2)}, u32[]{:S(2)}) collective-permute-start(bf16[16,4096]{1,0:T(8,128)(2,1)S(1)} %get-tuple-element.54), channel_id=1, source_target_pairs={{0,2},{1,3},{2,0},{3,1},{4,6},{5,7},{6,4},{7,5},{8,10},{9,11},{10,... | collective-permute-start | bytes 393224 | tf_op jit(solution)/shard_map/ppermute | solution.py:28
  20.2 0.0 collective-permute-done.4
  20.2 4.2 %shard_map.95 = (f32[32,2048]{1,0:T(8,128)S(1)}, bf16[32,2048]{1,0:T(8,128)(2,1)S(1)}) custom-call(bf16[64,576]{1,0:T(8,128)(2,1)S(1)} %constant_dynamic-update-slice_fusion.refs_0_, bf16[64,576]{1,0:T(8,128)(2,1)S(1)} %get-tuple-element.59.refs_1_, bf16[64,576]{1,0:T(8,128)(2,1)S(1)} %bitcast.37, bf16[64,576]{1,0:T(8,128)(2,1)S(1)} %get-tuple-element.58.refs_3_, ...), custom_call_target="tpu_custom_call" | custom-call | flops 603979776 | bytes 9437184 | tf_op jit(solution)/shard_map/pallas_call | solution.py:146
  24.4 0.9 %collective-permute-start.9 = (bf16[32,2048]{1,0:T(8,128)(2,1)S(1)}, bf16[32,2048]{1,0:T(8,128)(2,1)S(1)}, u32[]{:S(2)}, u32[]{:S(2)}) collective-permute-start(bf16[32,2048]{1,0:T(8,128)(2,1)S(1)} %get-tuple-element.37), channel_id=1, source_target_pairs={{0,1},{1,0},{2,3},{3,2},{4,5},{5,4},{6,7},{7,6},{8,9},{9,8},{10,11... | collective-permute-start | bytes 393224 | tf_op jit(solution)/shard_map/ppermute | solution.py:28
  25.3 0.0 collective-permute-done.5
  25.3 0.0 copy-done.1
  25.3 0.0 copy-done.2
  25.3 0.1 fusion.3.refs_5_.refs_4_
  25.4 1.3 %collective-permute-start.7 = (bf16[16,4096]{1,0:T(8,128)(2,1)S(1)}, bf16[16,4096]{1,0:T(8,128)(2,1)S(1)}, u32[]{:S(2)}, u32[]{:S(2)}) collective-permute-start(bf16[16,4096]{1,0:T(8,128)(2,1)S(1)} %fusion.3.refs_5_.refs_4_), channel_id=1, source_target_pairs={{0,1},{1,0},{2,3},{3,2},{4,5},{5,4},{6,7},{7,6},{8,9},{9,8},{10,11... | collective-permute-start | bytes 393224 | tf_op jit(solution)/shard_map/ppermute | solution.py:28
  26.6 4.2 %shard_map.96 = (f32[32,2048]{1,0:T(8,128)S(1)}, bf16[32,2048]{1,0:T(8,128)(2,1)S(1)}) custom-call(bf16[64,576]{1,0:T(8,128)(2,1)S(1)} %constant_dynamic-update-slice_fusion.refs_0_, bf16[64,576]{1,0:T(8,128)(2,1)S(1)} %get-tuple-element.59.refs_1_, bf16[64,576]{1,0:T(8,128)(2,1)S(1)} %bitcast.38, bf16[64,576]{1,0:T(8,128)(2,1)S(1)} %get-tuple-element.58.refs_3_, ...), custom_call_target="tpu_custom_call" | custom-call | flops 603979776 | bytes 9437184 | tf_op jit(solution)/shard_map/pallas_call | solution.py:146
  30.8 0.9 %collective-permute-start.11 = (bf16[32,2048]{1,0:T(8,128)(2,1)S(1)}, bf16[32,2048]{1,0:T(8,128)(2,1)S(1)}, u32[]{:S(2)}, u32[]{:S(2)}) collective-permute-start(bf16[32,2048]{1,0:T(8,128)(2,1)S(1)} %get-tuple-element.40), channel_id=1, source_target_pairs={{0,1},{1,0},{2,3},{3,2},{4,5},{5,4},{6,7},{7,6},{8,9},{9,8},{10,11... | collective-permute-start | bytes 393224 | tf_op jit(solution)/shard_map/ppermute | solution.py:28
  31.7 0.0 collective-permute-done.9
  31.7 0.0 collective-permute-done.8
  31.7 0.1 fusion.2.refs_6_
  31.8 1.3 %collective-permute-start.10 = (bf16[16,4096]{1,0:T(8,128)(2,1)S(1)}, bf16[16,4096]{1,0:T(8,128)(2,1)S(1)}, u32[]{:S(2)}, u32[]{:S(2)}) collective-permute-start(bf16[16,4096]{1,0:T(8,128)(2,1)S(1)} %fusion.2.refs_6_), channel_id=1, source_target_pairs={{0,1},{1,0},{2,3},{3,2},{4,5},{5,4},{6,7},{7,6},{8,9},{9,8},{10,11... | collective-permute-start | bytes 393224 | tf_op jit(solution)/shard_map/ppermute | solution.py:28
  33.1 2.0 %collective-permute-start.12 = (bf16[32,2048]{1,0:T(8,128)(2,1)S(1)}, bf16[32,2048]{1,0:T(8,128)(2,1)S(1)}, u32[]{:S(2)}, u32[]{:S(2)}) collective-permute-start(bf16[32,2048]{1,0:T(8,128)(2,1)S(1)} %get-tuple-element.52), channel_id=1, source_target_pairs={{0,2},{1,3},{2,0},{3,1},{4,6},{5,7},{6,4},{7,5},{8,10},{9,11},{10,... | collective-permute-start | bytes 393224 | tf_op jit(solution)/shard_map/ppermute | solution.py:28
  35.1 4.6 %collective-permute-done.11 = bf16[32,2048]{1,0:T(8,128)(2,1)S(1)} collective-permute-done((bf16[32,2048]{1,0:T(8,128)(2,1)S(1)}, bf16[32,2048]{1,0:T(8,128)(2,1)S(1)}, u32[]{:S(2)}, u32[]{:S(2)}) %collective-permute-start.11) | collective-permute-done | bytes 131104 | tf_op jit(solution)/shard_map/ppermute | solution.py:28
  39.8 0.2 collective-permute-start.13
  39.9 0.0 collective-permute-done.7.refs_5_
  39.9 1.3 %collective-permute-done.10.refs_7_ = bf16[16,4096]{1,0:T(8,128)(2,1)S(1)} collective-permute-done((bf16[16,4096]{1,0:T(8,128)(2,1)S(1)}, bf16[16,4096]{1,0:T(8,128)(2,1)S(1)}, u32[]{:S(2)}, u32[]{:S(2)}) %collective-permute-start.10) | collective-permute-done | bytes 131104 | tf_op jit(solution)/shard_map/ppermute | solution.py:28
  41.2 4.2 %shard_map.97.refs_8_ = bf16[4,576,4096]{2,1,0:T(8,128)(2,1)} custom-call(bf16[64,576]{1,0:T(8,128)(2,1)S(1)} %constant_dynamic-update-slice_fusion.refs_0_, bf16[64,576]{1,0:T(8,128)(2,1)S(1)} %get-tuple-element.59.refs_1_, bf16[64,576]{1,0:T(8,128)(2,1)S(1)} %bitcast.39, bf16[64,576]{1,0:T(8,128)(2,1)S(1)} %get-tuple-element.58.refs_3_, ...), custom_call_target="tpu_custom_call" | custom-call | flops 603979776 | bytes 9437184 | tf_op jit(solution)/shard_map/pallas_call | solution.py:211
  45.4 0.0 collective-permute-done.12
  45.4 1.3 %collective-permute-start.14 = (bf16[32,2048]{1,0:T(8,128)(2,1)S(1)}, bf16[32,2048]{1,0:T(8,128)(2,1)S(1)}, u32[]{:S(2)}, u32[]{:S(2)}) collective-permute-start(bf16[32,2048]{1,0:T(8,128)(2,1)S(1)} %fusion.1.refs_9_), channel_id=1, source_target_pairs={{0,1},{1,0},{2,3},{3,2},{4,5},{5,4},{6,7},{7,6},{8,9},{9,8},{10,11... | collective-permute-start | bytes 393224 | tf_op jit(solution)/shard_map/ppermute | solution.py:28
  46.7 0.4 collective-permute-done.13
  47.2 0.5 collective-permute-start.15
  47.7 0.0 copy-start
  47.7 4.2 %shard_map.98 = bf16[4,576,4096]{2,1,0:T(8,128)(2,1)} custom-call(bf16[64,576]{1,0:T(8,128)(2,1)S(1)} %constant_dynamic-update-slice_fusion.refs_0_, bf16[64,576]{1,0:T(8,128)(2,1)S(1)} %get-tuple-element.59.refs_1_, bf16[64,576]{1,0:T(8,128)(2,1)S(1)} %bitcast.40, bf16[64,576]{1,0:T(8,128)(2,1)S(1)} %get-tuple-element.58.refs_3_, ...), custom_call_target="tpu_custom_call", output_to_operand_aliasing={{}: (8, {})} | custom-call | flops 603979776 | bytes 9437184 | tf_op jit(solution)/shard_map/pallas_call | solution.py:211
  51.9 1.2 %collective-permute-done.15 = bf16[32,2048]{1,0:T(8,128)(2,1)S(1)} collective-permute-done((bf16[32,2048]{1,0:T(8,128)(2,1)S(1)}, bf16[32,2048]{1,0:T(8,128)(2,1)S(1)}, u32[]{:S(2)}, u32[]{:S(2)}) %collective-permute-start.15) | collective-permute-done | bytes 131104 | tf_op jit(solution)/shard_map/ppermute | solution.py:28
  53.1 0.0 collective-permute-done.14
  53.1 0.0 copy-done
  53.1 2.8 %shard_map.99 = (bf16[576,4096]{1,0:T(8,128)(2,1)}, f32[1,4096]{1,0:T(1,128)}, bf16[64,4096]{1,0:T(8,128)(2,1)}) custom-call(bf16[32,576]{1,0:T(8,128)(2,1)S(1)} %bitcast.42, bf16[32,576]{1,0:T(8,128)(2,1)S(1)} %bitcast.44, bf16[32,4096]{1,0:T(8,128)(2,1)S(1)} %pad_maximum_fusion.refs_2_, bf16[32,4096]{1,0:T(8,128)(2,1)S(1)} %pad_maximum_fusion.1.refs_3_), custom_call_target="tpu_custom_call" | custom-call | flops 301989888 | bytes 4718592 | tf_op jit(solution)/shard_map/pallas_call | solution.py:269
  (12 shorter events, 0.3 us)
Async XLA Ops:
  0.6 24.6 %copy-start.1 = (s32[1,64,4096]{2,1,0:T(8,128)S(1)}, s32[1,64,4096]{2,1,0:T(8,128)}, u32[]{:S(2)}) copy-start(s32[1,64,4096]{2,1,0:T(8,128)} %param.11) | copy-start | bytes 3145732
  0.6 24.6 %copy-start.2 = (f32[1,4096]{1,0:T(1,128)S(1)}, f32[1,4096]{1,0:T(1,128)}, u32[]{:S(2)}) copy-start(f32[1,4096]{1,0:T(1,128)} %param.9) | copy-start | bytes 49156
  0.7 8.1 %collective-permute-start.1 = (bf16[1,32,576]{2,1,0:T(8,128)(2,1)}, bf16[1,32,576]{2,1,0:T(8,128)(2,1)S(1)}, u32[]{:S(2)}, u32[]{:S(2)}) collective-permute-start(bf16[1,32,576]{2,1,0:T(8,128)(2,1)} %param.6), channel_id=1, source_target_pairs={{0,4},{4,0},{1,5},{5,1},{2,6},{6,2},{3,7},{7,3},{8,12},{12,8},{9,1... | collective-permute-start | bytes 110600 | tf_op jit(solution)/shard_map/ppermute | solution.py:28
  6.5 5.1 %collective-permute-start = (bf16[32,576]{1,0:T(8,128)(2,1)S(1)}, bf16[32,576]{1,0:T(8,128)(2,1)S(1)}, u32[]{:S(2)}, u32[]{:S(2)}) collective-permute-start(bf16[32,576]{1,0:T(8,128)(2,1)S(1)} %get-tuple-element.27), channel_id=1, source_target_pairs={{0,4},{4,0},{1,5},{5,1},{2,6},{6,2},{3,7},{7,3},{8,12},{12,8},{9,1... | collective-permute-start | bytes 110600 | tf_op jit(solution)/shard_map/ppermute | solution.py:28
  6.7 7.0 %collective-permute-start.3 = (bf16[16,4096]{1,0:T(8,128)(2,1)S(1)}, bf16[16,4096]{1,0:T(8,128)(2,1)S(1)}, u32[]{:S(2)}, u32[]{:S(2)}) collective-permute-start(bf16[16,4096]{1,0:T(8,128)(2,1)S(1)} %get-tuple-element.28), channel_id=1, source_target_pairs={{0,1},{1,0},{2,3},{3,2},{4,5},{5,4},{6,7},{7,6},{8,9},{9,8},{10,11... | collective-permute-start | bytes 393224 | tf_op jit(solution)/shard_map/ppermute | solution.py:28
  11.6 6.4 %collective-permute-start.6 = (bf16[16,4096]{1,0:T(8,128)(2,1)S(1)}, bf16[16,4096]{1,0:T(8,128)(2,1)S(1)}, u32[]{:S(2)}, u32[]{:S(2)}) collective-permute-start(bf16[16,4096]{1,0:T(8,128)(2,1)S(1)} %get-tuple-element.30), channel_id=1, source_target_pairs={{0,1},{1,0},{2,3},{3,2},{4,5},{5,4},{6,7},{7,6},{8,9},{9,8},{10,11... | collective-permute-start | bytes 393224 | tf_op jit(solution)/shard_map/ppermute | solution.py:28
  11.7 4.7 %collective-permute-start.2 = (bf16[1,64,576]{2,1,0:T(8,128)(2,1)S(1)}, bf16[1,64,576]{2,1,0:T(8,128)(2,1)S(1)}, u32[]{:S(2)}, u32[]{:S(2)}) collective-permute-start(bf16[1,64,576]{2,1,0:T(8,128)(2,1)S(1)} %bitcast.35), channel_id=1, source_target_pairs={{0,16},{8,24},{16,0},{24,8},{1,17},{9,25},{17,1},{25,9},{2,18},{10... | collective-permute-start | bytes 221192 | tf_op jit(solution)/shard_map/ppermute | solution.py:28
  13.7 11.6 %collective-permute-start.5 = (bf16[16,4096]{1,0:T(8,128)(2,1)S(1)}, bf16[16,4096]{1,0:T(8,128)(2,1)S(1)}, u32[]{:S(2)}, u32[]{:S(2)}) collective-permute-start(bf16[16,4096]{1,0:T(8,128)(2,1)S(1)} %get-tuple-element.56), channel_id=1, source_target_pairs={{0,2},{1,3},{2,0},{3,1},{4,6},{5,7},{6,4},{7,5},{8,10},{9,11},{10,... | collective-permute-start | bytes 393224 | tf_op jit(solution)/shard_map/ppermute | solution.py:28
  16.4 3.8 %collective-permute-start.4 = (bf16[2,64,576]{2,1,0:T(8,128)(2,1)S(1)}, bf16[2,64,576]{2,1,0:T(8,128)(2,1)S(1)}, u32[]{:S(2)}, u32[]{:S(2)}) collective-permute-start(bf16[2,64,576]{2,1,0:T(8,128)(2,1)S(1)} %pad_maximum_fusion.2), channel_id=1, source_target_pairs={{0,8},{8,0},{16,24},{24,16},{1,9},{9,1},{17,25},{25,17},{2,10},{10... | collective-permute-start | bytes 442376 | tf_op jit(solution)/shard_map/ppermute | solution.py:28
  18.0 13.7 %collective-permute-start.8 = (bf16[16,4096]{1,0:T(8,128)(2,1)S(1)}, bf16[16,4096]{1,0:T(8,128)(2,1)S(1)}, u32[]{:S(2)}, u32[]{:S(2)}) collective-permute-start(bf16[16,4096]{1,0:T(8,128)(2,1)S(1)} %get-tuple-element.54), channel_id=1, source_target_pairs={{0,2},{1,3},{2,0},{3,1},{4,6},{5,7},{6,4},{7,5},{8,10},{9,11},{10,... | collective-permute-start | bytes 393224 | tf_op jit(solution)/shard_map/ppermute | solution.py:28
  24.4 7.3 %collective-permute-start.9 = (bf16[32,2048]{1,0:T(8,128)(2,1)S(1)}, bf16[32,2048]{1,0:T(8,128)(2,1)S(1)}, u32[]{:S(2)}, u32[]{:S(2)}) collective-permute-start(bf16[32,2048]{1,0:T(8,128)(2,1)S(1)} %get-tuple-element.37), channel_id=1, source_target_pairs={{0,1},{1,0},{2,3},{3,2},{4,5},{5,4},{6,7},{7,6},{8,9},{9,8},{10,11... | collective-permute-start | bytes 393224 | tf_op jit(solution)/shard_map/ppermute | solution.py:28
  25.4 14.6 %collective-permute-start.7 = (bf16[16,4096]{1,0:T(8,128)(2,1)S(1)}, bf16[16,4096]{1,0:T(8,128)(2,1)S(1)}, u32[]{:S(2)}, u32[]{:S(2)}) collective-permute-start(bf16[16,4096]{1,0:T(8,128)(2,1)S(1)} %fusion.3.refs_5_.refs_4_), channel_id=1, source_target_pairs={{0,1},{1,0},{2,3},{3,2},{4,5},{5,4},{6,7},{7,6},{8,9},{9,8},{10,11... | collective-permute-start | bytes 393224 | tf_op jit(solution)/shard_map/ppermute | solution.py:28
  30.8 8.9 %collective-permute-start.11 = (bf16[32,2048]{1,0:T(8,128)(2,1)S(1)}, bf16[32,2048]{1,0:T(8,128)(2,1)S(1)}, u32[]{:S(2)}, u32[]{:S(2)}) collective-permute-start(bf16[32,2048]{1,0:T(8,128)(2,1)S(1)} %get-tuple-element.40), channel_id=1, source_target_pairs={{0,1},{1,0},{2,3},{3,2},{4,5},{5,4},{6,7},{7,6},{8,9},{9,8},{10,11... | collective-permute-start | bytes 393224 | tf_op jit(solution)/shard_map/ppermute | solution.py:28
  31.8 9.4 %collective-permute-start.10 = (bf16[16,4096]{1,0:T(8,128)(2,1)S(1)}, bf16[16,4096]{1,0:T(8,128)(2,1)S(1)}, u32[]{:S(2)}, u32[]{:S(2)}) collective-permute-start(bf16[16,4096]{1,0:T(8,128)(2,1)S(1)} %fusion.2.refs_6_), channel_id=1, source_target_pairs={{0,1},{1,0},{2,3},{3,2},{4,5},{5,4},{6,7},{7,6},{8,9},{9,8},{10,11... | collective-permute-start | bytes 393224 | tf_op jit(solution)/shard_map/ppermute | solution.py:28
  33.1 12.3 %collective-permute-start.12 = (bf16[32,2048]{1,0:T(8,128)(2,1)S(1)}, bf16[32,2048]{1,0:T(8,128)(2,1)S(1)}, u32[]{:S(2)}, u32[]{:S(2)}) collective-permute-start(bf16[32,2048]{1,0:T(8,128)(2,1)S(1)} %get-tuple-element.52), channel_id=1, source_target_pairs={{0,2},{1,3},{2,0},{3,1},{4,6},{5,7},{6,4},{7,5},{8,10},{9,11},{10,... | collective-permute-start | bytes 393224 | tf_op jit(solution)/shard_map/ppermute | solution.py:28
  39.8 7.4 %collective-permute-start.13 = (bf16[32,2048]{1,0:T(8,128)(2,1)S(1)}, bf16[32,2048]{1,0:T(8,128)(2,1)S(1)}, u32[]{:S(2)}, u32[]{:S(2)}) collective-permute-start(bf16[32,2048]{1,0:T(8,128)(2,1)S(1)} %get-tuple-element.50), channel_id=1, source_target_pairs={{0,2},{1,3},{2,0},{3,1},{4,6},{5,7},{6,4},{7,5},{8,10},{9,11},{10,... | collective-permute-start | bytes 393224 | tf_op jit(solution)/shard_map/ppermute | solution.py:28
  45.4 7.6 %collective-permute-start.14 = (bf16[32,2048]{1,0:T(8,128)(2,1)S(1)}, bf16[32,2048]{1,0:T(8,128)(2,1)S(1)}, u32[]{:S(2)}, u32[]{:S(2)}) collective-permute-start(bf16[32,2048]{1,0:T(8,128)(2,1)S(1)} %fusion.1.refs_9_), channel_id=1, source_target_pairs={{0,1},{1,0},{2,3},{3,2},{4,5},{5,4},{6,7},{7,6},{8,9},{9,8},{10,11... | collective-permute-start | bytes 393224 | tf_op jit(solution)/shard_map/ppermute | solution.py:28
  47.2 5.9 %collective-permute-start.15 = (bf16[32,2048]{1,0:T(8,128)(2,1)S(1)}, bf16[32,2048]{1,0:T(8,128)(2,1)S(1)}, u32[]{:S(2)}, u32[]{:S(2)}) collective-permute-start(bf16[32,2048]{1,0:T(8,128)(2,1)S(1)} %fusion), channel_id=1, source_target_pairs={{0,1},{1,0},{2,3},{3,2},{4,5},{5,4},{6,7},{7,6},{8,9},{9,8},{10,11... | collective-permute-start | bytes 393224 | tf_op jit(solution)/shard_map/ppermute | solution.py:28
  47.7 5.4 %copy-start = (bf16[1,32,576]{2,1,0:T(8,128)(2,1)S(1)}, bf16[1,32,576]{2,1,0:T(8,128)(2,1)}, u32[]{:S(2)}) copy-start(bf16[1,32,576]{2,1,0:T(8,128)(2,1)} %param.6) | copy-start | bytes 110596

commit v5 on v4

--- a/solution.py
+++ b/solution.py
@@ -373,15 +373,15 @@
 
     keep, send = feat_part(feat_size, grads, weight, 0, count, [act_sums[-1][0]])
     first = keep, neighbour(send)
-    acts = [activation(0, send)]
+    acts = [activation(0, keep)]
     backs = [neighbour(acts[0])]
     keep, send = feat_part(feat_size, grads, weight, count, count, acts)
     second = keep, neighbour(send)
-    feat_sums = [across(*pair_sum(*first, send))]
+    feat_sums = [across(*pair_sum(*first, keep))]
     for i in range(1, len(blocks)):
         acts.append(activation(i, feat_sums[0][0]))
         backs.append(neighbour(acts[i]))
-    feat_sums.append(across(*pair_sum(*second, acts[-1])))
+    feat_sums.append(across(*pair_sum(*second, feat_sums[0][0])))
 
     pieces = [piece for pair in zip(acts, backs) for piece in pair]
     kept, middle = halves[0][0].shape[0], layers // 2

time: 56 us -> 55.4 us (0.989)
  waiting for transfers between devices: 8.97 us -> 7.99 us
    ppermute x16, waiting for transfers between devices: 8.97 us -> 7.99 us  [swap(): return lax.ppermute(x, axis, [(i, i ^ bit) for i in range(size)])]
  transfers between devices with their start and end apart: 16 -> 16, of which waited for: 5 -> 3; matrix products, arithmetic and copies ran while one was open for 1% -> 1% of each run, Pallas kernels for 40% -> 41%
where the time goes in v5:
time: 55.4 us; the launch traced here: 55.3 us
  Pallas kernels  25.2 us (45%)
  starting transfers between devices  20.8 us (38%)
  waiting for transfers between devices  7.99 us (14%)
  between operations  0.85 us (2%)
    ppermute x16, starting transfers between devices, swap(): return lax.ppermute(x, axis, [(i, i ^ bit) for i in range(size)])  20.8 us
    pallas_call x2, Pallas kernels, dec_product(): pl.pallas_call(body, in_specs=[VMEM] * (layers + len(acts)) + [ANY] * (le...  8.4 us
    pallas_call x2, Pallas kernels, feat_part(): pl.pallas_call(functools.partial(feat_part_kernel, feat_size, first, len(...  8.36 us
    ppermute x16, waiting for transfers between devices, swap(): return lax.ppermute(x, axis, [(i, i ^ bit) for i in range(size)])  7.99 us
    pallas_call x2, Pallas kernels, enc_part(): pl.pallas_call(functools.partial(enc_part_kernel, steps, len(carried)), i...  5.71 us
    pallas_call x1, Pallas kernels, enc_product(): pl.pallas_call(body, in_specs=[VMEM] * ends[2], out_specs=[HBM] * 3, out_...  2.76 us
  transfers between devices with their start and end apart: 16, of which 3 were waited for; matrix products, arithmetic and copies ran while one was open for 1% of the time, Pallas kernels for 41%

profile of v5, /device:TPU:0, one launch (start us, length us, event | category | flops | bytes accessed | tf_op | source)
XLA Modules:
  0.0 55.3 jit_solution(18331668385821887566)
XLA Ops:
  0.6 0.0 copy-start.1
  0.6 0.0 copy-start.2
  0.7 3.0 %collective-permute-start.1 = (bf16[1,32,576]{2,1,0:T(8,128)(2,1)}, bf16[1,32,576]{2,1,0:T(8,128)(2,1)S(1)}, u32[]{:S(2)}, u32[]{:S(2)}) collective-permute-start(bf16[1,32,576]{2,1,0:T(8,128)(2,1)} %param.6), channel_id=1, source_target_pairs={{0,4},{4,0},{1,5},{5,1},{2,6},{6,2},{3,7},{7,3},{8,12},{12,8},{9,1... | collective-permute-start | bytes 110600 | tf_op jit(solution)/shard_map/ppermute | solution.py:28
  3.7 2.9 %shard_map.93 = (f32[16,4096]{1,0:T(8,128)S(1)}, bf16[16,4096]{1,0:T(8,128)(2,1)S(1)}, bf16[32,576]{1,0:T(8,128)(2,1)S(1)}) custom-call(bf16[32,576]{1,0:T(8,128)(2,1)} %bitcast.41, bf16[576,4096]{1,0:T(8,128)(2,1)} %bitcast.48, bf16[32,576]{1,0:T(8,128)(2,1)} %bitcast.52), custom_call_target="tpu_custom_call" | custom-call | flops 150994944 | bytes 4718592 | tf_op jit(solution)/shard_map/pallas_call | solution.py:88
  6.5 0.1 collective-permute-start
  6.7 2.0 %collective-permute-start.3 = (bf16[16,4096]{1,0:T(8,128)(2,1)S(1)}, bf16[16,4096]{1,0:T(8,128)(2,1)S(1)}, u32[]{:S(2)}, u32[]{:S(2)}) collective-permute-start(bf16[16,4096]{1,0:T(8,128)(2,1)S(1)} %get-tuple-element.28), channel_id=1, source_target_pairs={{0,1},{1,0},{2,3},{3,2},{4,5},{5,4},{6,7},{7,6},{8,9},{9,8},{10,11... | collective-permute-start | bytes 393224 | tf_op jit(solution)/shard_map/ppermute | solution.py:28
  8.7 0.0 collective-permute-done.1
  8.7 2.9 %shard_map.94 = (f32[16,4096]{1,0:T(8,128)S(1)}, bf16[16,4096]{1,0:T(8,128)(2,1)S(1)}) custom-call(bf16[32,576]{1,0:T(8,128)(2,1)S(1)} %bitcast.43, bf16[576,4096]{1,0:T(8,128)(2,1)} %bitcast.49), custom_call_target="tpu_custom_call" | custom-call | flops 150994944 | bytes 4718592 | tf_op jit(solution)/shard_map/pallas_call | solution.py:88
  11.6 0.1 collective-permute-start.6
  11.7 0.0 collective-permute-done
  11.7 2.0 %collective-permute-start.2 = (bf16[1,64,576]{2,1,0:T(8,128)(2,1)S(1)}, bf16[1,64,576]{2,1,0:T(8,128)(2,1)S(1)}, u32[]{:S(2)}, u32[]{:S(2)}) collective-permute-start(bf16[1,64,576]{2,1,0:T(8,128)(2,1)S(1)} %bitcast.35), channel_id=1, source_target_pairs={{0,16},{8,24},{16,0},{24,8},{1,17},{9,25},{17,1},{25,9},{2,18},{10... | collective-permute-start | bytes 221192 | tf_op jit(solution)/shard_map/ppermute | solution.py:28
  13.7 0.0 collective-permute-done.3
  13.7 2.7 %collective-permute-start.5 = (bf16[16,4096]{1,0:T(8,128)(2,1)S(1)}, bf16[16,4096]{1,0:T(8,128)(2,1)S(1)}, u32[]{:S(2)}, u32[]{:S(2)}) collective-permute-start(bf16[16,4096]{1,0:T(8,128)(2,1)S(1)} %get-tuple-element.56), channel_id=1, source_target_pairs={{0,2},{1,3},{2,0},{3,1},{4,6},{5,7},{6,4},{7,5},{8,10},{9,11},{10,... | collective-permute-start | bytes 393224 | tf_op jit(solution)/shard_map/ppermute | solution.py:28
  16.3 0.0 collective-permute-done.2
  16.4 0.1 collective-permute-start.4
  16.5 1.5 %collective-permute-done.6 = bf16[16,4096]{1,0:T(8,128)(2,1)S(1)} collective-permute-done((bf16[16,4096]{1,0:T(8,128)(2,1)S(1)}, bf16[16,4096]{1,0:T(8,128)(2,1)S(1)}, u32[]{:S(2)}, u32[]{:S(2)}) %collective-permute-start.6) | collective-permute-done | bytes 131104 | tf_op jit(solution)/shard_map/ppermute | solution.py:28
  18.0 2.2 %collective-permute-start.8 = (bf16[16,4096]{1,0:T(8,128)(2,1)S(1)}, bf16[16,4096]{1,0:T(8,128)(2,1)S(1)}, u32[]{:S(2)}, u32[]{:S(2)}) collective-permute-start(bf16[16,4096]{1,0:T(8,128)(2,1)S(1)} %get-tuple-element.54), channel_id=1, source_target_pairs={{0,2},{1,3},{2,0},{3,1},{4,6},{5,7},{6,4},{7,5},{8,10},{9,11},{10,... | collective-permute-start | bytes 393224 | tf_op jit(solution)/shard_map/ppermute | solution.py:28
  20.2 0.0 collective-permute-done.4
  20.2 4.2 %shard_map.95 = (f32[32,2048]{1,0:T(8,128)S(1)}, bf16[32,2048]{1,0:T(8,128)(2,1)S(1)}) custom-call(bf16[64,576]{1,0:T(8,128)(2,1)S(1)} %constant_dynamic-update-slice_fusion.refs_0_, bf16[64,576]{1,0:T(8,128)(2,1)S(1)} %get-tuple-element.59.refs_1_, bf16[64,576]{1,0:T(8,128)(2,1)S(1)} %bitcast.37, bf16[64,576]{1,0:T(8,128)(2,1)S(1)} %get-tuple-element.58.refs_3_, ...), custom_call_target="tpu_custom_call" | custom-call | flops 603979776 | bytes 9437184 | tf_op jit(solution)/shard_map/pallas_call | solution.py:146
  24.4 0.0 collective-permute-done.5
  24.4 0.9 %collective-permute-start.9 = (bf16[32,2048]{1,0:T(8,128)(2,1)S(1)}, bf16[32,2048]{1,0:T(8,128)(2,1)S(1)}, u32[]{:S(2)}, u32[]{:S(2)}) collective-permute-start(bf16[32,2048]{1,0:T(8,128)(2,1)S(1)} %get-tuple-element.39), channel_id=1, source_target_pairs={{0,1},{1,0},{2,3},{3,2},{4,5},{5,4},{6,7},{7,6},{8,9},{9,8},{10,11... | collective-permute-start | bytes 393224 | tf_op jit(solution)/shard_map/ppermute | solution.py:28
  25.3 0.0 copy-done.1
  25.3 0.0 copy-done.2
  25.3 0.1 fusion.3.refs_5_.refs_4_
  25.3 1.3 %collective-permute-start.7 = (bf16[16,4096]{1,0:T(8,128)(2,1)S(1)}, bf16[16,4096]{1,0:T(8,128)(2,1)S(1)}, u32[]{:S(2)}, u32[]{:S(2)}) collective-permute-start(bf16[16,4096]{1,0:T(8,128)(2,1)S(1)} %fusion.3.refs_5_.refs_4_), channel_id=1, source_target_pairs={{0,1},{1,0},{2,3},{3,2},{4,5},{5,4},{6,7},{7,6},{8,9},{9,8},{10,11... | collective-permute-start | bytes 393224 | tf_op jit(solution)/shard_map/ppermute | solution.py:28
  26.6 4.2 %shard_map.96 = (f32[32,2048]{1,0:T(8,128)S(1)}, bf16[32,2048]{1,0:T(8,128)(2,1)S(1)}) custom-call(bf16[64,576]{1,0:T(8,128)(2,1)S(1)} %constant_dynamic-update-slice_fusion.refs_0_, bf16[64,576]{1,0:T(8,128)(2,1)S(1)} %get-tuple-element.59.refs_1_, bf16[64,576]{1,0:T(8,128)(2,1)S(1)} %bitcast.38, bf16[64,576]{1,0:T(8,128)(2,1)S(1)} %get-tuple-element.58.refs_3_, ...), custom_call_target="tpu_custom_call" | custom-call | flops 603979776 | bytes 9437184 | tf_op jit(solution)/shard_map/pallas_call | solution.py:146
  30.8 0.9 %collective-permute-start.11 = (bf16[32,2048]{1,0:T(8,128)(2,1)S(1)}, bf16[32,2048]{1,0:T(8,128)(2,1)S(1)}, u32[]{:S(2)}, u32[]{:S(2)}) collective-permute-start(bf16[32,2048]{1,0:T(8,128)(2,1)S(1)} %get-tuple-element.43), channel_id=1, source_target_pairs={{0,1},{1,0},{2,3},{3,2},{4,5},{5,4},{6,7},{7,6},{8,9},{9,8},{10,11... | collective-permute-start | bytes 393224 | tf_op jit(solution)/shard_map/ppermute | solution.py:28
  31.7 0.0 collective-permute-done.9
  31.7 0.0 collective-permute-done.8
  31.7 0.1 fusion.2.refs_6_
  31.8 1.3 %collective-permute-start.10 = (bf16[16,4096]{1,0:T(8,128)(2,1)S(1)}, bf16[16,4096]{1,0:T(8,128)(2,1)S(1)}, u32[]{:S(2)}, u32[]{:S(2)}) collective-permute-start(bf16[16,4096]{1,0:T(8,128)(2,1)S(1)} %fusion.2.refs_6_), channel_id=1, source_target_pairs={{0,1},{1,0},{2,3},{3,2},{4,5},{5,4},{6,7},{7,6},{8,9},{9,8},{10,11... | collective-permute-start | bytes 393224 | tf_op jit(solution)/shard_map/ppermute | solution.py:28
  33.1 2.1 %collective-permute-start.12 = (bf16[32,2048]{1,0:T(8,128)(2,1)S(1)}, bf16[32,2048]{1,0:T(8,128)(2,1)S(1)}, u32[]{:S(2)}, u32[]{:S(2)}) collective-permute-start(bf16[32,2048]{1,0:T(8,128)(2,1)S(1)} %get-tuple-element.52), channel_id=1, source_target_pairs={{0,2},{1,3},{2,0},{3,1},{4,6},{5,7},{6,4},{7,5},{8,10},{9,11},{10,... | collective-permute-start | bytes 393224 | tf_op jit(solution)/shard_map/ppermute | solution.py:28
  35.2 5.2 %collective-permute-done.11 = bf16[32,2048]{1,0:T(8,128)(2,1)S(1)} collective-permute-done((bf16[32,2048]{1,0:T(8,128)(2,1)S(1)}, bf16[32,2048]{1,0:T(8,128)(2,1)S(1)}, u32[]{:S(2)}, u32[]{:S(2)}) %collective-permute-start.11) | collective-permute-done | bytes 131104 | tf_op jit(solution)/shard_map/ppermute | solution.py:28
  40.4 0.1 collective-permute-start.13
  40.5 0.0 collective-permute-done.7.refs_5_
  40.5 1.3 %collective-permute-done.10.refs_7_ = bf16[16,4096]{1,0:T(8,128)(2,1)S(1)} collective-permute-done((bf16[16,4096]{1,0:T(8,128)(2,1)S(1)}, bf16[16,4096]{1,0:T(8,128)(2,1)S(1)}, u32[]{:S(2)}, u32[]{:S(2)}) %collective-permute-start.10) | collective-permute-done | bytes 131104 | tf_op jit(solution)/shard_map/ppermute | solution.py:28
  41.8 4.2 %shard_map.97.refs_8_ = bf16[4,576,4096]{2,1,0:T(8,128)(2,1)} custom-call(bf16[64,576]{1,0:T(8,128)(2,1)S(1)} %constant_dynamic-update-slice_fusion.refs_0_, bf16[64,576]{1,0:T(8,128)(2,1)S(1)} %get-tuple-element.59.refs_1_, bf16[64,576]{1,0:T(8,128)(2,1)S(1)} %bitcast.39, bf16[64,576]{1,0:T(8,128)(2,1)S(1)} %get-tuple-element.58.refs_3_, ...), custom_call_target="tpu_custom_call" | custom-call | flops 603979776 | bytes 9437184 | tf_op jit(solution)/shard_map/pallas_call | solution.py:211
  45.9 0.0 collective-permute-done.12
  46.0 0.9 %collective-permute-start.14 = (bf16[32,2048]{1,0:T(8,128)(2,1)S(1)}, bf16[32,2048]{1,0:T(8,128)(2,1)S(1)}, u32[]{:S(2)}, u32[]{:S(2)}) collective-permute-start(bf16[32,2048]{1,0:T(8,128)(2,1)S(1)} %fusion.1.refs_9_), channel_id=1, source_target_pairs={{0,1},{1,0},{2,3},{3,2},{4,5},{5,4},{6,7},{7,6},{8,9},{9,8},{10,11... | collective-permute-start | bytes 393224 | tf_op jit(solution)/shard_map/ppermute | solution.py:28
  46.9 0.0 collective-permute-done.13
  47.0 1.2 %collective-permute-start.15 = (bf16[32,2048]{1,0:T(8,128)(2,1)S(1)}, bf16[32,2048]{1,0:T(8,128)(2,1)S(1)}, u32[]{:S(2)}, u32[]{:S(2)}) collective-permute-start(bf16[32,2048]{1,0:T(8,128)(2,1)S(1)} %fusion), channel_id=1, source_target_pairs={{0,1},{1,0},{2,3},{3,2},{4,5},{5,4},{6,7},{7,6},{8,9},{9,8},{10,11... | collective-permute-start | bytes 393224 | tf_op jit(solution)/shard_map/ppermute | solution.py:28
  48.2 0.0 copy-start
  48.3 4.2 %shard_map.98 = bf16[4,576,4096]{2,1,0:T(8,128)(2,1)} custom-call(bf16[64,576]{1,0:T(8,128)(2,1)S(1)} %constant_dynamic-update-slice_fusion.refs_0_, bf16[64,576]{1,0:T(8,128)(2,1)S(1)} %get-tuple-element.59.refs_1_, bf16[64,576]{1,0:T(8,128)(2,1)S(1)} %bitcast.40, bf16[64,576]{1,0:T(8,128)(2,1)S(1)} %get-tuple-element.58.refs_3_, ...), custom_call_target="tpu_custom_call", output_to_operand_aliasing={{}: (8, {})} | custom-call | flops 603979776 | bytes 9437184 | tf_op jit(solution)/shard_map/pallas_call | solution.py:211
  52.5 0.0 collective-permute-done.15
  52.5 0.0 collective-permute-done.14
  52.5 0.0 copy-done
  52.5 2.8 %shard_map.99 = (bf16[576,4096]{1,0:T(8,128)(2,1)}, f32[1,4096]{1,0:T(1,128)}, bf16[64,4096]{1,0:T(8,128)(2,1)}) custom-call(bf16[32,576]{1,0:T(8,128)(2,1)S(1)} %bitcast.42, bf16[32,576]{1,0:T(8,128)(2,1)S(1)} %bitcast.44, bf16[32,4096]{1,0:T(8,128)(2,1)S(1)} %pad_maximum_fusion.refs_2_, bf16[32,4096]{1,0:T(8,128)(2,1)S(1)} %pad_maximum_fusion.1.refs_3_), custom_call_target="tpu_custom_call" | custom-call | flops 301989888 | bytes 4718592 | tf_op jit(solution)/shard_map/pallas_call | solution.py:269
  (12 shorter events, 0.3 us)
Async XLA Ops:
  0.6 24.7 %copy-start.1 = (s32[1,64,4096]{2,1,0:T(8,128)S(1)}, s32[1,64,4096]{2,1,0:T(8,128)}, u32[]{:S(2)}) copy-start(s32[1,64,4096]{2,1,0:T(8,128)} %param.11) | copy-start | bytes 3145732
  0.6 24.7 %copy-start.2 = (f32[1,4096]{1,0:T(1,128)S(1)}, f32[1,4096]{1,0:T(1,128)}, u32[]{:S(2)}) copy-start(f32[1,4096]{1,0:T(1,128)} %param.9) | copy-start | bytes 49156
  0.7 8.1 %collective-permute-start.1 = (bf16[1,32,576]{2,1,0:T(8,128)(2,1)}, bf16[1,32,576]{2,1,0:T(8,128)(2,1)S(1)}, u32[]{:S(2)}, u32[]{:S(2)}) collective-permute-start(bf16[1,32,576]{2,1,0:T(8,128)(2,1)} %param.6), channel_id=1, source_target_pairs={{0,4},{4,0},{1,5},{5,1},{2,6},{6,2},{3,7},{7,3},{8,12},{12,8},{9,1... | collective-permute-start | bytes 110600 | tf_op jit(solution)/shard_map/ppermute | solution.py:28
  6.5 5.1 %collective-permute-start = (bf16[32,576]{1,0:T(8,128)(2,1)S(1)}, bf16[32,576]{1,0:T(8,128)(2,1)S(1)}, u32[]{:S(2)}, u32[]{:S(2)}) collective-permute-start(bf16[32,576]{1,0:T(8,128)(2,1)S(1)} %get-tuple-element.27), channel_id=1, source_target_pairs={{0,4},{4,0},{1,5},{5,1},{2,6},{6,2},{3,7},{7,3},{8,12},{12,8},{9,1... | collective-permute-start | bytes 110600 | tf_op jit(solution)/shard_map/ppermute | solution.py:28
  6.7 7.0 %collective-permute-start.3 = (bf16[16,4096]{1,0:T(8,128)(2,1)S(1)}, bf16[16,4096]{1,0:T(8,128)(2,1)S(1)}, u32[]{:S(2)}, u32[]{:S(2)}) collective-permute-start(bf16[16,4096]{1,0:T(8,128)(2,1)S(1)} %get-tuple-element.28), channel_id=1, source_target_pairs={{0,1},{1,0},{2,3},{3,2},{4,5},{5,4},{6,7},{7,6},{8,9},{9,8},{10,11... | collective-permute-start | bytes 393224 | tf_op jit(solution)/shard_map/ppermute | solution.py:28
  11.6 6.4 %collective-permute-start.6 = (bf16[16,4096]{1,0:T(8,128)(2,1)S(1)}, bf16[16,4096]{1,0:T(8,128)(2,1)S(1)}, u32[]{:S(2)}, u32[]{:S(2)}) collective-permute-start(bf16[16,4096]{1,0:T(8,128)(2,1)S(1)} %get-tuple-element.30), channel_id=1, source_target_pairs={{0,1},{1,0},{2,3},{3,2},{4,5},{5,4},{6,7},{7,6},{8,9},{9,8},{10,11... | collective-permute-start | bytes 393224 | tf_op jit(solution)/shard_map/ppermute | solution.py:28
  11.7 4.7 %collective-permute-start.2 = (bf16[1,64,576]{2,1,0:T(8,128)(2,1)S(1)}, bf16[1,64,576]{2,1,0:T(8,128)(2,1)S(1)}, u32[]{:S(2)}, u32[]{:S(2)}) collective-permute-start(bf16[1,64,576]{2,1,0:T(8,128)(2,1)S(1)} %bitcast.35), channel_id=1, source_target_pairs={{0,16},{8,24},{16,0},{24,8},{1,17},{9,25},{17,1},{25,9},{2,18},{10... | collective-permute-start | bytes 221192 | tf_op jit(solution)/shard_map/ppermute | solution.py:28
  13.7 10.7 %collective-permute-start.5 = (bf16[16,4096]{1,0:T(8,128)(2,1)S(1)}, bf16[16,4096]{1,0:T(8,128)(2,1)S(1)}, u32[]{:S(2)}, u32[]{:S(2)}) collective-permute-start(bf16[16,4096]{1,0:T(8,128)(2,1)S(1)} %get-tuple-element.56), channel_id=1, source_target_pairs={{0,2},{1,3},{2,0},{3,1},{4,6},{5,7},{6,4},{7,5},{8,10},{9,11},{10,... | collective-permute-start | bytes 393224 | tf_op jit(solution)/shard_map/ppermute | solution.py:28
  16.4 3.8 %collective-permute-start.4 = (bf16[2,64,576]{2,1,0:T(8,128)(2,1)S(1)}, bf16[2,64,576]{2,1,0:T(8,128)(2,1)S(1)}, u32[]{:S(2)}, u32[]{:S(2)}) collective-permute-start(bf16[2,64,576]{2,1,0:T(8,128)(2,1)S(1)} %pad_maximum_fusion.2), channel_id=1, source_target_pairs={{0,8},{8,0},{16,24},{24,16},{1,9},{9,1},{17,25},{25,17},{2,10},{10... | collective-permute-start | bytes 442376 | tf_op jit(solution)/shard_map/ppermute | solution.py:28
  18.0 13.7 %collective-permute-start.8 = (bf16[16,4096]{1,0:T(8,128)(2,1)S(1)}, bf16[16,4096]{1,0:T(8,128)(2,1)S(1)}, u32[]{:S(2)}, u32[]{:S(2)}) collective-permute-start(bf16[16,4096]{1,0:T(8,128)(2,1)S(1)} %get-tuple-element.54), channel_id=1, source_target_pairs={{0,2},{1,3},{2,0},{3,1},{4,6},{5,7},{6,4},{7,5},{8,10},{9,11},{10,... | collective-permute-start | bytes 393224 | tf_op jit(solution)/shard_map/ppermute | solution.py:28
  24.4 7.3 %collective-permute-start.9 = (bf16[32,2048]{1,0:T(8,128)(2,1)S(1)}, bf16[32,2048]{1,0:T(8,128)(2,1)S(1)}, u32[]{:S(2)}, u32[]{:S(2)}) collective-permute-start(bf16[32,2048]{1,0:T(8,128)(2,1)S(1)} %get-tuple-element.39), channel_id=1, source_target_pairs={{0,1},{1,0},{2,3},{3,2},{4,5},{5,4},{6,7},{7,6},{8,9},{9,8},{10,11... | collective-permute-start | bytes 393224 | tf_op jit(solution)/shard_map/ppermute | solution.py:28
  25.3 15.1 %collective-permute-start.7 = (bf16[16,4096]{1,0:T(8,128)(2,1)S(1)}, bf16[16,4096]{1,0:T(8,128)(2,1)S(1)}, u32[]{:S(2)}, u32[]{:S(2)}) collective-permute-start(bf16[16,4096]{1,0:T(8,128)(2,1)S(1)} %fusion.3.refs_5_.refs_4_), channel_id=1, source_target_pairs={{0,1},{1,0},{2,3},{3,2},{4,5},{5,4},{6,7},{7,6},{8,9},{9,8},{10,11... | collective-permute-start | bytes 393224 | tf_op jit(solution)/shard_map/ppermute | solution.py:28
  30.8 9.5 %collective-permute-start.11 = (bf16[32,2048]{1,0:T(8,128)(2,1)S(1)}, bf16[32,2048]{1,0:T(8,128)(2,1)S(1)}, u32[]{:S(2)}, u32[]{:S(2)}) collective-permute-start(bf16[32,2048]{1,0:T(8,128)(2,1)S(1)} %get-tuple-element.43), channel_id=1, source_target_pairs={{0,1},{1,0},{2,3},{3,2},{4,5},{5,4},{6,7},{7,6},{8,9},{9,8},{10,11... | collective-permute-start | bytes 393224 | tf_op jit(solution)/shard_map/ppermute | solution.py:28
  31.8 9.9 %collective-permute-start.10 = (bf16[16,4096]{1,0:T(8,128)(2,1)S(1)}, bf16[16,4096]{1,0:T(8,128)(2,1)S(1)}, u32[]{:S(2)}, u32[]{:S(2)}) collective-permute-start(bf16[16,4096]{1,0:T(8,128)(2,1)S(1)} %fusion.2.refs_6_), channel_id=1, source_target_pairs={{0,1},{1,0},{2,3},{3,2},{4,5},{5,4},{6,7},{7,6},{8,9},{9,8},{10,11... | collective-permute-start | bytes 393224 | tf_op jit(solution)/shard_map/ppermute | solution.py:28
  33.1 12.8 %collective-permute-start.12 = (bf16[32,2048]{1,0:T(8,128)(2,1)S(1)}, bf16[32,2048]{1,0:T(8,128)(2,1)S(1)}, u32[]{:S(2)}, u32[]{:S(2)}) collective-permute-start(bf16[32,2048]{1,0:T(8,128)(2,1)S(1)} %get-tuple-element.52), channel_id=1, source_target_pairs={{0,2},{1,3},{2,0},{3,1},{4,6},{5,7},{6,4},{7,5},{8,10},{9,11},{10,... | collective-permute-start | bytes 393224 | tf_op jit(solution)/shard_map/ppermute | solution.py:28
  40.4 6.6 %collective-permute-start.13 = (bf16[32,2048]{1,0:T(8,128)(2,1)S(1)}, bf16[32,2048]{1,0:T(8,128)(2,1)S(1)}, u32[]{:S(2)}, u32[]{:S(2)}) collective-permute-start(bf16[32,2048]{1,0:T(8,128)(2,1)S(1)} %get-tuple-element.50), channel_id=1, source_target_pairs={{0,2},{1,3},{2,0},{3,1},{4,6},{5,7},{6,4},{7,5},{8,10},{9,11},{10,... | collective-permute-start | bytes 393224 | tf_op jit(solution)/shard_map/ppermute | solution.py:28
  46.0 6.5 %collective-permute-start.14 = (bf16[32,2048]{1,0:T(8,128)(2,1)S(1)}, bf16[32,2048]{1,0:T(8,128)(2,1)S(1)}, u32[]{:S(2)}, u32[]{:S(2)}) collective-permute-start(bf16[32,2048]{1,0:T(8,128)(2,1)S(1)} %fusion.1.refs_9_), channel_id=1, source_target_pairs={{0,1},{1,0},{2,3},{3,2},{4,5},{5,4},{6,7},{7,6},{8,9},{9,8},{10,11... | collective-permute-start | bytes 393224 | tf_op jit(solution)/shard_map/ppermute | solution.py:28
  47.0 5.5 %collective-permute-start.15 = (bf16[32,2048]{1,0:T(8,128)(2,1)S(1)}, bf16[32,2048]{1,0:T(8,128)(2,1)S(1)}, u32[]{:S(2)}, u32[]{:S(2)}) collective-permute-start(bf16[32,2048]{1,0:T(8,128)(2,1)S(1)} %fusion), channel_id=1, source_target_pairs={{0,1},{1,0},{2,3},{3,2},{4,5},{5,4},{6,7},{7,6},{8,9},{9,8},{10,11... | collective-permute-start | bytes 393224 | tf_op jit(solution)/shard_map/ppermute | solution.py:28
  48.2 4.3 %copy-start = (bf16[1,32,576]{2,1,0:T(8,128)(2,1)S(1)}, bf16[1,32,576]{2,1,0:T(8,128)(2,1)}, u32[]{:S(2)}) copy-start(bf16[1,32,576]{2,1,0:T(8,128)(2,1)} %param.6) | copy-start | bytes 110596
